TPU v7x, 32 devices: a whole 2x2x4 slice. The times are simulated.
32 devices in a mesh: groups: 2 (over y), pool: 4 (over z), tensor: 2 (over x), sub: 2 (over core).
Axes of the slice: x: 2, y: 2, z: 4, core: 2. Of those that a mesh axis runs over, the one named last changes fastest.
Arguments:
- queries: bfloat16 [8, 160, 8192], P(('groups', 'pool'), None, ('tensor', 'sub')), parts along dimension 0, may hold values from -16 to 16
- new_keys: bfloat16 [8, 160, 1024], P(('groups', 'pool'), None, ('tensor', 'sub')), parts along dimension 0, may hold values from -9.6 to 9.6
- new_values: bfloat16 [8, 160, 1024], P(('groups', 'pool'), None, ('tensor', 'sub')), parts along dimension 0, may hold values from -6 to 6
- store_keys: bfloat16 [256, 256, 1024], P(('groups', 'pool'), None, ('tensor', 'sub')), parts along dimension 0, may hold values from -9.5625 to 9.5625
- store_values: bfloat16 [256, 256, 1024], P(('groups', 'pool'), None, ('tensor', 'sub')), parts along dimension 0, may hold values from -6 to 6
- prefix_blocks: int32 [8], P('groups'), parts along dimension 0, may hold values from 8 to 32, as said below
- hit_store: int32 [8, 32], P('groups'), parts along dimension 0, may hold values from 0 to 3, as said below
- hit_slot: int32 [8, 32], P('groups'), parts along dimension 0, may hold values from 0 to 31, as said below
- decode_owner: int32 [8], P('groups'), parts along dimension 0, may hold values from 0 to 3, as said below
Outputs:
- attended: bfloat16 [8, 160, 8192], P(('groups', 'pool'), None, ('tensor', 'sub')), parts along dimension 0
- pushed_keys: bfloat16 [16, 160, 1024], P(('groups', 'pool'), None, ('tensor', 'sub')), parts along dimension 0
- pushed_values: bfloat16 [16, 160, 1024], P(('groups', 'pool'), None, ('tensor', 'sub')), parts along dimension 0
There are 2 independent parts, one for each index of `groups`. A program takes and returns all parts, laid end to end along the dimension named above; each array names one. Nothing has to cross between parts.
Inputs may be any that keep to these rules, and one draw needn't show every extreme that they name: `prefix_blocks`: some request has exactly 32 cached blocks. `hit_store`: consecutive blocks of a request lie on store devices of consecutive index, wrapping around, so one store device holds at most 8 blocks of a request, and the request with 32 blocks puts exactly 8 on some store device. Entries past a request's count mean nothing. `hit_slot`: the cached blocks held by one store device occupy distinct slots. Entries past a request's count mean nothing. `decode_owner`: no instance decodes more than 2 requests, and some instance decodes exactly 2.
All inputs are finite; a program needn't handle non-finite values.
Results may differ from a plain program's by a relative error of at most 0.004.
Values may be sent and summed in bfloat16 or wider, within the bound.
No kernel may reach another device: no remote copies, remote signals or barrier semaphores. Data moves between devices by JAX's collectives and lax.ppermute only.
A program may use at most 128 MiB of HBM per device.

v0:
```python
import functools
import math

import jax
import jax.numpy as jnp
from jax import lax
from jax.experimental import pallas as pl
from jax.experimental.pallas import tpu as pltpu
from jax.sharding import PartitionSpec as P

HEADS = 64
KVH = 8
HD = 128
MAXBLK = 32
CAPP = 2
GROUP = HEADS // KVH
EMPTY = -1e30
LINE = 8
SCALE = 1.0 / math.sqrt(HD)
EXP2_SCALE = SCALE * math.log2(math.e)
VMEM_LIMIT = 48 * 1024 * 1024


def place(meta_ref, request, pool_size):
    prefix = meta_ref[1 + request]
    first = lax.rem(meta_ref[0] - meta_ref[1 + pool_size + request] + pool_size, pool_size)
    count = lax.max(lax.div(prefix - first + pool_size - 1, pool_size), 0)
    return count, 1 + 2 * pool_size + request * MAXBLK + first


def block_copies(meta_ref, base, entry, stores, buffers, sems, pool_size):
    slot = meta_ref[base + entry * pool_size]
    return [
        pltpu.make_async_copy(stores[i].at[slot], buffers[i].at[entry], sems.at[i, entry])
        for i in range(2)
    ]


def attend(
    query_ref, key_ref, value_ref, count, ready, new_refs, query_rows, scores, peaks, totals, acc, put
):
    new_rows = query_ref.shape[0]
    kv_local = key_ref.shape[2] // HD
    rows = GROUP * new_rows
    for kv in range(kv_local):
        lanes = slice(kv * HD, (kv + 1) * HD)
        for g in range(GROUP):
            head = kv * GROUP + g
            query_rows[g * new_rows : (g + 1) * new_rows, :] = query_ref[
                :, head * HD : (head + 1) * HD
            ]
        peaks[...] = jnp.full(peaks.shape, EMPTY, jnp.float32)
        if new_refs is not None:
            new_key_ref, new_value_ref, new_scores = new_refs
            fresh = lax.dot_general(
                query_rows[...],
                new_key_ref[:, lanes],
                (((1,), (1,)), ((), ())),
                preferred_element_type=jnp.float32,
            )
            row = lax.broadcasted_iota(jnp.int32, (new_rows, new_key_ref.shape[0]), 0)
            column = lax.broadcasted_iota(jnp.int32, (new_rows, new_key_ref.shape[0]), 1)
            for g in range(GROUP):
                part = slice(g * new_rows, (g + 1) * new_rows)
                masked = jnp.where(column <= row, fresh[part], EMPTY)
                new_scores[part, :] = masked
                peaks[part, :] = jnp.maximum(masked[:, :HD], masked[:, HD:])

        def score_block(entry, carry):
            if kv == 0:
                ready(entry)
            block = lax.dot_general(
                query_rows[...],
                key_ref[entry, :, lanes],
                (((1,), (1,)), ((), ())),
                preferred_element_type=jnp.float32,
            )
            scores[entry] = block
            best = peaks[...]
            for piece in range(block.shape[1] // HD):
                best = jnp.maximum(best, block[:, piece * HD : (piece + 1) * HD])
            peaks[...] = best
            return carry

        lax.fori_loop(0, count, score_block, 0)
        peak = jnp.max(peaks[...], axis=1, keepdims=True)
        peaks[...] = jnp.broadcast_to(peak, peaks.shape)

        def weigh(block, values):
            weights = jnp.exp2((block - peaks[:, 0:1]) * EXP2_SCALE)
            total = weights[:, :HD]
            for piece in range(1, weights.shape[1] // HD):
                total = total + weights[:, piece * HD : (piece + 1) * HD]
            mixed = lax.dot_general(
                weights.astype(jnp.bfloat16),
                values,
                (((1,), (0,)), ((), ())),
                preferred_element_type=jnp.float32,
            )
            return total, mixed

        if new_refs is not None:
            total, mixed = weigh(new_scores[...], new_value_ref[:, lanes])
            totals[...] = total
            acc[...] = mixed
        else:
            totals[...] = jnp.zeros(totals.shape, jnp.float32)
            acc[...] = jnp.zeros(acc.shape, jnp.float32)

        def weigh_block(entry, carry):
            total, mixed = weigh(scores[entry], value_ref[entry, :, lanes])
            totals[...] += total
            acc[...] += mixed
            return carry

        lax.fori_loop(0, count, weigh_block, 0)
        total = jnp.sum(totals[...], axis=1, keepdims=True)
        safe = jnp.where(total > 0, total, 1.0)
        out = acc[...] / safe
        log_total = jnp.where(total > 0, peak * SCALE + jnp.log(safe), EMPTY)
        for g in range(GROUP):
            part = slice(g * new_rows, (g + 1) * new_rows)
            put(kv * GROUP + g, out[part], log_total[part])


def add_lane(tile, heads, head, column):
    lane = lax.broadcasted_iota(jnp.int32, tile.shape, 1)
    hit = (lax.rem(lane, heads) == head) & (lane < 3 * heads)
    return jnp.where(hit, column, tile)


def split_lanes(tile, heads):
    lane = lax.broadcasted_iota(jnp.int32, tile.shape, 1)
    high = tile.astype(jnp.bfloat16).astype(jnp.float32)
    middle = (tile - high).astype(jnp.bfloat16).astype(jnp.float32)
    low = tile - high - middle
    return jnp.where(lane < heads, high, jnp.where(lane < 2 * heads, middle, low)).astype(
        jnp.bfloat16
    )


def fetch(pool_size, meta_ref, request, stores, buffers, sems):
    count, base = place(meta_ref, request, pool_size)

    def copies(entry):
        return block_copies(meta_ref, base, entry, stores, buffers, sems, pool_size)

    def start(entry, carry):
        for copy in copies(entry):
            copy.start()
        return carry

    lax.fori_loop(0, count, start, 0)

    def ready(entry):
        for copy in copies(entry):
            copy.wait()

    return count, ready


def own_kernel(
    pool_size,
    meta_ref,
    query_ref,
    new_key_ref,
    new_value_ref,
    store_keys,
    store_values,
    out_ref,
    log_ref,
    key_buf,
    value_buf,
    new_key_buf,
    new_value_buf,
    query_rows,
    scores,
    new_scores,
    peaks,
    totals,
    acc,
    sems,
):
    count, ready = fetch(
        pool_size, meta_ref, meta_ref[0], (store_keys, store_values), (key_buf, value_buf), sems
    )
    new_rows, width = query_ref.shape
    heads = width // HD
    for buffer, source in ((new_key_buf, new_key_ref), (new_value_buf, new_value_ref)):
        buffer[:new_rows, :] = source[...]
        buffer[new_rows:, :] = jnp.zeros(
            (buffer.shape[0] - new_rows, buffer.shape[1]), jnp.bfloat16
        )
    log_ref[...] = jnp.zeros(log_ref.shape, jnp.float32)

    def put(head, out, log_total):
        out_ref[:, head * HD : (head + 1) * HD] = out
        log_ref[...] = add_lane(log_ref[...], heads, head, log_total)

    attend(
        query_ref,
        key_buf,
        value_buf,
        count,
        ready,
        (new_key_buf, new_value_buf, new_scores),
        query_rows,
        scores,
        peaks,
        totals,
        acc,
        put,
    )


def other_kernel(
    pool_size,
    offset,
    meta_ref,
    query_ref,
    store_keys,
    store_values,
    out_ref,
    key_buf,
    value_buf,
    query_rows,
    scores,
    peaks,
    totals,
    acc,
    log_tile,
    sems,
):
    if offset is None:
        request = meta_ref[1 + 2 * pool_size + pool_size * MAXBLK]
    else:
        request = meta_ref[0] + offset

    @pl.when((request >= 0) & (request < pool_size))
    def _():
        count, ready = fetch(
            pool_size, meta_ref, request, (store_keys, store_values), (key_buf, value_buf), sems
        )
        width = query_ref.shape[1]
        heads = width // HD
        log_tile[...] = jnp.zeros(log_tile.shape, jnp.float32)

        def put(head, out, log_total):
            out_ref[:, head * HD : (head + 1) * HD] = out.astype(jnp.bfloat16)
            log_tile[...] = add_lane(log_tile[...], heads, head, log_total)

        attend(
            query_ref,
            key_buf,
            value_buf,
            count,
            ready,
            None,
            query_rows,
            scores,
            peaks,
            totals,
            acc,
            put,
        )
        out_ref[:, width:] = split_lanes(log_tile[...], heads)


def combine_kernel(sources, pool_size, meta_ref, own_ref, log_ref, *refs):
    out_ref = refs[-1]
    width = own_ref.shape[1]
    heads = width // HD
    logs = [log_ref[...]]
    valid = []
    for (relative, source), part in zip(sources, refs[:-1]):
        if relative:
            there = (meta_ref[0] + source >= 0) & (meta_ref[0] + source < pool_size)
        else:
            there = meta_ref[0] != source
        valid.append(there)
        tile = part[:, width:].astype(jnp.float32)
        whole = (
            tile + pltpu.roll(tile, HD - heads, 1) + pltpu.roll(tile, HD - 2 * heads, 1)
        )
        logs.append(jnp.where(there, whole, EMPTY))
    peak = functools.reduce(jnp.maximum, logs)
    shares = [jnp.exp(x - peak) for x in logs]
    scale = 1.0 / functools.reduce(jnp.add, shares)
    shares = [x * scale for x in shares]
    for head in range(heads):
        lanes = slice(head * HD, (head + 1) * HD)
        mixed = own_ref[:, lanes] * shares[0][:, head : head + 1]
        for share, there, part in zip(shares[1:], valid, refs[:-1]):
            mixed = mixed + jnp.where(
                there, part[:, lanes].astype(jnp.float32) * share[:, head : head + 1], 0.0
            )
        out_ref[:, lanes] = mixed.astype(jnp.bfloat16)


def shards(
    queries,
    new_keys,
    new_values,
    store_keys,
    store_values,
    prefix_blocks,
    hit_store,
    hit_slot,
    decode_owner,
):
    pool_size = lax.axis_size("pool")
    my_index = lax.axis_index("pool").astype(jnp.int32)
    capacity = (MAXBLK + pool_size - 1) // pool_size
    new_rows = queries.shape[1]
    width = queries.shape[2]
    kv_width = new_keys.shape[2]
    block_len = store_keys.shape[1]
    rows = GROUP * new_rows
    padded_rows = -(-new_rows // (2 * HD)) * 2 * HD
    meta = jnp.concatenate(
        [my_index.reshape(1), prefix_blocks, hit_store[:, 0], hit_slot.reshape(-1)]
    )
    flops = 4 * rows * block_len * kv_width * capacity
    smem_spec = pl.BlockSpec(memory_space=pltpu.SMEM)
    any_spec = pl.BlockSpec(memory_space=pl.ANY)
    vmem_spec = pl.BlockSpec(memory_space=pltpu.VMEM)
    params = pltpu.CompilerParams(vmem_limit_bytes=VMEM_LIMIT)
    cost = pl.CostEstimate(
        flops=8 * flops, bytes_accessed=4 * capacity * block_len * kv_width, transcendentals=0
    )
    buffers = [pltpu.VMEM((capacity, block_len, kv_width), jnp.bfloat16)] * 2
    work = [
        pltpu.VMEM((rows, HD), jnp.bfloat16),
        pltpu.VMEM((capacity, rows, block_len), jnp.float32),
    ]
    state = [pltpu.VMEM((rows, HD), jnp.float32)] * 3
    sems = pltpu.SemaphoreType.DMA((2, capacity))

    def own_part(query):
        return pl.pallas_call(
            functools.partial(own_kernel, pool_size),
            in_specs=[smem_spec] + [vmem_spec] * 3 + [any_spec] * 2,
            out_specs=[vmem_spec] * 2,
            scratch_shapes=[
                *buffers,
                *[pltpu.VMEM((padded_rows, kv_width), jnp.bfloat16)] * 2,
                *work,
                pltpu.VMEM((rows, padded_rows), jnp.float32),
                *state,
                sems,
            ],
            out_shape=[
                jax.ShapeDtypeStruct((new_rows, width), jnp.float32),
                jax.ShapeDtypeStruct((new_rows, HD), jnp.float32),
            ],
            compiler_params=params,
            cost_estimate=cost,
            name="own_part",
        )(meta, query, new_keys[0], new_values[0], store_keys, store_values)

    def other_part(offset, query, meta=meta):
        return pl.pallas_call(
            functools.partial(other_kernel, pool_size, offset),
            in_specs=[smem_spec, vmem_spec] + [any_spec] * 2,
            out_specs=vmem_spec,
            scratch_shapes=[
                *buffers,
                *work,
                *state,
                pltpu.VMEM((new_rows, HD), jnp.float32),
                sems,
            ],
            out_shape=jax.ShapeDtypeStruct((new_rows, width + HD), jnp.bfloat16),
            compiler_params=params,
            cost_estimate=cost,
            name="other_part",
        )(meta, query, store_keys, store_values)

    def shift(array, distance, first=0):
        pairs = [
            (i, i + distance)
            for i in range(pool_size)
            if 0 <= i + distance < pool_size and 0 <= i - first < pool_size
        ]
        return lax.ppermute(array, "pool", pairs)

    query = queries[0]
    fresh = jnp.concatenate([new_keys[0], new_values[0]], axis=1)
    own_out, own_log = own_part(query)
    if pool_size <= LINE:
        sources = []
        parts = []
        right, left = query, query
        for step in range(1, pool_size):
            right = shift(right, 1, step - 1)
            left = shift(left, -1, 1 - step)
            right, left = lax.optimization_barrier((right, left))
            for offset, held in ((-step, right), (step, left)):
                packed = other_part(offset, held)
                sources.append((True, -offset))
                parts.append(shift(packed, offset, -offset))
        fresh, right = lax.optimization_barrier((fresh, right))
        moved = [(my_index, fresh)]
        right, left = fresh, fresh
        for step in range(1, pool_size):
            right = shift(right, 1, step - 1)
            left = shift(left, -1, 1 - step)
            moved.append((my_index - step, right))
            moved.append((my_index + step, left))
    else:
        gathered = lax.all_gather(query, "pool", axis=0, tiled=False)
        packed = lax.map(
            lambda pair: other_part(None, pair[0], jnp.concatenate([meta, pair[1].reshape(1)])),
            (gathered, jnp.arange(pool_size, dtype=jnp.int32)),
        )
        parts = lax.all_to_all(packed, "pool", split_axis=0, concat_axis=0, tiled=True)
        sources = [(False, source) for source in range(pool_size)]
        moved = [
            (jnp.int32(source), array)
            for source, array in enumerate(lax.all_gather(fresh, "pool", axis=0, tiled=False))
        ]

    attended = pl.pallas_call(
        functools.partial(combine_kernel, tuple(sources), pool_size),
        in_specs=[smem_spec] + [vmem_spec] * (2 + len(sources)),
        out_specs=vmem_spec,
        out_shape=jax.ShapeDtypeStruct((new_rows, width), jnp.bfloat16),
        compiler_params=params,
        name="combine",
    )(meta, own_out, own_log, *parts)

    mine = decode_owner == my_index
    rank = jnp.cumsum(mine) - 1
    places = jnp.where(mine, rank, CAPP)
    padded_places = jnp.concatenate(
        [jnp.full((pool_size,), CAPP), places, jnp.full((pool_size,), CAPP)]
    )
    pushed = []
    for place_id in range(CAPP):
        total = jnp.zeros(fresh.shape, fresh.dtype)
        for source, array in moved:
            total = jnp.where(padded_places[source + pool_size] == place_id, array, total)
        pushed.append(total)
    pushed = jnp.stack(pushed)
    return (attended[None], pushed[:, :, :kv_width], pushed[:, :, kv_width:])


def solution(mesh):
    in_specs = (
        P(("groups", "pool"), None, ("tensor", "sub")),
        P(("groups", "pool"), None, ("tensor", "sub")),
        P(("groups", "pool"), None, ("tensor", "sub")),
        P(("groups", "pool"), None, ("tensor", "sub")),
        P(("groups", "pool"), None, ("tensor", "sub")),
        P("groups"),
        P("groups", None),
        P("groups", None),
        P("groups"),
    )
    out_specs = (
        P(("groups", "pool"), None, ("tensor", "sub")),
        P(("groups", "pool"), None, ("tensor", "sub")),
        P(("groups", "pool"), None, ("tensor", "sub")),
    )
    return jax.shard_map(shards, mesh=mesh, in_specs=in_specs, out_specs=out_specs, check_vma=False)
```

profile of v0, /device:TPU:6, one launch (start us, length us, event | category | flops | bytes accessed | tf_op | source)
XLA Modules:
  0.0 203.6 jit_solution(12220535879392078500)
XLA Ops:
  0.6 1.3 collective-permute-start.1
  1.9 4.6 %collective-permute-start = (bf16[160,2048]{1,0:T(8,128)(2,1)}, bf16[160,2048]{1,0:T(8,128)(2,1)S(1)}, u32[]{:S(2)}, u32[]{:S(2)}) collective-permute-start(bf16[160,2048]{1,0:T(8,128)(2,1)} %bitcast.32), channel_id=1, source_target_pairs={{0,4},{4,8},{8,12},{1,5},{5,9},{9,13},{2,6},{6,10},{10,14},{3,7},{... | collective-permute-start | bytes 1966088 | tf_op jit(solution)/shard_map/ppermute | solution.py:385
  6.5 0.8 slice_reduce_fusion
  7.3 0.8 reshape.68
  8.8 0.9 copy-done
  9.7 0.9 copy-done.2
  10.6 1.1 copy-done.5
  11.7 6.6 %own_part.1 = (f32[160,2048]{1,0:T(8,128)S(1)}, f32[160,128]{1,0:T(8,128)S(1)}) custom-call(s32[137]{0:T(256)S(1)} %pad_add_fusion.meta_ref, bf16[160,2048]{1,0:T(8,128)(2,1)S(1)} %bitcast.33, bf16[160,256]{1,0:T(8,128)(2,1)S(1)} %bitcast.27, bf16[160,256]{1,0:T(8,128)(2,1)S(1)} %bitcast.29, bf16[32,256,256]{2,1,0:T(8,128)(2,1)} %store_keys.13, ...), custom_call_target="tpu_custom_call" | custom-call | flops 21474836480 | bytes 2097152 | tf_op jit(solution)/shard_map/own_part/pallas_call | solution.py:340
  19.2 1.3 collective-permute-done.query_ref
  21.2 2.2 %copy-done.4 = bf16[32,256,256]{2,1,0:T(8,128)(2,1)S(1)} copy-done((bf16[32,256,256]{2,1,0:T(8,128)(2,1)S(1)}, bf16[32,256,256]{2,1,0:T(8,128)(2,1)}, u32[]{:S(2)}) %copy-start.4) | copy-done | bytes 4194328
  24.1 1.3 collective-permute-start.5
  25.4 15.5 %other_part.7 = bf16[160,2176]{1,0:T(8,128)(2,1)S(1)} custom-call(s32[137]{0:T(256)S(1)} %pad_add_fusion.meta_ref, bf16[160,2048]{1,0:T(8,128)(2,1)S(1)} %collective-permute-done.1.query_ref, bf16[32,256,256]{2,1,0:T(8,128)(2,1)S(1)} %copy-done.4, bf16[32,256,256]{2,1,0:T(8,128)(2,1)} %store_values.13), custom_call_target="tpu_custom_call" | custom-call | flops 21474836480 | bytes 2097152 | tf_op jit(solution)/shard_map/other_part/pallas_call | solution.py:362
  40.9 19.3 %collective-permute-start.3 = (bf16[160,2176]{1,0:T(8,128)(2,1)S(1)}, bf16[160,2176]{1,0:T(8,128)(2,1)S(1)}, u32[]{:S(2)}, u32[]{:S(2)}) collective-permute-start(bf16[160,2176]{1,0:T(8,128)(2,1)S(1)} %other_part.7), channel_id=1, source_target_pairs={{0,4},{4,8},{8,12},{1,5},{5,9},{9,13},{2,6},{6,10},{10,14},{3,7},{... | collective-permute-start | bytes 2088968 | tf_op jit(solution)/shard_map/ppermute | solution.py:385
  60.2 1.3 collective-permute-start.2
  62.2 1.3 collective-permute-start.9
  63.5 0.9 other_part.8
  64.4 32.0 %collective-permute-done.9.query_ref = bf16[160,2048]{1,0:T(8,128)(2,1)S(1)} collective-permute-done((bf16[160,2048]{1,0:T(8,128)(2,1)S(1)}, bf16[160,2048]{1,0:T(8,128)(2,1)S(1)}, u32[]{:S(2)}, u32[]{:S(2)}) %collective-permute-start.9) | collective-permute-done | bytes 655392 | tf_op jit(solution)/shard_map/ppermute | solution.py:385
  96.4 1.4 collective-permute-start.15
  97.9 1.3 collective-permute-start.12
  99.2 15.5 %other_part.9 = bf16[160,2176]{1,0:T(8,128)(2,1)S(1)} custom-call(s32[137]{0:T(256)S(1)} %pad_add_fusion.meta_ref, bf16[160,2048]{1,0:T(8,128)(2,1)S(1)} %collective-permute-done.5.query_ref, bf16[32,256,256]{2,1,0:T(8,128)(2,1)S(1)} %copy-done.4, bf16[32,256,256]{2,1,0:T(8,128)(2,1)} %store_values.13), custom_call_target="tpu_custom_call" | custom-call | flops 21474836480 | bytes 2097152 | tf_op jit(solution)/shard_map/other_part/pallas_call | solution.py:362
  114.7 1.3 collective-permute-start.7
  116.7 1.3 collective-permute-start.13
  119.4 4.5 %collective-permute-done.13 = bf16[160,512]{1,0:T(8,128)(2,1)S(1)} collective-permute-done((bf16[160,512]{1,0:T(8,128)(2,1)S(1)}, bf16[160,512]{1,0:T(8,128)(2,1)S(1)}, u32[]{:S(2)}, u32[]{:S(2)}) %collective-permute-start.13) | collective-permute-done | bytes 163872 | tf_op jit(solution)/shard_map/ppermute | solution.py:385
  123.9 1.3 collective-permute-start.14
  125.2 13.7 %other_part.11 = bf16[160,2176]{1,0:T(8,128)(2,1)S(1)} custom-call(s32[137]{0:T(256)S(1)} %pad_add_fusion.meta_ref, bf16[160,2048]{1,0:T(8,128)(2,1)S(1)} %collective-permute-done.9.query_ref, bf16[32,256,256]{2,1,0:T(8,128)(2,1)S(1)} %copy-done.4, bf16[32,256,256]{2,1,0:T(8,128)(2,1)} %store_values.13), custom_call_target="tpu_custom_call" | custom-call | flops 21474836480 | bytes 2097152 | tf_op jit(solution)/shard_map/other_part/pallas_call | solution.py:362
  139.0 1.3 collective-permute-start.6
  140.3 1.3 collective-permute-start.10
  141.6 12.5 %collective-permute-done.14 = bf16[160,512]{1,0:T(8,128)(2,1)S(1)} collective-permute-done((bf16[160,512]{1,0:T(8,128)(2,1)S(1)}, bf16[160,512]{1,0:T(8,128)(2,1)S(1)}, u32[]{:S(2)}, u32[]{:S(2)}) %collective-permute-start.14) | collective-permute-done | bytes 163872 | tf_op jit(solution)/shard_map/ppermute | solution.py:385
  154.0 6.0 %collective-permute-start.11 = (bf16[160,2176]{1,0:T(8,128)(2,1)S(1)}, bf16[160,2176]{1,0:T(8,128)(2,1)S(1)}, u32[]{:S(2)}, u32[]{:S(2)}) collective-permute-start(bf16[160,2176]{1,0:T(8,128)(2,1)S(1)} %other_part.11), channel_id=1, source_target_pairs={{0,12},{1,13},{2,14},{3,15},{16,28},{17,29},{18,30},{19,31}} | collective-permute-start | bytes 2088968 | tf_op jit(solution)/shard_map/ppermute | solution.py:385
  170.2 0.7 pad_maximum_fusion
  170.9 28.3 %collective-permute-done.6.refs_2_ = bf16[160,2176]{1,0:T(8,128)(2,1)S(1)} collective-permute-done((bf16[160,2176]{1,0:T(8,128)(2,1)S(1)}, bf16[160,2176]{1,0:T(8,128)(2,1)S(1)}, u32[]{:S(2)}, u32[]{:S(2)}) %collective-permute-start.6) | collective-permute-done | bytes 696352 | tf_op jit(solution)/shard_map/ppermute | solution.py:385
  199.3 4.4 %combine.1 = bf16[160,2048]{1,0:T(8,128)(2,1)} custom-call(s32[137]{0:T(256)S(1)} %pad_add_fusion.meta_ref, f32[160,2048]{1,0:T(8,128)S(1)} %get-tuple-element.12.own_ref, f32[160,128]{1,0:T(8,128)S(1)} %get-tuple-element.13.log_ref, bf16[160,2176]{1,0:T(8,128)(2,1)S(1)} %collective-permute-done.2.refs_0_, ...), custom_call_target="tpu_custom_call" | custom-call | tf_op jit(solution)/shard_map/combine/pallas_call | solution.py:423
  (39 shorter events, 6.6 us)
Async XLA Ops:
  0.6 18.6 %collective-permute-start.1 = (bf16[160,2048]{1,0:T(8,128)(2,1)}, bf16[160,2048]{1,0:T(8,128)(2,1)S(1)}, u32[]{:S(2)}, u32[]{:S(2)}) collective-permute-start(bf16[160,2048]{1,0:T(8,128)(2,1)} %bitcast.31), channel_id=1, source_target_pairs={{4,0},{8,4},{12,8},{5,1},{9,5},{13,9},{6,2},{10,6},{14,10},{7,3},{... | collective-permute-start | bytes 1966088 | tf_op jit(solution)/shard_map/ppermute | solution.py:385
  1.9 18.6 %collective-permute-start = (bf16[160,2048]{1,0:T(8,128)(2,1)}, bf16[160,2048]{1,0:T(8,128)(2,1)S(1)}, u32[]{:S(2)}, u32[]{:S(2)}) collective-permute-start(bf16[160,2048]{1,0:T(8,128)(2,1)} %bitcast.32), channel_id=1, source_target_pairs={{0,4},{4,8},{8,12},{1,5},{5,9},{9,13},{2,6},{6,10},{10,14},{3,7},{... | collective-permute-start | bytes 1966088 | tf_op jit(solution)/shard_map/ppermute | solution.py:385
  8.8 0.9 copy-start
  9.7 0.9 copy-start.2
  10.6 1.1 copy-start.5
  11.7 6.6 %copy-start.6 = (s32[4]{0:T(128)S(1)}, s32[4]{0:T(128)}, u32[]{:S(2)}) copy-start(s32[4]{0:T(128)} %param.17) | copy-start | bytes 52
  11.7 6.8 %copy-start.1 = (bf16[1,160,256]{2,1,0:T(8,128)(2,1)S(1)}, bf16[1,160,256]{2,1,0:T(8,128)(2,1)}, u32[]{:S(2)}) copy-start(bf16[1,160,256]{2,1,0:T(8,128)(2,1)} %param.10) | copy-start | bytes 245764
  11.7 6.8 %copy-start.3 = (bf16[1,160,256]{2,1,0:T(8,128)(2,1)S(1)}, bf16[1,160,256]{2,1,0:T(8,128)(2,1)}, u32[]{:S(2)}) copy-start(bf16[1,160,256]{2,1,0:T(8,128)(2,1)} %param.11) | copy-start | bytes 245764
  20.5 41.0 %collective-permute-start.4 = (bf16[160,2048]{1,0:T(8,128)(2,1)S(1)}, bf16[160,2048]{1,0:T(8,128)(2,1)S(1)}, u32[]{:S(2)}, u32[]{:S(2)}) collective-permute-start(bf16[160,2048]{1,0:T(8,128)(2,1)S(1)} %collective-permute-done.query_ref), channel_id=1, source_target_pairs={{4,8},{8,12},{5,9},{9,13},{6,10},{10,14},{7,11},{11,15},{20,24},{2... | collective-permute-start | bytes 1966088 | tf_op jit(solution)/shard_map/ppermute | solution.py:385
  21.2 2.2 %copy-start.4 = (bf16[32,256,256]{2,1,0:T(8,128)(2,1)S(1)}, bf16[32,256,256]{2,1,0:T(8,128)(2,1)}, u32[]{:S(2)}) copy-start(bf16[32,256,256]{2,1,0:T(8,128)(2,1)} %store_keys.13) | copy-start | bytes 12582916
  24.1 37.4 %collective-permute-start.5 = (bf16[160,2048]{1,0:T(8,128)(2,1)S(1)}, bf16[160,2048]{1,0:T(8,128)(2,1)S(1)}, u32[]{:S(2)}, u32[]{:S(2)}) collective-permute-start(bf16[160,2048]{1,0:T(8,128)(2,1)S(1)} %collective-permute-done.1.query_ref), channel_id=1, source_target_pairs={{4,0},{8,4},{5,1},{9,5},{6,2},{10,6},{7,3},{11,7},{20,16},{24,20},... | collective-permute-start | bytes 1966088 | tf_op jit(solution)/shard_map/ppermute | solution.py:385
  40.9 98.1 %collective-permute-start.3 = (bf16[160,2176]{1,0:T(8,128)(2,1)S(1)}, bf16[160,2176]{1,0:T(8,128)(2,1)S(1)}, u32[]{:S(2)}, u32[]{:S(2)}) collective-permute-start(bf16[160,2176]{1,0:T(8,128)(2,1)S(1)} %other_part.7), channel_id=1, source_target_pairs={{0,4},{4,8},{8,12},{1,5},{5,9},{9,13},{2,6},{6,10},{10,14},{3,7},{... | collective-permute-start | bytes 2088968 | tf_op jit(solution)/shard_map/ppermute | solution.py:385
  60.2 110.7 %collective-permute-start.2 = (bf16[160,2176]{1,0:T(8,128)(2,1)S(1)}, bf16[160,2176]{1,0:T(8,128)(2,1)S(1)}, u32[]{:S(2)}, u32[]{:S(2)}) collective-permute-start(bf16[160,2176]{1,0:T(8,128)(2,1)S(1)} %other_part.6), channel_id=1, source_target_pairs={{4,0},{8,4},{12,8},{5,1},{9,5},{13,9},{6,2},{10,6},{14,10},{7,3},{... | collective-permute-start | bytes 2088968 | tf_op jit(solution)/shard_map/ppermute | solution.py:385
  61.5 2.9 %collective-permute-start.8 = (bf16[160,2048]{1,0:T(8,128)(2,1)S(1)}, bf16[160,2048]{1,0:T(8,128)(2,1)S(1)}, u32[]{:S(2)}, u32[]{:S(2)}) collective-permute-start(bf16[160,2048]{1,0:T(8,128)(2,1)S(1)} %collective-permute-done.4.query_ref), channel_id=1, source_target_pairs={{8,12},{9,13},{10,14},{11,15},{24,28},{25,29},{26,30},{27,31}} | collective-permute-start | bytes 1966088 | tf_op jit(solution)/shard_map/ppermute | solution.py:385
  62.2 34.2 %collective-permute-start.9 = (bf16[160,2048]{1,0:T(8,128)(2,1)S(1)}, bf16[160,2048]{1,0:T(8,128)(2,1)S(1)}, u32[]{:S(2)}, u32[]{:S(2)}) collective-permute-start(bf16[160,2048]{1,0:T(8,128)(2,1)S(1)} %collective-permute-done.5.query_ref), channel_id=1, source_target_pairs={{4,0},{5,1},{6,2},{7,3},{20,16},{21,17},{22,18},{23,19}} | collective-permute-start | bytes 1966088 | tf_op jit(solution)/shard_map/ppermute | solution.py:385
  96.4 19.6 %collective-permute-start.15 = (bf16[160,512]{1,0:T(8,128)(2,1)S(1)}, bf16[160,512]{1,0:T(8,128)(2,1)S(1)}, u32[]{:S(2)}, u32[]{:S(2)}) collective-permute-start(bf16[160,512]{1,0:T(8,128)(2,1)S(1)} %pad_maximum_fusion.1), channel_id=1, source_target_pairs={{0,4},{4,8},{8,12},{1,5},{5,9},{9,13},{2,6},{6,10},{10,14},{3,7},{... | collective-permute-start | bytes 491528 | tf_op jit(solution)/shard_map/ppermute | solution.py:385
  97.9 18.8 %collective-permute-start.12 = (bf16[160,512]{1,0:T(8,128)(2,1)S(1)}, bf16[160,512]{1,0:T(8,128)(2,1)S(1)}, u32[]{:S(2)}, u32[]{:S(2)}) collective-permute-start(bf16[160,512]{1,0:T(8,128)(2,1)S(1)} %pad_maximum_fusion.1), channel_id=1, source_target_pairs={{4,0},{8,4},{12,8},{5,1},{9,5},{13,9},{6,2},{10,6},{14,10},{7,3},{... | collective-permute-start | bytes 491528 | tf_op jit(solution)/shard_map/ppermute | solution.py:385
  114.7 56.3 %collective-permute-start.7 = (bf16[160,2176]{1,0:T(8,128)(2,1)S(1)}, bf16[160,2176]{1,0:T(8,128)(2,1)S(1)}, u32[]{:S(2)}, u32[]{:S(2)}) collective-permute-start(bf16[160,2176]{1,0:T(8,128)(2,1)S(1)} %other_part.9), channel_id=1, source_target_pairs={{0,8},{4,12},{1,9},{5,13},{2,10},{6,14},{3,11},{7,15},{16,24},{20,... | collective-permute-start | bytes 2088968 | tf_op jit(solution)/shard_map/ppermute | solution.py:385
  116.0 2.7 %collective-permute-start.16 = (bf16[160,512]{1,0:T(8,128)(2,1)S(1)}, bf16[160,512]{1,0:T(8,128)(2,1)S(1)}, u32[]{:S(2)}, u32[]{:S(2)}) collective-permute-start(bf16[160,512]{1,0:T(8,128)(2,1)S(1)} %collective-permute-done.15), channel_id=1, source_target_pairs={{4,8},{8,12},{5,9},{9,13},{6,10},{10,14},{7,11},{11,15},{20,24},{2... | collective-permute-start | bytes 491528 | tf_op jit(solution)/shard_map/ppermute | solution.py:385
  116.7 7.2 %collective-permute-start.13 = (bf16[160,512]{1,0:T(8,128)(2,1)S(1)}, bf16[160,512]{1,0:T(8,128)(2,1)S(1)}, u32[]{:S(2)}, u32[]{:S(2)}) collective-permute-start(bf16[160,512]{1,0:T(8,128)(2,1)S(1)} %collective-permute-done.12), channel_id=1, source_target_pairs={{4,0},{8,4},{5,1},{9,5},{6,2},{10,6},{7,3},{11,7},{20,16},{24,20},... | collective-permute-start | bytes 491528 | tf_op jit(solution)/shard_map/ppermute | solution.py:385
  118.7 21.5 %collective-permute-start.17 = (bf16[160,512]{1,0:T(8,128)(2,1)S(1)}, bf16[160,512]{1,0:T(8,128)(2,1)S(1)}, u32[]{:S(2)}, u32[]{:S(2)}) collective-permute-start(bf16[160,512]{1,0:T(8,128)(2,1)S(1)} %collective-permute-done.16), channel_id=1, source_target_pairs={{8,12},{9,13},{10,14},{11,15},{24,28},{25,29},{26,30},{27,31}} | collective-permute-start | bytes 491528 | tf_op jit(solution)/shard_map/ppermute | solution.py:385
  123.9 30.1 %collective-permute-start.14 = (bf16[160,512]{1,0:T(8,128)(2,1)S(1)}, bf16[160,512]{1,0:T(8,128)(2,1)S(1)}, u32[]{:S(2)}, u32[]{:S(2)}) collective-permute-start(bf16[160,512]{1,0:T(8,128)(2,1)S(1)} %collective-permute-done.13), channel_id=1, source_target_pairs={{4,0},{5,1},{6,2},{7,3},{20,16},{21,17},{22,18},{23,19}} | collective-permute-start | bytes 491528 | tf_op jit(solution)/shard_map/ppermute | solution.py:385
  139.0 60.3 %collective-permute-start.6 = (bf16[160,2176]{1,0:T(8,128)(2,1)S(1)}, bf16[160,2176]{1,0:T(8,128)(2,1)S(1)}, u32[]{:S(2)}, u32[]{:S(2)}) collective-permute-start(bf16[160,2176]{1,0:T(8,128)(2,1)S(1)} %other_part.8), channel_id=1, source_target_pairs={{8,0},{12,4},{9,1},{13,5},{10,2},{14,6},{11,3},{15,7},{24,16},{28,... | collective-permute-start | bytes 2088968 | tf_op jit(solution)/shard_map/ppermute | solution.py:385
  140.3 59.0 %collective-permute-start.10 = (bf16[160,2176]{1,0:T(8,128)(2,1)S(1)}, bf16[160,2176]{1,0:T(8,128)(2,1)S(1)}, u32[]{:S(2)}, u32[]{:S(2)}) collective-permute-start(bf16[160,2176]{1,0:T(8,128)(2,1)S(1)} %other_part.10), channel_id=1, source_target_pairs={{12,0},{13,1},{14,2},{15,3},{28,16},{29,17},{30,18},{31,19}} | collective-permute-start | bytes 2088968 | tf_op jit(solution)/shard_map/ppermute | solution.py:385
  154.0 45.2 %collective-permute-start.11 = (bf16[160,2176]{1,0:T(8,128)(2,1)S(1)}, bf16[160,2176]{1,0:T(8,128)(2,1)S(1)}, u32[]{:S(2)}, u32[]{:S(2)}) collective-permute-start(bf16[160,2176]{1,0:T(8,128)(2,1)S(1)} %other_part.11), channel_id=1, source_target_pairs={{0,12},{1,13},{2,14},{3,15},{16,28},{17,29},{18,30},{19,31}} | collective-permute-start | bytes 2088968 | tf_op jit(solution)/shard_map/ppermute | solution.py:385
where the time goes:
time: 204 us
  waiting for transfers between devices  79.3 us (39%)
  Pallas kernels  58 us (28%)
  starting transfers between devices  47 us (23%)
  between operations  10.2 us (5%)
  local copies, waits for them, and re-layouts  7.3 us (4%)
    ppermute x18, waiting for transfers between devices, shift(): return lax.ppermute(array, 'pool', pairs)  79.3 us
    ppermute x18, starting transfers between devices, shift(): return lax.ppermute(array, 'pool', pairs)  47 us
    pallas_call x6, Pallas kernels, other_part(): pl.pallas_call(functools.partial(other_kernel, pool_size, offset), in_spe...  47 us
    pallas_call x1, Pallas kernels, own_part(): pl.pallas_call(functools.partial(own_kernel, pool_size), in_specs=[smem_s...  6.63 us
    unnamed x14, local copies, waits for them, and re-layouts  5.06 us
    pallas_call x1, Pallas kernels, shards(): pl.pallas_call(functools.partial(combine_kernel, tuple(sources), pool_siz...  4.38 us
  transfers between devices with their start and end apart: 18, of which 6 were waited for; matrix products, arithmetic and copies ran while one was open for 2% of the time, Pallas kernels for 26%

commit v1 on v0

--- a/solution.py
+++ b/solution.py
@@ -16,6 +16,7 @@
 GROUP = HEADS // KVH
 EMPTY = -1e30
 LINE = 8
+CHUNK_HEADS = 2
 SCALE = 1.0 / math.sqrt(HD)
 EXP2_SCALE = SCALE * math.log2(math.e)
 VMEM_LIMIT = 48 * 1024 * 1024
@@ -37,90 +38,111 @@
 
 
 def attend(
-    query_ref, key_ref, value_ref, count, ready, new_refs, query_rows, scores, peaks, totals, acc, put
+    load,
+    key_ref,
+    value_ref,
+    count,
+    ready,
+    new_refs,
+    new_rows,
+    query_rows,
+    scores,
+    peaks,
+    totals,
+    acc,
+    put,
 ):
-    new_rows = query_ref.shape[0]
     kv_local = key_ref.shape[2] // HD
     rows = GROUP * new_rows
+    chunks = [slice(i, i + CHUNK_HEADS * new_rows) for i in range(0, rows, CHUNK_HEADS * new_rows)]
+
+    def dot_keys(part, keys):
+        return lax.dot_general(
+            query_rows[part, :], keys, (((1,), (1,)), ((), ())), preferred_element_type=jnp.float32
+        )
+
+    def peak_of(block):
+        pieces = [block[:, i : i + HD] for i in range(0, block.shape[1], HD)]
+        return functools.reduce(jnp.maximum, pieces)
+
+    def weigh(part, block, values):
+        peak = peaks[part, :]
+        pieces = [
+            jnp.exp2(block[:, i : i + HD] * EXP2_SCALE - peak) for i in range(0, block.shape[1], HD)
+        ]
+        mixed = lax.dot_general(
+            jnp.concatenate(pieces, axis=1).astype(jnp.bfloat16),
+            values,
+            (((1,), (0,)), ((), ())),
+            preferred_element_type=jnp.float32,
+        )
+        return functools.reduce(jnp.add, pieces), mixed
+
     for kv in range(kv_local):
         lanes = slice(kv * HD, (kv + 1) * HD)
-        for g in range(GROUP):
-            head = kv * GROUP + g
-            query_rows[g * new_rows : (g + 1) * new_rows, :] = query_ref[
-                :, head * HD : (head + 1) * HD
-            ]
-        peaks[...] = jnp.full(peaks.shape, EMPTY, jnp.float32)
-        if new_refs is not None:
+        load(kv)
+        if new_refs is None:
+            peaks[...] = jnp.full(peaks.shape, EMPTY, jnp.float32)
+        else:
             new_key_ref, new_value_ref, new_scores = new_refs
-            fresh = lax.dot_general(
-                query_rows[...],
-                new_key_ref[:, lanes],
-                (((1,), (1,)), ((), ())),
-                preferred_element_type=jnp.float32,
+            shape = (new_rows, new_key_ref.shape[0])
+            seen = lax.broadcasted_iota(jnp.int32, shape, 1) <= lax.broadcasted_iota(
+                jnp.int32, shape, 0
             )
-            row = lax.broadcasted_iota(jnp.int32, (new_rows, new_key_ref.shape[0]), 0)
-            column = lax.broadcasted_iota(jnp.int32, (new_rows, new_key_ref.shape[0]), 1)
             for g in range(GROUP):
                 part = slice(g * new_rows, (g + 1) * new_rows)
-                masked = jnp.where(column <= row, fresh[part], EMPTY)
-                new_scores[part, :] = masked
-                peaks[part, :] = jnp.maximum(masked[:, :HD], masked[:, HD:])
+                block = jnp.where(seen, dot_keys(part, new_key_ref[:, lanes]), EMPTY)
+                new_scores[part, :] = block
+                peaks[part, :] = peak_of(block)
 
         def score_block(entry, carry):
             if kv == 0:
                 ready(entry)
-            block = lax.dot_general(
-                query_rows[...],
-                key_ref[entry, :, lanes],
-                (((1,), (1,)), ((), ())),
-                preferred_element_type=jnp.float32,
-            )
-            scores[entry] = block
-            best = peaks[...]
-            for piece in range(block.shape[1] // HD):
-                best = jnp.maximum(best, block[:, piece * HD : (piece + 1) * HD])
-            peaks[...] = best
+            keys = key_ref[entry, :, lanes]
+            for part in chunks:
+                block = dot_keys(part, keys)
+                scores[entry, part, :] = block
+                peaks[part, :] = jnp.maximum(peaks[part, :], peak_of(block))
             return carry
 
         lax.fori_loop(0, count, score_block, 0)
-        peak = jnp.max(peaks[...], axis=1, keepdims=True)
-        peaks[...] = jnp.broadcast_to(peak, peaks.shape)
-
-        def weigh(block, values):
-            weights = jnp.exp2((block - peaks[:, 0:1]) * EXP2_SCALE)
-            total = weights[:, :HD]
-            for piece in range(1, weights.shape[1] // HD):
-                total = total + weights[:, piece * HD : (piece + 1) * HD]
-            mixed = lax.dot_general(
-                weights.astype(jnp.bfloat16),
-                values,
-                (((1,), (0,)), ((), ())),
-                preferred_element_type=jnp.float32,
-            )
-            return total, mixed
-
-        if new_refs is not None:
-            total, mixed = weigh(new_scores[...], new_value_ref[:, lanes])
-            totals[...] = total
-            acc[...] = mixed
-        else:
-            totals[...] = jnp.zeros(totals.shape, jnp.float32)
-            acc[...] = jnp.zeros(acc.shape, jnp.float32)
+        for part in chunks:
+            peak = jnp.max(peaks[part, :], axis=1, keepdims=True) * EXP2_SCALE
+            peaks[part, :] = jnp.broadcast_to(peak, (part.stop - part.start, HD))
+            if new_refs is None:
+                totals[part, :] = jnp.zeros((part.stop - part.start, HD), jnp.float32)
+                acc[part, :] = jnp.zeros((part.stop - part.start, HD), jnp.float32)
+            else:
+                total, mixed = weigh(part, new_scores[part, :], new_value_ref[:, lanes])
+                totals[part, :] = total
+                acc[part, :] = mixed
 
         def weigh_block(entry, carry):
-            total, mixed = weigh(scores[entry], value_ref[entry, :, lanes])
-            totals[...] += total
-            acc[...] += mixed
+            values = value_ref[entry, :, lanes]
+            for part in chunks:
+                total, mixed = weigh(part, scores[entry, part, :], values)
+                totals[part, :] += total
+                acc[part, :] += mixed
             return carry
 
         lax.fori_loop(0, count, weigh_block, 0)
-        total = jnp.sum(totals[...], axis=1, keepdims=True)
-        safe = jnp.where(total > 0, total, 1.0)
-        out = acc[...] / safe
-        log_total = jnp.where(total > 0, peak * SCALE + jnp.log(safe), EMPTY)
         for g in range(GROUP):
             part = slice(g * new_rows, (g + 1) * new_rows)
-            put(kv * GROUP + g, out[part], log_total[part])
+            total = jnp.sum(totals[part, :], axis=1, keepdims=True)
+            safe = jnp.where(total > 0, total, 1.0)
+            log_total = jnp.where(
+                total > 0, peaks[part, 0:1] * math.log(2.0) + jnp.log(safe), EMPTY
+            )
+            put(kv * GROUP + g, acc[part, :] * (1.0 / safe), log_total)
+
+
+def load_heads(query_ref, query_rows, kv):
+    new_rows = query_ref.shape[0]
+    for g in range(GROUP):
+        head = kv * GROUP + g
+        query_rows[g * new_rows : (g + 1) * new_rows, :] = query_ref[
+            :, head * HD : (head + 1) * HD
+        ]
 
 
 def add_lane(tile, heads, head, column):
@@ -198,12 +220,13 @@
         log_ref[...] = add_lane(log_ref[...], heads, head, log_total)
 
     attend(
-        query_ref,
+        functools.partial(load_heads, query_ref, query_rows),
         key_buf,
         value_buf,
         count,
         ready,
         (new_key_buf, new_value_buf, new_scores),
+        new_rows,
         query_rows,
         scores,
         peaks,
@@ -213,49 +236,56 @@
     )
 
 
-def other_kernel(
-    pool_size,
-    offset,
-    meta_ref,
-    query_ref,
-    store_keys,
-    store_values,
-    out_ref,
-    key_buf,
-    value_buf,
-    query_rows,
-    scores,
-    peaks,
-    totals,
-    acc,
-    log_tile,
-    sems,
-):
-    if offset is None:
-        request = meta_ref[1 + 2 * pool_size + pool_size * MAXBLK]
+def other_kernel(pool_size, offsets, meta_ref, *refs):
+    query_refs = refs[: len(offsets)]
+    (
+        store_keys,
+        store_values,
+        out_ref,
+        key_buf,
+        value_buf,
+        query_rows,
+        scores,
+        peaks,
+        totals,
+        acc,
+        log_tile,
+        sems,
+    ) = refs[len(offsets) :]
+    if offsets[0] is None:
+        wanted = [meta_ref[1 + 2 * pool_size + pool_size * MAXBLK]]
     else:
-        request = meta_ref[0] + offset
-
-    @pl.when((request >= 0) & (request < pool_size))
+        wanted = [meta_ref[0] + offset for offset in offsets]
+    there = [(x >= 0) & (x < pool_size) for x in wanted]
+    request = wanted[0]
+    for other, hit in zip(wanted[1:], there[1:]):
+        request = jnp.where(hit, other, request)
+
+    @pl.when(functools.reduce(jnp.logical_or, there))
     def _():
         count, ready = fetch(
             pool_size, meta_ref, request, (store_keys, store_values), (key_buf, value_buf), sems
         )
-        width = query_ref.shape[1]
+        new_rows, width = query_refs[0].shape
         heads = width // HD
         log_tile[...] = jnp.zeros(log_tile.shape, jnp.float32)
+
+        def load(kv):
+            for query_ref, hit in zip(query_refs, there):
+                pl.when(hit)(functools.partial(load_heads, query_ref, query_rows, kv))
 
         def put(head, out, log_total):
             out_ref[:, head * HD : (head + 1) * HD] = out.astype(jnp.bfloat16)
             log_tile[...] = add_lane(log_tile[...], heads, head, log_total)
 
         attend(
-            query_ref,
+            load,
             key_buf,
             value_buf,
             count,
             ready,
             None,
+            new_rows,
             query_rows,
             scores,
             peaks,
@@ -272,9 +302,12 @@
     heads = width // HD
     logs = [log_ref[...]]
     valid = []
-    for (relative, source), part in zip(sources, refs[:-1]):
-        if relative:
-            there = (meta_ref[0] + source >= 0) & (meta_ref[0] + source < pool_size)
+    for (offsets, source), part in zip(sources, refs[:-1]):
+        if offsets:
+            wanted = [meta_ref[0] + offset for offset in offsets]
+            there = functools.reduce(
+                jnp.logical_or, [(x >= 0) & (x < pool_size) for x in wanted]
+            )
         else:
             there = meta_ref[0] != source
         valid.append(there)
@@ -320,14 +353,11 @@
     meta = jnp.concatenate(
         [my_index.reshape(1), prefix_blocks, hit_store[:, 0], hit_slot.reshape(-1)]
     )
-    flops = 4 * rows * block_len * kv_width * capacity
     smem_spec = pl.BlockSpec(memory_space=pltpu.SMEM)
-    any_spec = pl.BlockSpec(memory_space=pl.ANY)
+    hbm_spec = pl.BlockSpec(memory_space=pltpu.HBM)
     vmem_spec = pl.BlockSpec(memory_space=pltpu.VMEM)
     params = pltpu.CompilerParams(vmem_limit_bytes=VMEM_LIMIT)
-    cost = pl.CostEstimate(
-        flops=8 * flops, bytes_accessed=4 * capacity * block_len * kv_width, transcendentals=0
-    )
+    cost = pl.CostEstimate(flops=rows, bytes_accessed=rows, transcendentals=0)
     buffers = [pltpu.VMEM((capacity, block_len, kv_width), jnp.bfloat16)] * 2
     work = [
         pltpu.VMEM((rows, HD), jnp.bfloat16),
@@ -339,7 +369,7 @@
     def own_part(query):
         return pl.pallas_call(
             functools.partial(own_kernel, pool_size),
-            in_specs=[smem_spec] + [vmem_spec] * 3 + [any_spec] * 2,
+            in_specs=[smem_spec] + [vmem_spec] * 3 + [hbm_spec] * 2,
             out_specs=[vmem_spec] * 2,
             scratch_shapes=[
                 *buffers,
@@ -358,10 +388,10 @@
             name="own_part",
         )(meta, query, new_keys[0], new_values[0], store_keys, store_values)
 
-    def other_part(offset, query, meta=meta):
+    def other_part(offsets, held, meta=meta):
         return pl.pallas_call(
-            functools.partial(other_kernel, pool_size, offset),
-            in_specs=[smem_spec, vmem_spec] + [any_spec] * 2,
+            functools.partial(other_kernel, pool_size, offsets),
+            in_specs=[smem_spec] + [vmem_spec] * len(held) + [hbm_spec] * 2,
             out_specs=vmem_spec,
             scratch_shapes=[
                 *buffers,
@@ -374,13 +404,16 @@
             compiler_params=params,
             cost_estimate=cost,
             name="other_part",
-        )(meta, query, store_keys, store_values)
-
-    def shift(array, distance, first=0):
+        )(meta, *held, store_keys, store_values)
+
+    def inside(index):
+        return 0 <= index < pool_size
+
+    def forward(array, distance, first):
         pairs = [
             (i, i + distance)
             for i in range(pool_size)
-            if 0 <= i + distance < pool_size and 0 <= i - first < pool_size
+            if inside(i + distance) and inside(i - first)
         ]
         return lax.ppermute(array, "pool", pairs)
 
@@ -391,34 +424,40 @@
         sources = []
         parts = []
         right, left = query, query
+        done = (own_out, own_log)
         for step in range(1, pool_size):
-            right = shift(right, 1, step - 1)
-            left = shift(left, -1, 1 - step)
-            right, left = lax.optimization_barrier((right, left))
-            for offset, held in ((-step, right), (step, left)):
-                packed = other_part(offset, held)
-                sources.append((True, -offset))
-                parts.append(shift(packed, offset, -offset))
+            right = forward(right, 1, step - 1)
+            left = forward(left, -1, 1 - step)
+            right, left, *done = lax.optimization_barrier((right, left, *done))
+            if step == 1:
+                own_out, own_log = done
+            done = []
+            if 2 * step < pool_size:
+                groups = [((-step,), (right,)), ((step,), (left,))]
+            else:
+                groups = [((-step, step), (right, left))]
+            for offsets, held in groups:
+                packed = other_part(offsets, held)
+                done.append(packed)
+                pairs = [(i, i + x) for x in offsets for i in range(pool_size) if inside(i + x)]
+                parts.append(lax.ppermute(packed, "pool", pairs))
+                sources.append((tuple(-x for x in offsets), None))
         fresh, right = lax.optimization_barrier((fresh, right))
-        moved = [(my_index, fresh)]
-        right, left = fresh, fresh
-        for step in range(1, pool_size):
-            right = shift(right, 1, step - 1)
-            left = shift(left, -1, 1 - step)
-            moved.append((my_index - step, right))
-            moved.append((my_index + step, left))
+        aimed = jnp.where(
+            (jnp.arange(pool_size) == decode_owner[my_index])[:, None, None], fresh[None], 0
+        )
+        moved = lax.all_to_all(aimed, "pool", split_axis=0, concat_axis=0, tiled=True)
     else:
         gathered = lax.all_gather(query, "pool", axis=0, tiled=False)
         packed = lax.map(
-            lambda pair: other_part(None, pair[0], jnp.concatenate([meta, pair[1].reshape(1)])),
+            lambda pair: other_part(
+                (None,), (pair[0],), jnp.concatenate([meta, pair[1].reshape(1)])
+            ),
             (gathered, jnp.arange(pool_size, dtype=jnp.int32)),
         )
         parts = lax.all_to_all(packed, "pool", split_axis=0, concat_axis=0, tiled=True)
-        sources = [(False, source) for source in range(pool_size)]
-        moved = [
-            (jnp.int32(source), array)
-            for source, array in enumerate(lax.all_gather(fresh, "pool", axis=0, tiled=False))
-        ]
+        sources = [(None, source) for source in range(pool_size)]
+        moved = lax.all_gather(fresh, "pool", axis=0, tiled=False)
 
     attended = pl.pallas_call(
         functools.partial(combine_kernel, tuple(sources), pool_size),
@@ -431,15 +470,11 @@
 
     mine = decode_owner == my_index
     rank = jnp.cumsum(mine) - 1
-    places = jnp.where(mine, rank, CAPP)
-    padded_places = jnp.concatenate(
-        [jnp.full((pool_size,), CAPP), places, jnp.full((pool_size,), CAPP)]
-    )
     pushed = []
     for place_id in range(CAPP):
         total = jnp.zeros(fresh.shape, fresh.dtype)
-        for source, array in moved:
-            total = jnp.where(padded_places[source + pool_size] == place_id, array, total)
+        for source in range(pool_size):
+            total = jnp.where(mine[source] & (rank[source] == place_id), moved[source], total)
         pushed.append(total)
     pushed = jnp.stack(pushed)
     return (attended[None], pushed[:, :, :kv_width], pushed[:, :, kv_width:])

time: 204 us -> 173 us (0.85)
  the two profiles are of different devices: /device:TPU:6 before, /device:TPU:4 now
where the time goes in v1:
time: 173 us; the launch traced here: 175 us
  Pallas kernels  64.1 us (37%)
  waiting for transfers between devices  46.4 us (27%)
  starting transfers between devices  37.4 us (22%)
  local copies, waits for them, and re-layouts  11.3 us (7%)
  between operations  11 us (6%)
  other arithmetic  4.51 us (3%)
    pallas_call x4, Pallas kernels, other_part(): pl.pallas_call(functools.partial(other_kernel, pool_size, offsets), in_sp...  43.8 us
    ppermute x4, waiting for transfers between devices, shards(): parts.append(lax.ppermute(packed, 'pool', pairs))  32.7 us
    pallas_call x1, Pallas kernels, own_part(): pl.pallas_call(functools.partial(own_kernel, pool_size), in_specs=[smem_s...  15.6 us
    all_to_all x1, starting transfers between devices, shards(): lax.all_to_all(aimed, 'pool', split_axis=0, concat_axis=0, tiled=True)  14 us
    ppermute x6, waiting for transfers between devices, forward(): return lax.ppermute(array, 'pool', pairs)  13.6 us
    ppermute x4, starting transfers between devices, shards(): parts.append(lax.ppermute(packed, 'pool', pairs))  13 us
    ppermute x6, starting transfers between devices, forward(): return lax.ppermute(array, 'pool', pairs)  10.4 us
    unnamed x22, local copies, waits for them, and re-layouts  7.89 us
  transfers between devices with their start and end apart: 11, of which 3 were waited for; matrix products, arithmetic and copies ran while one was open for 3% of the time, Pallas kernels for 37%

profile of v1, /device:TPU:4, one launch (start us, length us, event | category | flops | bytes accessed | tf_op | source)
XLA Modules:
  0.0 174.7 jit_solution(14997524944529648486)
XLA Ops:
  0.6 3.5 %collective-permute-start = (bf16[160,2048]{1,0:T(8,128)(2,1)}, bf16[160,2048]{1,0:T(8,128)(2,1)S(1)}, u32[]{:S(2)}, u32[]{:S(2)}) collective-permute-start(bf16[160,2048]{1,0:T(8,128)(2,1)} %bitcast.24), channel_id=1, source_target_pairs={{0,4},{4,8},{8,12},{1,5},{5,9},{9,13},{2,6},{6,10},{10,14},{3,7},{... | collective-permute-start | bytes 1966088 | tf_op jit(solution)/shard_map/ppermute | solution.py:418
  4.2 1.3 collective-permute-start.1
  5.5 0.8 reshape.89
  6.2 0.8 slice_reduce_fusion
  7.0 0.7 pad_add_fusion.meta_ref
  7.8 1.1 copy-done.3
  8.9 0.9 copy-done.4
  9.7 0.9 copy-done.6
  10.6 15.6 %own_part.1 = (f32[160,2048]{1,0:T(8,128)S(1)}, f32[160,128]{1,0:T(8,128)S(1)}) custom-call(s32[137]{0:T(256)S(1)} %pad_add_fusion.meta_ref, bf16[160,2048]{1,0:T(8,128)(2,1)S(1)} %bitcast.26, bf16[160,256]{1,0:T(8,128)(2,1)S(1)} %bitcast.27, bf16[160,256]{1,0:T(8,128)(2,1)S(1)} %bitcast.29, bf16[32,256,256]{2,1,0:T(8,128)(2,1)} %refs_2_.7, ...), custom_call_target="tpu_custom_call" | custom-call | flops 1280 | bytes 1280 | tf_op jit(solution)/shard_map/own_part/pallas_call | solution.py:370
  26.9 1.5 collective-permute-start.4
  28.4 1.3 collective-permute-start.5
  29.7 14.4 %other_part.5 = bf16[160,2176]{1,0:T(8,128)(2,1)S(1)} custom-call(s32[137]{0:T(256)S(1)} %pad_add_fusion.meta_ref, bf16[160,2048]{1,0:T(8,128)(2,1)} %collective-permute-done.1.refs_0_, bf16[32,256,256]{2,1,0:T(8,128)(2,1)S(1)} %copy-done, bf16[32,256,256]{2,1,0:T(8,128)(2,1)} %refs_3_.3), custom_call_target="tpu_custom_call" | custom-call | flops 1280 | bytes 1280 | tf_op jit(solution)/shard_map/other_part/pallas_call | solution.py:392
  44.1 0.7 other_part.4
  44.8 1.9 %collective-permute-done.5.refs_1_ = bf16[160,2048]{1,0:T(8,128)(2,1)} collective-permute-done((bf16[160,2048]{1,0:T(8,128)(2,1)}, bf16[160,2048]{1,0:T(8,128)(2,1)}, u32[]{:S(2)}, u32[]{:S(2)}) %collective-permute-start.5) | collective-permute-done | bytes 655392 | tf_op jit(solution)/shard_map/ppermute | solution.py:418
  46.8 1.5 collective-permute-start.7
  48.3 1.3 collective-permute-start.8
  50.9 2.2 %copy-done.1 = bf16[32,256,256]{2,1,0:T(8,128)(2,1)S(1)} copy-done((bf16[32,256,256]{2,1,0:T(8,128)(2,1)S(1)}, bf16[32,256,256]{2,1,0:T(8,128)(2,1)}, u32[]{:S(2)}) %copy-start.1) | copy-done | bytes 4194328
  53.1 11.6 %other_part.6 = bf16[160,2176]{1,0:T(8,128)(2,1)S(1)} custom-call(s32[137]{0:T(256)S(1)} %pad_add_fusion.meta_ref, bf16[160,2048]{1,0:T(8,128)(2,1)} %collective-permute-done.4.refs_0_, bf16[160,2048]{1,0:T(8,128)(2,1)} %collective-permute-done.5.refs_1_, bf16[32,256,256]{2,1,0:T(8,128)(2,1)S(1)} %copy-done.1, bf16[32,256,256]{2,1,0:T(8,128)(2,1)} %refs_3_.3), custom_call_target="tpu_custom_call" | custom-call | flops 1280 | bytes 1280 | tf_op jit(solution)/shard_map/other_part/pallas_call | solution.py:392
  64.7 11.7 %collective-permute-done.8.refs_1_ = bf16[160,2048]{1,0:T(8,128)(2,1)} collective-permute-done((bf16[160,2048]{1,0:T(8,128)(2,1)}, bf16[160,2048]{1,0:T(8,128)(2,1)}, u32[]{:S(2)}, u32[]{:S(2)}) %collective-permute-start.8) | collective-permute-done | bytes 655392 | tf_op jit(solution)/shard_map/ppermute | solution.py:418
  76.4 1.0 broadcast_select_fusion
  77.3 14.0 %all-to-all-start = ((bf16[4,160,512]{2,1,0:T(8,128)(2,1)}), bf16[4,160,512]{2,1,0:T(8,128)(2,1)}, u32[]{:S(2)}, u32[]{:S(2)}) async-start(bf16[4,160,512]{2,1,0:T(8,128)(2,1)} %broadcast_select_fusion), calls=%async_computation | async-start | bytes 1310720 | tf_op jit(solution)/shard_map/all_to_all | solution.py:449
  91.3 4.8 %collective-permute-start.3 = (bf16[160,2176]{1,0:T(8,128)(2,1)S(1)}, bf16[160,2176]{1,0:T(8,128)(2,1)}, u32[]{:S(2)}, u32[]{:S(2)}) collective-permute-start(bf16[160,2176]{1,0:T(8,128)(2,1)S(1)} %other_part.5), channel_id=1, source_target_pairs={{0,4},{4,8},{8,12},{1,5},{5,9},{9,13},{2,6},{6,10},{10,14},{3,7},{... | collective-permute-start | bytes 2088968 | tf_op jit(solution)/shard_map/ppermute | solution.py:443
  96.1 1.3 collective-permute-start.2
  97.4 2.7 %collective-permute-start.6 = (bf16[160,2176]{1,0:T(8,128)(2,1)S(1)}, bf16[160,2176]{1,0:T(8,128)(2,1)}, u32[]{:S(2)}, u32[]{:S(2)}) collective-permute-start(bf16[160,2176]{1,0:T(8,128)(2,1)S(1)} %other_part.6), channel_id=1, source_target_pairs={{8,0},{12,4},{0,8},{4,12},{9,1},{13,5},{1,9},{5,13},{10,2},{14,6},... | collective-permute-start | bytes 2088968 | tf_op jit(solution)/shard_map/ppermute | solution.py:443
  100.1 2.2 %copy-done.2 = bf16[32,256,256]{2,1,0:T(8,128)(2,1)S(1)} copy-done((bf16[32,256,256]{2,1,0:T(8,128)(2,1)S(1)}, bf16[32,256,256]{2,1,0:T(8,128)(2,1)}, u32[]{:S(2)}) %copy-start.2) | copy-done | bytes 4194328
  102.3 17.2 %other_part.7 = bf16[160,2176]{1,0:T(8,128)(2,1)} custom-call(s32[137]{0:T(256)S(1)} %pad_add_fusion.meta_ref, bf16[160,2048]{1,0:T(8,128)(2,1)} %collective-permute-done.7.refs_0_, bf16[160,2048]{1,0:T(8,128)(2,1)} %collective-permute-done.8.refs_1_, bf16[32,256,256]{2,1,0:T(8,128)(2,1)S(1)} %copy-done.2, bf16[32,256,256]{2,1,0:T(8,128)(2,1)} %refs_3_.3), custom_call_target="tpu_custom_call" | custom-call | flops 1280 | bytes 1280 | tf_op jit(solution)/shard_map/other_part/pallas_call | solution.py:392
  119.5 4.2 %collective-permute-start.9 = (bf16[160,2176]{1,0:T(8,128)(2,1)}, bf16[160,2176]{1,0:T(8,128)(2,1)}, u32[]{:S(2)}, u32[]{:S(2)}) collective-permute-start(bf16[160,2176]{1,0:T(8,128)(2,1)} %other_part.7), channel_id=1, source_target_pairs={{12,0},{0,12},{13,1},{1,13},{14,2},{2,14},{15,3},{3,15},{28,16},{1... | collective-permute-start | bytes 2088968 | tf_op jit(solution)/shard_map/ppermute | solution.py:443
  129.5 0.7 fusion.2
  135.4 32.7 %collective-permute-done.6.refs_2_ = bf16[160,2176]{1,0:T(8,128)(2,1)} collective-permute-done((bf16[160,2176]{1,0:T(8,128)(2,1)S(1)}, bf16[160,2176]{1,0:T(8,128)(2,1)}, u32[]{:S(2)}, u32[]{:S(2)}) %collective-permute-start.6) | collective-permute-done | bytes 696352 | tf_op jit(solution)/shard_map/ppermute | solution.py:443
  168.1 4.7 %combine.1 = bf16[160,2048]{1,0:T(8,128)(2,1)} custom-call(s32[137]{0:T(256)S(1)} %pad_add_fusion.meta_ref, f32[160,2048]{1,0:T(8,128)S(1)} %get-tuple-element.16.own_ref, f32[160,128]{1,0:T(8,128)S(1)} %copy-done.9, bf16[160,2176]{1,0:T(8,128)(2,1)} %collective-permute-done.2.refs_0_, bf16[160,2176]{1,0:T(8,128)(2,1)} %collective-permute-done.3.refs_1_, ...), custom_call_target="tpu_custom_call" | custom-call | tf_op jit(solution)/shard_map/combine/pallas_call | solution.py:462
  172.8 1.2 select_select_fusion
  174.0 0.7 pad_maximum_fusion
  (32 shorter events, 2.7 us)
Async XLA Ops:
  0.6 26.2 %collective-permute-start = (bf16[160,2048]{1,0:T(8,128)(2,1)}, bf16[160,2048]{1,0:T(8,128)(2,1)S(1)}, u32[]{:S(2)}, u32[]{:S(2)}) collective-permute-start(bf16[160,2048]{1,0:T(8,128)(2,1)} %bitcast.24), channel_id=1, source_target_pairs={{0,4},{4,8},{8,12},{1,5},{5,9},{9,13},{2,6},{6,10},{10,14},{3,7},{... | collective-permute-start | bytes 1966088 | tf_op jit(solution)/shard_map/ppermute | solution.py:418
  4.2 22.7 %collective-permute-start.1 = (bf16[160,2048]{1,0:T(8,128)(2,1)}, bf16[160,2048]{1,0:T(8,128)(2,1)}, u32[]{:S(2)}, u32[]{:S(2)}) collective-permute-start(bf16[160,2048]{1,0:T(8,128)(2,1)} %bitcast.25), channel_id=1, source_target_pairs={{4,0},{8,4},{12,8},{5,1},{9,5},{13,9},{6,2},{10,6},{14,10},{7,3},{... | collective-permute-start | bytes 1966088 | tf_op jit(solution)/shard_map/ppermute | solution.py:418
  7.8 1.1 copy-start.3
  8.9 0.9 copy-start.4
  9.7 0.9 copy-start.6
  10.6 19.0 %copy-start = (bf16[32,256,256]{2,1,0:T(8,128)(2,1)S(1)}, bf16[32,256,256]{2,1,0:T(8,128)(2,1)}, u32[]{:S(2)}) copy-start(bf16[32,256,256]{2,1,0:T(8,128)(2,1)} %refs_2_.7) | copy-start | bytes 12582916
  26.2 0.6 copy-start.8
  26.9 18.0 %collective-permute-start.4 = (bf16[160,2048]{1,0:T(8,128)(2,1)S(1)}, bf16[160,2048]{1,0:T(8,128)(2,1)}, u32[]{:S(2)}, u32[]{:S(2)}) collective-permute-start(bf16[160,2048]{1,0:T(8,128)(2,1)S(1)} %collective-permute-done.refs_0_), channel_id=1, source_target_pairs={{4,8},{8,12},{5,9},{9,13},{6,10},{10,14},{7,11},{11,15},{20,24},{2... | collective-permute-start | bytes 1966088 | tf_op jit(solution)/shard_map/ppermute | solution.py:418
  28.4 18.4 %collective-permute-start.5 = (bf16[160,2048]{1,0:T(8,128)(2,1)}, bf16[160,2048]{1,0:T(8,128)(2,1)}, u32[]{:S(2)}, u32[]{:S(2)}) collective-permute-start(bf16[160,2048]{1,0:T(8,128)(2,1)} %collective-permute-done.1.refs_0_), channel_id=1, source_target_pairs={{4,0},{8,4},{5,1},{9,5},{6,2},{10,6},{7,3},{11,7},{20,16},{24,20},... | collective-permute-start | bytes 1966088 | tf_op jit(solution)/shard_map/ppermute | solution.py:418
  44.1 5.5 %copy-start.10 = (s32[4]{0:T(128)S(1)}, s32[4]{0:T(128)}, u32[]{:S(2)}) copy-start(s32[4]{0:T(128)} %param.17) | copy-start | bytes 52
  44.1 6.8 %copy-start.5 = (bf16[1,160,256]{2,1,0:T(8,128)(2,1)S(1)}, bf16[1,160,256]{2,1,0:T(8,128)(2,1)}, u32[]{:S(2)}) copy-start(bf16[1,160,256]{2,1,0:T(8,128)(2,1)} %param.10) | copy-start | bytes 245764
  44.1 6.7 %copy-start.7 = (bf16[1,160,256]{2,1,0:T(8,128)(2,1)S(1)}, bf16[1,160,256]{2,1,0:T(8,128)(2,1)}, u32[]{:S(2)}) copy-start(bf16[1,160,256]{2,1,0:T(8,128)(2,1)} %param.11) | copy-start | bytes 245764
  46.8 17.9 %collective-permute-start.7 = (bf16[160,2048]{1,0:T(8,128)(2,1)}, bf16[160,2048]{1,0:T(8,128)(2,1)}, u32[]{:S(2)}, u32[]{:S(2)}) collective-permute-start(bf16[160,2048]{1,0:T(8,128)(2,1)} %collective-permute-done.4.refs_0_), channel_id=1, source_target_pairs={{8,12},{9,13},{10,14},{11,15},{24,28},{25,29},{26,30},{27,31}} | collective-permute-start | bytes 1966088 | tf_op jit(solution)/shard_map/ppermute | solution.py:418
  48.3 28.1 %collective-permute-start.8 = (bf16[160,2048]{1,0:T(8,128)(2,1)}, bf16[160,2048]{1,0:T(8,128)(2,1)}, u32[]{:S(2)}, u32[]{:S(2)}) collective-permute-start(bf16[160,2048]{1,0:T(8,128)(2,1)} %collective-permute-done.5.refs_1_), channel_id=1, source_target_pairs={{4,0},{5,1},{6,2},{7,3},{20,16},{21,17},{22,18},{23,19}} | collective-permute-start | bytes 1966088 | tf_op jit(solution)/shard_map/ppermute | solution.py:418
  50.9 2.2 %copy-start.1 = (bf16[32,256,256]{2,1,0:T(8,128)(2,1)S(1)}, bf16[32,256,256]{2,1,0:T(8,128)(2,1)}, u32[]{:S(2)}) copy-start(bf16[32,256,256]{2,1,0:T(8,128)(2,1)} %refs_2_.7) | copy-start | bytes 12582916
  77.3 90.7 %copy-start.9 = (f32[160,128]{1,0:T(8,128)S(1)}, f32[160,128]{1,0:T(8,128)}, u32[]{:S(2)}) copy-start(f32[160,128]{1,0:T(8,128)} %copy-done.8) | copy-start | bytes 245764
  77.3 95.4 %all-to-all-start = ((bf16[4,160,512]{2,1,0:T(8,128)(2,1)}), bf16[4,160,512]{2,1,0:T(8,128)(2,1)}, u32[]{:S(2)}, u32[]{:S(2)}) async-start(bf16[4,160,512]{2,1,0:T(8,128)(2,1)} %broadcast_select_fusion), calls=%async_computation | async-start | bytes 1310720 | tf_op jit(solution)/shard_map/all_to_all | solution.py:449
  91.3 44.0 %collective-permute-start.3 = (bf16[160,2176]{1,0:T(8,128)(2,1)S(1)}, bf16[160,2176]{1,0:T(8,128)(2,1)}, u32[]{:S(2)}, u32[]{:S(2)}) collective-permute-start(bf16[160,2176]{1,0:T(8,128)(2,1)S(1)} %other_part.5), channel_id=1, source_target_pairs={{0,4},{4,8},{8,12},{1,5},{5,9},{9,13},{2,6},{6,10},{10,14},{3,7},{... | collective-permute-start | bytes 2088968 | tf_op jit(solution)/shard_map/ppermute | solution.py:443
  96.1 39.2 %collective-permute-start.2 = (bf16[160,2176]{1,0:T(8,128)(2,1)S(1)}, bf16[160,2176]{1,0:T(8,128)(2,1)}, u32[]{:S(2)}, u32[]{:S(2)}) collective-permute-start(bf16[160,2176]{1,0:T(8,128)(2,1)S(1)} %other_part.4), channel_id=1, source_target_pairs={{4,0},{8,4},{12,8},{5,1},{9,5},{13,9},{6,2},{10,6},{14,10},{7,3},{... | collective-permute-start | bytes 2088968 | tf_op jit(solution)/shard_map/ppermute | solution.py:443
  97.4 70.7 %collective-permute-start.6 = (bf16[160,2176]{1,0:T(8,128)(2,1)S(1)}, bf16[160,2176]{1,0:T(8,128)(2,1)}, u32[]{:S(2)}, u32[]{:S(2)}) collective-permute-start(bf16[160,2176]{1,0:T(8,128)(2,1)S(1)} %other_part.6), channel_id=1, source_target_pairs={{8,0},{12,4},{0,8},{4,12},{9,1},{13,5},{1,9},{5,13},{10,2},{14,6},... | collective-permute-start | bytes 2088968 | tf_op jit(solution)/shard_map/ppermute | solution.py:443
  100.1 2.2 %copy-start.2 = (bf16[32,256,256]{2,1,0:T(8,128)(2,1)S(1)}, bf16[32,256,256]{2,1,0:T(8,128)(2,1)}, u32[]{:S(2)}) copy-start(bf16[32,256,256]{2,1,0:T(8,128)(2,1)} %refs_2_.7) | copy-start | bytes 12582916
  119.5 48.6 %collective-permute-start.9 = (bf16[160,2176]{1,0:T(8,128)(2,1)}, bf16[160,2176]{1,0:T(8,128)(2,1)}, u32[]{:S(2)}, u32[]{:S(2)}) collective-permute-start(bf16[160,2176]{1,0:T(8,128)(2,1)} %other_part.7), channel_id=1, source_target_pairs={{12,0},{0,12},{13,1},{1,13},{14,2},{2,14},{15,3},{3,15},{28,16},{1... | collective-permute-start | bytes 2088968 | tf_op jit(solution)/shard_map/ppermute | solution.py:443

commit v2 on v1

--- a/solution.py
+++ b/solution.py
@@ -16,7 +16,7 @@
 GROUP = HEADS // KVH
 EMPTY = -1e30
 LINE = 8
-CHUNK_HEADS = 2
+TILE = 256
 SCALE = 1.0 / math.sqrt(HD)
 EXP2_SCALE = SCALE * math.log2(math.e)
 VMEM_LIMIT = 48 * 1024 * 1024
@@ -37,112 +37,74 @@
     ]
 
 
-def attend(
-    load,
-    key_ref,
-    value_ref,
-    count,
-    ready,
-    new_refs,
-    new_rows,
-    query_rows,
-    scores,
-    peaks,
-    totals,
-    acc,
-    put,
-):
-    kv_local = key_ref.shape[2] // HD
-    rows = GROUP * new_rows
-    chunks = [slice(i, i + CHUNK_HEADS * new_rows) for i in range(0, rows, CHUNK_HEADS * new_rows)]
-
-    def dot_keys(part, keys):
-        return lax.dot_general(
-            query_rows[part, :], keys, (((1,), (1,)), ((), ())), preferred_element_type=jnp.float32
-        )
-
-    def peak_of(block):
-        pieces = [block[:, i : i + HD] for i in range(0, block.shape[1], HD)]
-        return functools.reduce(jnp.maximum, pieces)
-
-    def weigh(part, block, values):
-        peak = peaks[part, :]
-        pieces = [
-            jnp.exp2(block[:, i : i + HD] * EXP2_SCALE - peak) for i in range(0, block.shape[1], HD)
-        ]
-        mixed = lax.dot_general(
-            jnp.concatenate(pieces, axis=1).astype(jnp.bfloat16),
-            values,
-            (((1,), (0,)), ((), ())),
-            preferred_element_type=jnp.float32,
-        )
-        return functools.reduce(jnp.add, pieces), mixed
-
+def attend(key_ref, value_ref, count, ready, new_refs, new_rows, columns, scores, weights, peaks, totals, acc, put):
+    kv_local, _, rows = columns.shape
+
+    def visit(kv, keys, values, seen):
+        block = lax.dot_general(
+            keys, columns[kv], (((1,), (0,)), ((), ())), preferred_element_type=jnp.float32
+        )
+        if seen is not None:
+            block = jnp.where(seen, block, EMPTY)
+        scores[kv] = block
+        turned = values.T
+        for i in range(0, rows, TILE):
+            part = slice(i, i + TILE)
+            before = peaks[kv, :, part]
+            block = scores[kv, :, part]
+            peak = jnp.maximum(before, jnp.max(block, axis=0, keepdims=True))
+            factor = jnp.exp2((before - peak) * EXP2_SCALE)
+            weight = jnp.exp2(block * EXP2_SCALE - peak[0:1] * EXP2_SCALE)
+            weights[kv, :, part] = weight.astype(jnp.bfloat16)
+            added = jnp.sum(weight.reshape(-1, 8, TILE), axis=0)
+            totals[kv, :, part] = totals[kv, :, part] * factor + added
+            peaks[kv, :, part] = peak
+            acc[kv, :, part] = acc[kv, :, part] * factor[0:1]
+        acc[kv] += lax.dot_general(
+            turned, weights[kv], (((1,), (0,)), ((), ())), preferred_element_type=jnp.float32
+        )
+
+    peaks[...] = jnp.full(peaks.shape, EMPTY, jnp.float32)
+    totals[...] = jnp.zeros(totals.shape, jnp.float32)
+    acc[...] = jnp.zeros(acc.shape, jnp.float32)
+    if new_refs is not None:
+        new_key_ref, new_value_ref = new_refs
+        shape = (new_key_ref.shape[0], rows)
+        seen = lax.broadcasted_iota(jnp.int32, shape, 0) <= lax.rem(
+            lax.broadcasted_iota(jnp.int32, (1, rows), 1), new_rows
+        )
+        for kv in range(kv_local):
+            lanes = slice(kv * HD, (kv + 1) * HD)
+            visit(kv, new_key_ref[:, lanes], new_value_ref[:, lanes], seen)
+
+    def visit_block(entry, carry):
+        ready(entry)
+        for kv in range(kv_local):
+            lanes = slice(kv * HD, (kv + 1) * HD)
+            visit(kv, key_ref[entry, :, lanes], value_ref[entry, :, lanes], None)
+        return carry
+
+    lax.fori_loop(0, count, visit_block, 0)
     for kv in range(kv_local):
-        lanes = slice(kv * HD, (kv + 1) * HD)
-        load(kv)
-        if new_refs is None:
-            peaks[...] = jnp.full(peaks.shape, EMPTY, jnp.float32)
-        else:
-            new_key_ref, new_value_ref, new_scores = new_refs
-            shape = (new_rows, new_key_ref.shape[0])
-            seen = lax.broadcasted_iota(jnp.int32, shape, 1) <= lax.broadcasted_iota(
-                jnp.int32, shape, 0
-            )
-            for g in range(GROUP):
-                part = slice(g * new_rows, (g + 1) * new_rows)
-                block = jnp.where(seen, dot_keys(part, new_key_ref[:, lanes]), EMPTY)
-                new_scores[part, :] = block
-                peaks[part, :] = peak_of(block)
-
-        def score_block(entry, carry):
-            if kv == 0:
-                ready(entry)
-            keys = key_ref[entry, :, lanes]
-            for part in chunks:
-                block = dot_keys(part, keys)
-                scores[entry, part, :] = block
-                peaks[part, :] = jnp.maximum(peaks[part, :], peak_of(block))
-            return carry
-
-        lax.fori_loop(0, count, score_block, 0)
-        for part in chunks:
-            peak = jnp.max(peaks[part, :], axis=1, keepdims=True) * EXP2_SCALE
-            peaks[part, :] = jnp.broadcast_to(peak, (part.stop - part.start, HD))
-            if new_refs is None:
-                totals[part, :] = jnp.zeros((part.stop - part.start, HD), jnp.float32)
-                acc[part, :] = jnp.zeros((part.stop - part.start, HD), jnp.float32)
-            else:
-                total, mixed = weigh(part, new_scores[part, :], new_value_ref[:, lanes])
-                totals[part, :] = total
-                acc[part, :] = mixed
-
-        def weigh_block(entry, carry):
-            values = value_ref[entry, :, lanes]
-            for part in chunks:
-                total, mixed = weigh(part, scores[entry, part, :], values)
-                totals[part, :] += total
-                acc[part, :] += mixed
-            return carry
-
-        lax.fori_loop(0, count, weigh_block, 0)
+        total = jnp.sum(totals[kv], axis=0, keepdims=True)
+        safe = jnp.where(total > 0, total, 1.0)
+        log_total = jnp.where(total > 0, peaks[kv, 0:1] * SCALE + jnp.log(safe), EMPTY)
+        log_column = jnp.broadcast_to(log_total, (8, rows)).T
+        out = (acc[kv] * (1.0 / safe)).T
         for g in range(GROUP):
             part = slice(g * new_rows, (g + 1) * new_rows)
-            total = jnp.sum(totals[part, :], axis=1, keepdims=True)
-            safe = jnp.where(total > 0, total, 1.0)
-            log_total = jnp.where(
-                total > 0, peaks[part, 0:1] * math.log(2.0) + jnp.log(safe), EMPTY
-            )
-            put(kv * GROUP + g, acc[part, :] * (1.0 / safe), log_total)
-
-
-def load_heads(query_ref, query_rows, kv):
+            put(kv * GROUP + g, out[part], log_column[part, 0:1])
+
+
+def load_heads(query_ref, query_rows, columns):
     new_rows = query_ref.shape[0]
-    for g in range(GROUP):
-        head = kv * GROUP + g
-        query_rows[g * new_rows : (g + 1) * new_rows, :] = query_ref[
-            :, head * HD : (head + 1) * HD
-        ]
+    for kv in range(columns.shape[0]):
+        for g in range(GROUP):
+            head = kv * GROUP + g
+            query_rows[g * new_rows : (g + 1) * new_rows, :] = query_ref[
+                :, head * HD : (head + 1) * HD
+            ]
+        columns[kv] = query_rows[...].T
 
 
 def add_lane(tile, heads, head, column):
@@ -196,8 +158,9 @@
     new_key_buf,
     new_value_buf,
     query_rows,
+    columns,
     scores,
-    new_scores,
+    weights,
     peaks,
     totals,
     acc,
@@ -219,16 +182,17 @@
         out_ref[:, head * HD : (head + 1) * HD] = out
         log_ref[...] = add_lane(log_ref[...], heads, head, log_total)
 
+    load_heads(query_ref, query_rows, columns)
     attend(
-        functools.partial(load_heads, query_ref, query_rows),
         key_buf,
         value_buf,
         count,
         ready,
-        (new_key_buf, new_value_buf, new_scores),
+        (new_key_buf, new_value_buf),
         new_rows,
-        query_rows,
+        columns,
         scores,
+        weights,
         peaks,
         totals,
         acc,
@@ -245,7 +209,9 @@
         key_buf,
         value_buf,
         query_rows,
+        columns,
         scores,
+        weights,
         peaks,
         totals,
         acc,
@@ -270,24 +236,23 @@
         heads = width // HD
         log_tile[...] = jnp.zeros(log_tile.shape, jnp.float32)
 
-        def load(kv):
-            for query_ref, hit in zip(query_refs, there):
-                pl.when(hit)(functools.partial(load_heads, query_ref, query_rows, kv))
+        for query_ref, hit in zip(query_refs, there):
+            pl.when(hit)(functools.partial(load_heads, query_ref, query_rows, columns))
 
         def put(head, out, log_total):
             out_ref[:, head * HD : (head + 1) * HD] = out.astype(jnp.bfloat16)
             log_tile[...] = add_lane(log_tile[...], heads, head, log_total)
 
         attend(
-            load,
             key_buf,
             value_buf,
             count,
             ready,
             None,
             new_rows,
-            query_rows,
+            columns,
             scores,
+            weights,
             peaks,
             totals,
             acc,
@@ -349,7 +314,6 @@
     kv_width = new_keys.shape[2]
     block_len = store_keys.shape[1]
     rows = GROUP * new_rows
-    padded_rows = -(-new_rows // (2 * HD)) * 2 * HD
     meta = jnp.concatenate(
         [my_index.reshape(1), prefix_blocks, hit_store[:, 0], hit_slot.reshape(-1)]
     )
@@ -357,13 +321,20 @@
     hbm_spec = pl.BlockSpec(memory_space=pltpu.HBM)
     vmem_spec = pl.BlockSpec(memory_space=pltpu.VMEM)
     params = pltpu.CompilerParams(vmem_limit_bytes=VMEM_LIMIT)
-    cost = pl.CostEstimate(flops=rows, bytes_accessed=rows, transcendentals=0)
+    cost = pl.CostEstimate(
+        flops=8 * rows * block_len * kv_width * capacity, bytes_accessed=rows, transcendentals=0
+    )
     buffers = [pltpu.VMEM((capacity, block_len, kv_width), jnp.bfloat16)] * 2
+    kv_local = kv_width // HD
     work = [
         pltpu.VMEM((rows, HD), jnp.bfloat16),
-        pltpu.VMEM((capacity, rows, block_len), jnp.float32),
+        pltpu.VMEM((kv_local, HD, rows), jnp.bfloat16),
+        pltpu.VMEM((kv_local, block_len, rows), jnp.float32),
+        pltpu.VMEM((kv_local, block_len, rows), jnp.bfloat16),
+        pltpu.VMEM((kv_local, 8, rows), jnp.float32),
+        pltpu.VMEM((kv_local, 8, rows), jnp.float32),
+        pltpu.VMEM((kv_local, HD, rows), jnp.float32),
     ]
-    state = [pltpu.VMEM((rows, HD), jnp.float32)] * 3
     sems = pltpu.SemaphoreType.DMA((2, capacity))
 
     def own_part(query):
@@ -373,10 +344,8 @@
             out_specs=[vmem_spec] * 2,
             scratch_shapes=[
                 *buffers,
-                *[pltpu.VMEM((padded_rows, kv_width), jnp.bfloat16)] * 2,
+                *[pltpu.VMEM((block_len, kv_width), jnp.bfloat16)] * 2,
                 *work,
-                pltpu.VMEM((rows, padded_rows), jnp.float32),
-                *state,
                 sems,
             ],
             out_shape=[
@@ -396,7 +365,6 @@
             scratch_shapes=[
                 *buffers,
                 *work,
-                *state,
                 pltpu.VMEM((new_rows, HD), jnp.float32),
                 sems,
             ],
@@ -424,11 +392,14 @@
         sources = []
         parts = []
         right, left = query, query
-        done = (own_out, own_log)
+        done = [own_out, own_log]
         for step in range(1, pool_size):
             right = forward(right, 1, step - 1)
             left = forward(left, -1, 1 - step)
-            right, left, *done = lax.optimization_barrier((right, left, *done))
+            settled = len(parts) - 1 if step > 2 else 0
+            right, left, parts[:settled], done = lax.optimization_barrier(
+                (right, left, parts[:settled], done)
+            )
             if step == 1:
                 own_out, own_log = done
             done = []

time: 173 us -> 144 us (0.83)
  the two profiles are of different devices: /device:TPU:4 before, /device:TPU:0 now
where the time goes in v2:
time: 144 us
  starting transfers between devices  59.9 us (42%)
  Pallas kernels  53.8 us (37%)
  local copies, waits for them, and re-layouts  13 us (9%)
  between operations  11.3 us (8%)
  other arithmetic  4.48 us (3%)
  waiting for transfers between devices  1.76 us (1%)
    ppermute x4, starting transfers between devices, shards(): parts.append(lax.ppermute(packed, 'pool', pairs))  37.7 us
    pallas_call x4, Pallas kernels, other_part(): pl.pallas_call(functools.partial(other_kernel, pool_size, offsets), in_sp...  36 us
    pallas_call x1, Pallas kernels, own_part(): pl.pallas_call(functools.partial(own_kernel, pool_size), in_specs=[smem_s...  13.7 us
    all_to_all x1, starting transfers between devices, shards(): lax.all_to_all(aimed, 'pool', split_axis=0, concat_axis=0, tiled=True)  12 us
    ppermute x6, starting transfers between devices, forward(): return lax.ppermute(array, 'pool', pairs)  10.3 us
    unnamed x24, local copies, waits for them, and re-layouts  8.94 us
    pallas_call x1, Pallas kernels, shards(): pl.pallas_call(functools.partial(combine_kernel, tuple(sources), pool_siz...  4.05 us
  transfers between devices with their start and end apart: 11, of which 1 were waited for; matrix products, arithmetic and copies ran while one was open for 5% of the time, Pallas kernels for 37%

profile of v2, /device:TPU:0, one launch (start us, length us, event | category | flops | bytes accessed | tf_op | source)
XLA Modules:
  0.0 144.2 jit_solution(8155029987933428324)
XLA Ops:
  0.6 5.0 %collective-permute-start = (bf16[160,2048]{1,0:T(8,128)(2,1)}, bf16[160,2048]{1,0:T(8,128)(2,1)S(1)}, u32[]{:S(2)}, u32[]{:S(2)}) collective-permute-start(bf16[160,2048]{1,0:T(8,128)(2,1)} %bitcast.28), channel_id=1, source_target_pairs={{0,4},{4,8},{8,12},{1,5},{5,9},{9,13},{2,6},{6,10},{10,14},{3,7},{... | collective-permute-start | bytes 1966088 | tf_op jit(solution)/shard_map/ppermute | solution.py:386
  5.6 1.3 collective-permute-start.1
  6.9 0.8 slice_reduce_fusion
  7.7 0.8 reshape.89
  8.5 1.2 dynamic_slice.3
  9.7 0.7 pad_add_fusion.meta_ref
  10.4 0.9 copy-done
  11.3 0.9 copy-done.2
  12.2 1.1 copy-done.6
  13.3 13.7 %own_part.1 = (f32[160,2048]{1,0:T(8,128)S(1)}, f32[160,128]{1,0:T(8,128)S(1)}) custom-call(s32[137]{0:T(256)S(1)} %pad_add_fusion.meta_ref, bf16[160,2048]{1,0:T(8,128)(2,1)S(1)} %bitcast.30, bf16[160,256]{1,0:T(8,128)(2,1)S(1)} %bitcast.24, bf16[160,256]{1,0:T(8,128)(2,1)S(1)} %bitcast.26, bf16[32,256,256]{2,1,0:T(8,128)(2,1)} %refs_2_.7, ...), custom_call_target="tpu_custom_call" | custom-call | flops 5368709120 | bytes 1280 | tf_op jit(solution)/shard_map/own_part/pallas_call | solution.py:341
  27.0 0.7 collective-permute-start.2
  27.8 1.3 collective-permute-start.3
  29.1 0.7 other_part.4
  29.8 1.4 collective-permute-start.6
  31.2 12.9 %other_part.5 = bf16[160,2176]{1,0:T(8,128)(2,1)S(1)} custom-call(s32[137]{0:T(256)S(1)} %pad_add_fusion.meta_ref, bf16[160,2048]{1,0:T(8,128)(2,1)} %collective-permute-done.1.refs_0_, bf16[32,256,256]{2,1,0:T(8,128)(2,1)S(1)} %copy-done.4, bf16[32,256,256]{2,1,0:T(8,128)(2,1)} %refs_3_.3), custom_call_target="tpu_custom_call" | custom-call | flops 5368709120 | bytes 1280 | tf_op jit(solution)/shard_map/other_part/pallas_call | solution.py:361
  44.1 23.3 %collective-permute-start.7 = (bf16[160,2176]{1,0:T(8,128)(2,1)S(1)}, bf16[160,2176]{1,0:T(8,128)(2,1)S(1)}, u32[]{:S(2)}, u32[]{:S(2)}) collective-permute-start(bf16[160,2176]{1,0:T(8,128)(2,1)S(1)} %other_part.5), channel_id=1, source_target_pairs={{0,4},{4,8},{8,12},{1,5},{5,9},{9,13},{2,6},{6,10},{10,14},{3,7},{... | collective-permute-start | bytes 2088968 | tf_op jit(solution)/shard_map/ppermute | solution.py:414
  67.4 0.7 collective-permute-start.4
  68.1 1.3 collective-permute-start.5
  70.1 14.9 %other_part.6 = bf16[160,2176]{1,0:T(8,128)(2,1)} custom-call(s32[137]{0:T(256)S(1)} %pad_add_fusion.meta_ref, bf16[160,2048]{1,0:T(8,128)(2,1)S(1)} %collective-permute-done.2.refs_0_, bf16[160,2048]{1,0:T(8,128)(2,1)S(1)} %collective-permute-done.3.refs_1_, bf16[32,256,256]{2,1,0:T(8,128)(2,1)S(1)} %copy-done.4, bf16[32,256,256]{2,1,0:T(8,128)(2,1)} %refs_3_.3), custom_call_target="tpu_custom_call" | custom-call | flops 5368709120 | bytes 1280 | tf_op jit(solution)/shard_map/other_part/pallas_call | solution.py:361
  85.1 0.8 copy-done.7
  86.0 0.9 copy-done.9
  86.8 0.9 broadcast_select_fusion
  87.8 12.0 %all-to-all-start = ((bf16[4,160,512]{2,1,0:T(8,128)(2,1)}), bf16[4,160,512]{2,1,0:T(8,128)(2,1)}, u32[]{:S(2)}, u32[]{:S(2)}) async-start(bf16[4,160,512]{2,1,0:T(8,128)(2,1)} %broadcast_select_fusion), calls=%async_computation | async-start | bytes 1310720 | tf_op jit(solution)/shard_map/all_to_all | solution.py:420
  99.7 2.2 %copy-done.5 = bf16[32,256,256]{2,1,0:T(8,128)(2,1)S(1)} copy-done((bf16[32,256,256]{2,1,0:T(8,128)(2,1)S(1)}, bf16[32,256,256]{2,1,0:T(8,128)(2,1)}, u32[]{:S(2)}) %copy-start.5) | copy-done | bytes 4194328
  101.9 1.1 copy-done.8
  103.0 1.1 copy-done.10
  104.1 7.5 %other_part.7 = bf16[160,2176]{1,0:T(8,128)(2,1)} custom-call(s32[137]{0:T(256)S(1)} %pad_add_fusion.meta_ref, bf16[160,2048]{1,0:T(8,128)(2,1)S(1)} %copy-done.8, bf16[160,2048]{1,0:T(8,128)(2,1)S(1)} %copy-done.10, bf16[32,256,256]{2,1,0:T(8,128)(2,1)S(1)} %copy-done.5, bf16[32,256,256]{2,1,0:T(8,128)(2,1)} %refs_3_.3), custom_call_target="tpu_custom_call" | custom-call | flops 5368709120 | bytes 1280 | tf_op jit(solution)/shard_map/other_part/pallas_call | solution.py:361
  111.6 12.9 %collective-permute-start.9 = (bf16[160,2176]{1,0:T(8,128)(2,1)}, bf16[160,2176]{1,0:T(8,128)(2,1)}, u32[]{:S(2)}, u32[]{:S(2)}) collective-permute-start(bf16[160,2176]{1,0:T(8,128)(2,1)} %other_part.7), channel_id=1, source_target_pairs={{12,0},{0,12},{13,1},{1,13},{14,2},{2,14},{15,3},{3,15},{28,16},{1... | collective-permute-start | bytes 2088968 | tf_op jit(solution)/shard_map/ppermute | solution.py:414
  136.5 1.7 %collective-permute-done.9.refs_3_ = bf16[160,2176]{1,0:T(8,128)(2,1)} collective-permute-done((bf16[160,2176]{1,0:T(8,128)(2,1)}, bf16[160,2176]{1,0:T(8,128)(2,1)}, u32[]{:S(2)}, u32[]{:S(2)}) %collective-permute-start.9) | collective-permute-done | bytes 696352 | tf_op jit(solution)/shard_map/ppermute | solution.py:414
  138.2 4.1 %combine.1 = bf16[160,2048]{1,0:T(8,128)(2,1)} custom-call(s32[137]{0:T(256)S(1)} %pad_add_fusion.meta_ref, f32[160,2048]{1,0:T(8,128)S(1)} %get-tuple-element.18.own_ref, f32[160,128]{1,0:T(8,128)S(1)} %get-tuple-element.19.log_ref, bf16[160,2176]{1,0:T(8,128)(2,1)S(1)} %collective-permute-done.6.refs_0_, ...), custom_call_target="tpu_custom_call" | custom-call | tf_op jit(solution)/shard_map/combine/pallas_call | solution.py:433
  142.3 1.2 select_select_fusion
  143.5 0.7 pad_maximum_fusion
  (34 shorter events, 2.3 us)
Async XLA Ops:
  0.6 26.4 %collective-permute-start = (bf16[160,2048]{1,0:T(8,128)(2,1)}, bf16[160,2048]{1,0:T(8,128)(2,1)S(1)}, u32[]{:S(2)}, u32[]{:S(2)}) collective-permute-start(bf16[160,2048]{1,0:T(8,128)(2,1)} %bitcast.28), channel_id=1, source_target_pairs={{0,4},{4,8},{8,12},{1,5},{5,9},{9,13},{2,6},{6,10},{10,14},{3,7},{... | collective-permute-start | bytes 1966088 | tf_op jit(solution)/shard_map/ppermute | solution.py:386
  5.6 21.4 %collective-permute-start.1 = (bf16[160,2048]{1,0:T(8,128)(2,1)}, bf16[160,2048]{1,0:T(8,128)(2,1)}, u32[]{:S(2)}, u32[]{:S(2)}) collective-permute-start(bf16[160,2048]{1,0:T(8,128)(2,1)} %bitcast.29), channel_id=1, source_target_pairs={{4,0},{8,4},{12,8},{5,1},{9,5},{13,9},{6,2},{10,6},{14,10},{7,3},{... | collective-permute-start | bytes 1966088 | tf_op jit(solution)/shard_map/ppermute | solution.py:386
  10.4 0.9 copy-start
  11.3 0.9 copy-start.2
  12.2 1.1 copy-start.6
  13.3 15.7 %copy-start.4 = (bf16[32,256,256]{2,1,0:T(8,128)(2,1)S(1)}, bf16[32,256,256]{2,1,0:T(8,128)(2,1)}, u32[]{:S(2)}) copy-start(bf16[32,256,256]{2,1,0:T(8,128)(2,1)} %refs_2_.7) | copy-start | bytes 12582916
  27.0 40.3 %collective-permute-start.2 = (bf16[160,2048]{1,0:T(8,128)(2,1)S(1)}, bf16[160,2048]{1,0:T(8,128)(2,1)S(1)}, u32[]{:S(2)}, u32[]{:S(2)}) collective-permute-start(bf16[160,2048]{1,0:T(8,128)(2,1)S(1)} %collective-permute-done.refs_0_), channel_id=1, source_target_pairs={{4,8},{8,12},{5,9},{9,13},{6,10},{10,14},{7,11},{11,15},{20,24},{2... | collective-permute-start | bytes 1966088 | tf_op jit(solution)/shard_map/ppermute | solution.py:386
  27.8 39.6 %collective-permute-start.3 = (bf16[160,2048]{1,0:T(8,128)(2,1)}, bf16[160,2048]{1,0:T(8,128)(2,1)S(1)}, u32[]{:S(2)}, u32[]{:S(2)}) collective-permute-start(bf16[160,2048]{1,0:T(8,128)(2,1)} %collective-permute-done.1.refs_0_), channel_id=1, source_target_pairs={{4,0},{8,4},{5,1},{9,5},{6,2},{10,6},{7,3},{11,7},{20,16},{24,20},... | collective-permute-start | bytes 1966088 | tf_op jit(solution)/shard_map/ppermute | solution.py:386
  29.8 40.3 %copy-start.1 = (bf16[1,160,256]{2,1,0:T(8,128)(2,1)S(1)}, bf16[1,160,256]{2,1,0:T(8,128)(2,1)}, u32[]{:S(2)}) copy-start(bf16[1,160,256]{2,1,0:T(8,128)(2,1)} %param.10) | copy-start | bytes 245764
  29.8 40.3 %copy-start.3 = (bf16[1,160,256]{2,1,0:T(8,128)(2,1)S(1)}, bf16[1,160,256]{2,1,0:T(8,128)(2,1)}, u32[]{:S(2)}) copy-start(bf16[1,160,256]{2,1,0:T(8,128)(2,1)} %param.11) | copy-start | bytes 245764
  29.8 55.3 %collective-permute-start.6 = (bf16[160,2176]{1,0:T(8,128)(2,1)S(1)}, bf16[160,2176]{1,0:T(8,128)(2,1)S(1)}, u32[]{:S(2)}, u32[]{:S(2)}) collective-permute-start(bf16[160,2176]{1,0:T(8,128)(2,1)S(1)} %other_part.4), channel_id=1, source_target_pairs={{4,0},{8,4},{12,8},{5,1},{9,5},{13,9},{6,2},{10,6},{14,10},{7,3},{... | collective-permute-start | bytes 2088968 | tf_op jit(solution)/shard_map/ppermute | solution.py:414
  44.1 41.0 %collective-permute-start.7 = (bf16[160,2176]{1,0:T(8,128)(2,1)S(1)}, bf16[160,2176]{1,0:T(8,128)(2,1)S(1)}, u32[]{:S(2)}, u32[]{:S(2)}) collective-permute-start(bf16[160,2176]{1,0:T(8,128)(2,1)S(1)} %other_part.5), channel_id=1, source_target_pairs={{0,4},{4,8},{8,12},{1,5},{5,9},{9,13},{2,6},{6,10},{10,14},{3,7},{... | collective-permute-start | bytes 2088968 | tf_op jit(solution)/shard_map/ppermute | solution.py:414
  67.4 17.7 %collective-permute-start.4 = (bf16[160,2048]{1,0:T(8,128)(2,1)S(1)}, bf16[160,2048]{1,0:T(8,128)(2,1)S(1)}, u32[]{:S(2)}, u32[]{:S(2)}) collective-permute-start(bf16[160,2048]{1,0:T(8,128)(2,1)S(1)} %collective-permute-done.2.refs_0_), channel_id=1, source_target_pairs={{8,12},{9,13},{10,14},{11,15},{24,28},{25,29},{26,30},{27,31}} | collective-permute-start | bytes 1966088 | tf_op jit(solution)/shard_map/ppermute | solution.py:386
  68.1 17.9 %collective-permute-start.5 = (bf16[160,2048]{1,0:T(8,128)(2,1)S(1)}, bf16[160,2048]{1,0:T(8,128)(2,1)S(1)}, u32[]{:S(2)}, u32[]{:S(2)}) collective-permute-start(bf16[160,2048]{1,0:T(8,128)(2,1)S(1)} %collective-permute-done.3.refs_1_), channel_id=1, source_target_pairs={{4,0},{5,1},{6,2},{7,3},{20,16},{21,17},{22,18},{23,19}} | collective-permute-start | bytes 1966088 | tf_op jit(solution)/shard_map/ppermute | solution.py:386
  85.0 51.5 %collective-permute-start.8 = (bf16[160,2176]{1,0:T(8,128)(2,1)}, bf16[160,2176]{1,0:T(8,128)(2,1)S(1)}, u32[]{:S(2)}, u32[]{:S(2)}) collective-permute-start(bf16[160,2176]{1,0:T(8,128)(2,1)} %other_part.6), channel_id=1, source_target_pairs={{8,0},{12,4},{0,8},{4,12},{9,1},{13,5},{1,9},{5,13},{10,2},{14,6},... | collective-permute-start | bytes 2088968 | tf_op jit(solution)/shard_map/ppermute | solution.py:414
  85.1 0.8 copy-start.7
  86.0 0.9 copy-start.9
  87.8 54.5 %all-to-all-start = ((bf16[4,160,512]{2,1,0:T(8,128)(2,1)}), bf16[4,160,512]{2,1,0:T(8,128)(2,1)}, u32[]{:S(2)}, u32[]{:S(2)}) async-start(bf16[4,160,512]{2,1,0:T(8,128)(2,1)} %broadcast_select_fusion), calls=%async_computation | async-start | bytes 1310720 | tf_op jit(solution)/shard_map/all_to_all | solution.py:420
  99.7 2.2 %copy-start.5 = (bf16[32,256,256]{2,1,0:T(8,128)(2,1)S(1)}, bf16[32,256,256]{2,1,0:T(8,128)(2,1)}, u32[]{:S(2)}) copy-start(bf16[32,256,256]{2,1,0:T(8,128)(2,1)} %refs_2_.7) | copy-start | bytes 12582916
  101.9 1.1 copy-start.8
  103.0 1.1 copy-start.10
  104.1 20.5 %copy-start.11 = (s32[4]{0:T(128)S(1)}, s32[4]{0:T(128)}, u32[]{:S(2)}) copy-start(s32[4]{0:T(128)} %param.17) | copy-start | bytes 52
  111.6 26.6 %collective-permute-start.9 = (bf16[160,2176]{1,0:T(8,128)(2,1)}, bf16[160,2176]{1,0:T(8,128)(2,1)}, u32[]{:S(2)}, u32[]{:S(2)}) collective-permute-start(bf16[160,2176]{1,0:T(8,128)(2,1)} %other_part.7), channel_id=1, source_target_pairs={{12,0},{0,12},{13,1},{1,13},{14,2},{2,14},{15,3},{3,15},{28,16},{1... | collective-permute-start | bytes 2088968 | tf_op jit(solution)/shard_map/ppermute | solution.py:414

commit v3 on v2

v3 whole, which is shorter than its diff:
```python
import functools
import math

import jax
import jax.numpy as jnp
from jax import lax
from jax.experimental import pallas as pl
from jax.experimental.pallas import tpu as pltpu
from jax.sharding import PartitionSpec as P

HEADS = 64
KVH = 8
HD = 128
MAXBLK = 32
CAPP = 2
GROUP = HEADS // KVH
EMPTY = -1e30
LINE = 8
TILE = 256
ONES = 16
SCALE = 1.0 / math.sqrt(HD)
EXP2_SCALE = SCALE * math.log2(math.e)
VMEM_LIMIT = 61 * 1024 * 1024


def fetch(pool_size, tables, request, stores, buffers, sems):
    prefix_ref, store_ref, slot_ref = tables
    me = lax.axis_index("pool")
    first = lax.rem(me - store_ref[request, 0] + pool_size, pool_size)
    count = lax.max(lax.div(prefix_ref[request] - first + pool_size - 1, pool_size), 0)

    def copies(entry):
        slot = slot_ref[request, first + entry * pool_size]
        return [
            pltpu.make_async_copy(stores[i].at[slot], buffers[i].at[entry], sems.at[i, entry])
            for i in range(2)
        ]

    def start(entry, carry):
        for copy in copies(entry):
            copy.start()
        return carry

    lax.fori_loop(0, count, start, 0)

    def ready(entry):
        for copy in copies(entry):
            copy.wait()

    return count, ready


def attend(key_ref, value_ref, count, ready, fresh, new_rows, columns, scores, weights, peaks, factors, turned, acc, put):
    kv_local, _, rows = columns.shape

    def visit(kv, keys, values, seen):
        block = lax.dot_general(
            keys, columns[kv], (((1,), (0,)), ((), ())), preferred_element_type=jnp.float32
        )
        if seen is not None:
            block = jnp.where(seen, block, EMPTY)
        scores[kv] = block
        turned[kv, :HD, :] = values.T
        for i in range(0, rows, TILE):
            part = slice(i, i + TILE)
            before = peaks[kv, :, part]
            block = scores[kv, :, part]
            peak = jnp.maximum(before, jnp.max(block, axis=0, keepdims=True))
            factors[kv, :, part] = jnp.exp2((before - peak) * EXP2_SCALE)
            peaks[kv, :, part] = peak
            weight = jnp.exp2(block * EXP2_SCALE - peak[0:1] * EXP2_SCALE)
            weights[kv, :, part] = weight.astype(jnp.bfloat16)
        added = lax.dot_general(
            turned[kv], weights[kv], (((1,), (0,)), ((), ())), preferred_element_type=jnp.float32
        )
        acc[kv] = acc[kv] * factors[kv, 0:1, :] + added

    peaks[...] = jnp.full(peaks.shape, EMPTY, jnp.float32)
    acc[...] = jnp.zeros(acc.shape, jnp.float32)
    turned[:, HD:, :] = jnp.ones((kv_local, ONES, turned.shape[2]), jnp.bfloat16)
    if fresh is not None:
        new_key_ref, new_value_ref = fresh
        shape = (new_key_ref.shape[0], rows)
        seen = lax.broadcasted_iota(jnp.int32, shape, 0) <= lax.rem(
            lax.broadcasted_iota(jnp.int32, (1, rows), 1), new_rows
        )
        for kv in range(kv_local):
            lanes = slice(kv * HD, (kv + 1) * HD)
            visit(kv, new_key_ref[:, lanes], new_value_ref[:, lanes], seen)

    def visit_block(entry, carry):
        ready(entry)
        for kv in range(kv_local):
            lanes = slice(kv * HD, (kv + 1) * HD)
            visit(kv, key_ref[entry, :, lanes], value_ref[entry, :, lanes], None)
        return carry

    lax.fori_loop(0, count, visit_block, 0)
    for kv in range(kv_local):
        total = acc[kv, HD : HD + 1, :]
        safe = jnp.where(total > 0, total, 1.0)
        log_total = jnp.where(total > 0, peaks[kv, 0:1] * SCALE + jnp.log(safe), EMPTY)
        log_column = jnp.broadcast_to(log_total, (8, rows)).T
        out = (acc[kv, :HD, :] * (1.0 / safe)).T
        for g in range(GROUP):
            part = slice(g * new_rows, (g + 1) * new_rows)
            put(kv * GROUP + g, out[part], log_column[part, 0:1])


def load_heads(query_ref, query_rows, columns):
    new_rows = query_ref.shape[0]
    for kv in range(columns.shape[0]):
        for g in range(GROUP):
            head = kv * GROUP + g
            query_rows[g * new_rows : (g + 1) * new_rows, :] = query_ref[
                :, head * HD : (head + 1) * HD
            ]
        columns[kv] = query_rows[...].T


def add_lane(tile, heads, head, column):
    lane = lax.broadcasted_iota(jnp.int32, tile.shape, 1)
    hit = (lax.rem(lane, heads) == head) & (lane < 3 * heads)
    return jnp.where(hit, column, tile)


def split_lanes(tile, heads):
    lane = lax.broadcasted_iota(jnp.int32, tile.shape, 1)
    high = tile.astype(jnp.bfloat16).astype(jnp.float32)
    middle = (tile - high).astype(jnp.bfloat16).astype(jnp.float32)
    low = tile - high - middle
    return jnp.where(lane < heads, high, jnp.where(lane < 2 * heads, middle, low)).astype(
        jnp.bfloat16
    )


def own_kernel(
    pool_size,
    prefix_ref,
    store_ref,
    slot_ref,
    payload_ref,
    store_keys,
    store_values,
    out_ref,
    log_ref,
    key_buf,
    value_buf,
    new_key_buf,
    new_value_buf,
    query_rows,
    columns,
    *state,
):
    *work, sems = state
    count, ready = fetch(
        pool_size,
        (prefix_ref, store_ref, slot_ref),
        lax.axis_index("pool"),
        (store_keys, store_values),
        (key_buf, value_buf),
        sems,
    )
    new_rows, width = out_ref.shape
    kv_width = new_key_buf.shape[1]
    heads = width // HD
    for i, buffer in enumerate((new_key_buf, new_value_buf)):
        buffer[:new_rows, :] = payload_ref[:, width + i * kv_width : width + (i + 1) * kv_width]
        buffer[new_rows:, :] = jnp.zeros((buffer.shape[0] - new_rows, kv_width), jnp.bfloat16)
    log_ref[...] = jnp.zeros(log_ref.shape, jnp.float32)

    def put(head, out, log_total):
        out_ref[:, head * HD : (head + 1) * HD] = out
        log_ref[...] = add_lane(log_ref[...], heads, head, log_total)

    load_heads(payload_ref, query_rows, columns)
    attend(
        key_buf,
        value_buf,
        count,
        ready,
        (new_key_buf, new_value_buf),
        new_rows,
        columns,
        *work,
        put,
    )


def other_kernel(pool_size, offsets, *refs):
    if offsets[0] is None:
        wanted = [refs[0][0]]
        refs = refs[1:]
    else:
        wanted = [lax.axis_index("pool") + offset for offset in offsets]
    tables, refs = refs[:3], refs[3:]
    payload_refs = refs[: len(offsets)]
    store_keys, store_values, out_ref, key_buf, value_buf, query_rows, columns, *state = refs[
        len(offsets) :
    ]
    *work, log_tile, sems = state
    there = [(x >= 0) & (x < pool_size) for x in wanted]
    request = wanted[0]
    for other, hit in zip(wanted[1:], there[1:]):
        request = jnp.where(hit, other, request)

    @pl.when(functools.reduce(jnp.logical_or, there))
    def _():
        count, ready = fetch(
            pool_size, tables, request, (store_keys, store_values), (key_buf, value_buf), sems
        )
        new_rows = out_ref.shape[0]
        width = out_ref.shape[1] - HD
        heads = width // HD
        log_tile[...] = jnp.zeros(log_tile.shape, jnp.float32)
        for payload_ref, hit in zip(payload_refs, there):
            pl.when(hit)(functools.partial(load_heads, payload_ref, query_rows, columns))

        def put(head, out, log_total):
            out_ref[:, head * HD : (head + 1) * HD] = out.astype(jnp.bfloat16)
            log_tile[...] = add_lane(log_tile[...], heads, head, log_total)

        attend(key_buf, value_buf, count, ready, None, new_rows, columns, *work, put)
        out_ref[:, width:] = split_lanes(log_tile[...], heads)


def combine_kernel(sources, pool_size, own_ref, log_ref, *refs):
    out_ref = refs[-1]
    width = own_ref.shape[1]
    heads = width // HD
    logs = [log_ref[...]]
    me = lax.axis_index("pool")
    for (offsets, source), part in zip(sources, refs[:-1]):
        if offsets:
            wanted = [me + offset for offset in offsets]
            there = functools.reduce(
                jnp.logical_or, [(x >= 0) & (x < pool_size) for x in wanted]
            )
        else:
            there = me != source
        tile = part[:, width:].astype(jnp.float32)
        whole = (
            tile + pltpu.roll(tile, HD - heads, 1) + pltpu.roll(tile, HD - 2 * heads, 1)
        )
        logs.append(jnp.where(there, whole, EMPTY))
    peak = functools.reduce(jnp.maximum, logs)
    shares = [jnp.exp(x - peak) for x in logs]
    scale = 1.0 / functools.reduce(jnp.add, shares)
    shares = [x * scale for x in shares]
    for head in range(heads):
        lanes = slice(head * HD, (head + 1) * HD)
        mixed = own_ref[:, lanes] * shares[0][:, head : head + 1]
        for share, part in zip(shares[1:], refs[:-1]):
            mixed = mixed + part[:, lanes].astype(jnp.float32) * share[:, head : head + 1]
        out_ref[:, lanes] = mixed.astype(jnp.bfloat16)


def shards(
    queries,
    new_keys,
    new_values,
    store_keys,
    store_values,
    prefix_blocks,
    hit_store,
    hit_slot,
    decode_owner,
):
    pool_size = lax.axis_size("pool")
    my_index = lax.axis_index("pool").astype(jnp.int32)
    capacity = (MAXBLK + pool_size - 1) // pool_size
    new_rows = queries.shape[1]
    width = queries.shape[2]
    kv_width = new_keys.shape[2]
    block_len = store_keys.shape[1]
    rows = GROUP * new_rows
    tables = (prefix_blocks, hit_store, hit_slot)
    smem_spec = pl.BlockSpec(memory_space=pltpu.SMEM)
    hbm_spec = pl.BlockSpec(memory_space=pltpu.HBM)
    vmem_spec = pl.BlockSpec(memory_space=pltpu.VMEM)
    params = pltpu.CompilerParams(vmem_limit_bytes=VMEM_LIMIT)
    cost = pl.CostEstimate(
        flops=8 * rows * block_len * kv_width * capacity, bytes_accessed=rows, transcendentals=0
    )
    buffers = [pltpu.VMEM((capacity, block_len, kv_width), jnp.bfloat16)] * 2
    kv_local = kv_width // HD
    work = [
        pltpu.VMEM((rows, HD), jnp.bfloat16),
        pltpu.VMEM((kv_local, HD, rows), jnp.bfloat16),
        pltpu.VMEM((kv_local, block_len, rows), jnp.float32),
        pltpu.VMEM((kv_local, block_len, rows), jnp.bfloat16),
        pltpu.VMEM((kv_local, 8, rows), jnp.float32),
        pltpu.VMEM((kv_local, 8, rows), jnp.float32),
        pltpu.VMEM((kv_local, HD + ONES, block_len), jnp.bfloat16),
        pltpu.VMEM((kv_local, HD + ONES, rows), jnp.float32),
    ]
    sems = pltpu.SemaphoreType.DMA((2, capacity))

    def own_part(payload):
        return pl.pallas_call(
            functools.partial(own_kernel, pool_size),
            in_specs=[smem_spec] * 3 + [vmem_spec] + [hbm_spec] * 2,
            out_specs=[vmem_spec] * 2,
            scratch_shapes=[
                *buffers,
                *[pltpu.VMEM((block_len, kv_width), jnp.bfloat16)] * 2,
                *work,
                sems,
            ],
            out_shape=[
                jax.ShapeDtypeStruct((new_rows, width), jnp.float32),
                jax.ShapeDtypeStruct((new_rows, HD), jnp.float32),
            ],
            compiler_params=params,
            cost_estimate=cost,
            name="own_part",
        )(*tables, payload, store_keys, store_values)

    def other_part(offsets, held, *request):
        return pl.pallas_call(
            functools.partial(other_kernel, pool_size, offsets),
            in_specs=[smem_spec] * (3 + len(request)) + [vmem_spec] * len(held) + [hbm_spec] * 2,
            out_specs=vmem_spec,
            scratch_shapes=[
                *buffers,
                *work,
                pltpu.VMEM((new_rows, HD), jnp.float32),
                sems,
            ],
            out_shape=jax.ShapeDtypeStruct((new_rows, width + HD), jnp.bfloat16),
            compiler_params=params,
            cost_estimate=cost,
            name="other_part",
        )(*request, *tables, *held, store_keys, store_values)

    def inside(index):
        return 0 <= index < pool_size

    def forward(array, distance, first):
        pairs = [
            (i, i + distance)
            for i in range(pool_size)
            if inside(i + distance) and inside(i - first)
        ]
        return lax.ppermute(array, "pool", pairs)

    payload = jnp.concatenate([queries[0], new_keys[0], new_values[0]], axis=1)
    own_out, own_log = own_part(payload)
    mine = decode_owner == my_index
    if pool_size <= LINE:
        sources = []
        parts = []
        right, left = payload, payload
        moved = [(mine[my_index], my_index, payload)]
        done = [own_out, own_log]
        for step in range(1, pool_size):
            right = forward(right, 1, step - 1)
            left = forward(left, -1, 1 - step)
            settled = len(parts) - 1 if step > 2 else 0
            right, left, parts[:settled], done = lax.optimization_barrier(
                (right, left, parts[:settled], done)
            )
            if step == 1:
                own_out, own_log = done
            done = []
            for source, array in ((my_index - step, right), (my_index + step, left)):
                there = (source >= 0) & (source < pool_size)
                source = jnp.clip(source, 0, pool_size - 1)
                moved.append((there & mine[source], source, array))
            if 2 * step < pool_size:
                groups = [((-step,), (right,)), ((step,), (left,))]
            else:
                groups = [((-step, step), (right, left))]
            for offsets, held in groups:
                packed = other_part(offsets, held)
                done.append(packed)
                pairs = [(i, i + x) for x in offsets for i in range(pool_size) if inside(i + x)]
                parts.append(lax.ppermute(packed, "pool", pairs))
                sources.append((tuple(-x for x in offsets), None))
    else:
        gathered = lax.all_gather(payload, "pool", axis=0, tiled=False)
        packed = lax.map(
            lambda pair: other_part((None,), (pair[0],), pair[1].reshape(1)),
            (gathered, jnp.arange(pool_size, dtype=jnp.int32)),
        )
        parts = lax.all_to_all(packed, "pool", split_axis=0, concat_axis=0, tiled=True)
        sources = [(None, source) for source in range(pool_size)]
        moved = [(mine[source], source, gathered[source]) for source in range(pool_size)]

    attended = pl.pallas_call(
        functools.partial(combine_kernel, tuple(sources), pool_size),
        in_specs=[vmem_spec] * (2 + len(sources)),
        out_specs=vmem_spec,
        out_shape=jax.ShapeDtypeStruct((new_rows, width), jnp.bfloat16),
        compiler_params=params,
        name="combine",
    )(own_out, own_log, *parts)

    rank = jnp.cumsum(mine) - 1
    pushed = []
    for place in range(CAPP):
        total = jnp.zeros((new_rows, 2 * kv_width), jnp.bfloat16)
        for hit, source, array in moved:
            total = jnp.where(hit & (rank[source] == place), array[:, width:], total)
        pushed.append(total)
    pushed = jnp.stack(pushed)
    return (attended[None], pushed[:, :, :kv_width], pushed[:, :, kv_width:])


def solution(mesh):
    in_specs = (
        P(("groups", "pool"), None, ("tensor", "sub")),
        P(("groups", "pool"), None, ("tensor", "sub")),
        P(("groups", "pool"), None, ("tensor", "sub")),
        P(("groups", "pool"), None, ("tensor", "sub")),
        P(("groups", "pool"), None, ("tensor", "sub")),
        P("groups"),
        P("groups", None),
        P("groups", None),
        P("groups"),
    )
    out_specs = (
        P(("groups", "pool"), None, ("tensor", "sub")),
        P(("groups", "pool"), None, ("tensor", "sub")),
        P(("groups", "pool"), None, ("tensor", "sub")),
    )
    return jax.shard_map(shards, mesh=mesh, in_specs=in_specs, out_specs=out_specs, check_vma=False)
```

time: 144 us -> 139 us (0.965)
  the two profiles are of different devices: /device:TPU:0 before, /device:TPU:4 now
where the time goes in v3:
time: 139 us; the launch traced here: 140 us
  Pallas kernels  62.7 us (45%)
  starting transfers between devices  31.8 us (23%)
  waiting for transfers between devices  22.8 us (16%)
  between operations  14.7 us (11%)
  other arithmetic  5.09 us (4%)
  local copies, waits for them, and re-layouts  3.2 us (2%)
    pallas_call x4, Pallas kernels, other_part(): pl.pallas_call(functools.partial(other_kernel, pool_size, offsets), in_sp...  43.1 us
    ppermute x4, starting transfers between devices, shards(): parts.append(lax.ppermute(packed, 'pool', pairs))  21.3 us
    pallas_call x1, Pallas kernels, own_part(): pl.pallas_call(functools.partial(own_kernel, pool_size), in_specs=[smem_s...  14.5 us
    ppermute x6, waiting for transfers between devices, forward(): return lax.ppermute(array, 'pool', pairs)  11.6 us
    ppermute x4, waiting for transfers between devices, shards(): parts.append(lax.ppermute(packed, 'pool', pairs))  11.2 us
    ppermute x6, starting transfers between devices, forward(): return lax.ppermute(array, 'pool', pairs)  10.5 us
    pallas_call x1, Pallas kernels, shards(): pl.pallas_call(functools.partial(combine_kernel, tuple(sources), pool_siz...  5.03 us
    another operation x3, other arithmetic, shards(): pushed = jnp.stack(pushed)  3.67 us
  transfers between devices with their start and end apart: 10, of which 4 were waited for; matrix products, arithmetic and copies ran while one was open for 4% of the time, Pallas kernels for 41%

profile of v3, /device:TPU:4, one launch (start us, length us, event | category | flops | bytes accessed | tf_op | source)
XLA Modules:
  0.0 140.3 jit_solution(10685293223430728670)
XLA Ops:
  0.6 1.2 pad_maximum_fusion.payload_ref
  1.9 3.5 %collective-permute-start = (bf16[160,2560]{1,0:T(8,128)(2,1)S(1)}, bf16[160,2560]{1,0:T(8,128)(2,1)S(1)}, u32[]{:S(2)}, u32[]{:S(2)}) collective-permute-start(bf16[160,2560]{1,0:T(8,128)(2,1)S(1)} %pad_maximum_fusion.payload_ref), channel_id=1, source_target_pairs={{0,4},{4,8},{8,12},{1,5},{5,9},{9,13},{2,6},{6,10},{10,14},{3,7},{... | collective-permute-start | bytes 2457608 | tf_op jit(solution)/shard_map/ppermute | solution.py:345
  5.4 1.3 collective-permute-start.1
  6.7 14.5 %own_part.1 = (f32[160,2048]{1,0:T(8,128)}, f32[160,128]{1,0:T(8,128)}) custom-call(s32[4]{0:T(128)} %refs_0_.7, s32[4,32]{1,0:T(4,128)} %refs_1_.7, s32[4,32]{1,0:T(4,128)} %refs_2_.7, bf16[160,2560]{1,0:T(8,128)(2,1)} %copy-done, bf16[32,256,256]{2,1,0:T(8,128)(2,1)} %refs_5_.7, bf16[32,256,256]{2,1,0:T(8,128)(2,1)} %refs_6_.3), custom_call_target="tpu_custom_call" | custom-call | flops 5368709120 | bytes 1280 | tf_op jit(solution)/shard_map/own_part/pallas_call | solution.py:300
  21.2 1.6 %collective-permute-done.refs_3_ = bf16[160,2560]{1,0:T(8,128)(2,1)S(1)} collective-permute-done((bf16[160,2560]{1,0:T(8,128)(2,1)S(1)}, bf16[160,2560]{1,0:T(8,128)(2,1)S(1)}, u32[]{:S(2)}, u32[]{:S(2)}) %collective-permute-start) | collective-permute-done | bytes 819232 | tf_op jit(solution)/shard_map/ppermute | solution.py:345
  22.9 4.3 %collective-permute-done.1.refs_3_ = bf16[160,2560]{1,0:T(8,128)(2,1)} collective-permute-done((bf16[160,2560]{1,0:T(8,128)(2,1)S(1)}, bf16[160,2560]{1,0:T(8,128)(2,1)}, u32[]{:S(2)}, u32[]{:S(2)}) %collective-permute-start.1) | collective-permute-done | bytes 819232 | tf_op jit(solution)/shard_map/ppermute | solution.py:345
  27.1 1.6 %collective-permute-start.2 = (bf16[160,2560]{1,0:T(8,128)(2,1)S(1)}, bf16[160,2560]{1,0:T(8,128)(2,1)}, u32[]{:S(2)}, u32[]{:S(2)}) collective-permute-start(bf16[160,2560]{1,0:T(8,128)(2,1)S(1)} %collective-permute-done.refs_3_), channel_id=1, source_target_pairs={{4,8},{8,12},{5,9},{9,13},{6,10},{10,14},{7,11},{11,15},{20,24},{2... | collective-permute-start | bytes 2457608 | tf_op jit(solution)/shard_map/ppermute | solution.py:345
  28.7 1.3 collective-permute-start.3
  30.0 2.2 %other_part.4 = bf16[160,2176]{1,0:T(8,128)(2,1)} custom-call(s32[4]{0:T(128)} %refs_0_.7, s32[4,32]{1,0:T(4,128)} %refs_1_.7, s32[4,32]{1,0:T(4,128)} %refs_2_.7, bf16[160,2560]{1,0:T(8,128)(2,1)} %copy-done.7, bf16[32,256,256]{2,1,0:T(8,128)(2,1)} %refs_5_.7, bf16[32,256,256]{2,1,0:T(8,128)(2,1)} %refs_6_.3), custom_call_target="tpu_custom_call" | custom-call | flops 5368709120 | bytes 1280 | tf_op jit(solution)/shard_map/other_part/pallas_call | solution.py:320
  32.2 0.0 copy-start.8
  32.2 14.1 %other_part.5 = bf16[160,2176]{1,0:T(8,128)(2,1)} custom-call(s32[4]{0:T(128)} %refs_0_.7, s32[4,32]{1,0:T(4,128)} %refs_1_.7, s32[4,32]{1,0:T(4,128)} %refs_2_.7, bf16[160,2560]{1,0:T(8,128)(2,1)} %collective-permute-done.1.refs_3_, bf16[32,256,256]{2,1,0:T(8,128)(2,1)} %refs_5_.7, bf16[32,256,256]{2,1,0:T(8,128)(2,1)} %refs_6_.3), custom_call_target="tpu_custom_call" | custom-call | flops 5368709120 | bytes 1280 | tf_op jit(solution)/shard_map/other_part/pallas_call | solution.py:320
  46.3 5.7 %collective-permute-done.3.refs_4_ = bf16[160,2560]{1,0:T(8,128)(2,1)} collective-permute-done((bf16[160,2560]{1,0:T(8,128)(2,1)}, bf16[160,2560]{1,0:T(8,128)(2,1)}, u32[]{:S(2)}, u32[]{:S(2)}) %collective-permute-start.3) | collective-permute-done | bytes 819232 | tf_op jit(solution)/shard_map/ppermute | solution.py:345
  52.0 1.6 %collective-permute-start.4 = (bf16[160,2560]{1,0:T(8,128)(2,1)}, bf16[160,2560]{1,0:T(8,128)(2,1)}, u32[]{:S(2)}, u32[]{:S(2)}) collective-permute-start(bf16[160,2560]{1,0:T(8,128)(2,1)} %collective-permute-done.2.refs_3_), channel_id=1, source_target_pairs={{8,12},{9,13},{10,14},{11,15},{24,28},{25,29},{26,30},{27,31}} | collective-permute-start | bytes 2457608 | tf_op jit(solution)/shard_map/ppermute | solution.py:345
  53.6 1.3 collective-permute-start.5
  54.9 1.3 collective-permute-start.6
  56.2 14.6 %collective-permute-start.7 = (bf16[160,2176]{1,0:T(8,128)(2,1)}, bf16[160,2176]{1,0:T(8,128)(2,1)S(1)}, u32[]{:S(2)}, u32[]{:S(2)}) collective-permute-start(bf16[160,2176]{1,0:T(8,128)(2,1)} %other_part.5), channel_id=1, source_target_pairs={{0,4},{4,8},{8,12},{1,5},{5,9},{9,13},{2,6},{6,10},{10,14},{3,7},{... | collective-permute-start | bytes 2088968 | tf_op jit(solution)/shard_map/ppermute | solution.py:378
  70.8 0.2 reduce-window.9
  71.0 14.3 %other_part.6 = bf16[160,2176]{1,0:T(8,128)(2,1)} custom-call(s32[4]{0:T(128)} %refs_0_.7, s32[4,32]{1,0:T(4,128)} %refs_1_.7, s32[4,32]{1,0:T(4,128)} %refs_2_.7, bf16[160,2560]{1,0:T(8,128)(2,1)} %collective-permute-done.2.refs_3_, bf16[160,2560]{1,0:T(8,128)(2,1)} %collective-permute-done.3.refs_4_, bf16[32,256,256]{2,1,0:T(8,128)(2,1)} %refs_5_.7, ...), custom_call_target="tpu_custom_call" | custom-call | flops 5368709120 | bytes 1280 | tf_op jit(solution)/shard_map/other_part/pallas_call | solution.py:320
  85.3 0.0 copy-start.1
  85.3 0.0 copy-start.2
  85.3 1.5 %collective-permute-start.8 = (bf16[160,2176]{1,0:T(8,128)(2,1)}, bf16[160,2176]{1,0:T(8,128)(2,1)S(1)}, u32[]{:S(2)}, u32[]{:S(2)}) collective-permute-start(bf16[160,2176]{1,0:T(8,128)(2,1)} %other_part.6), channel_id=1, source_target_pairs={{8,0},{12,4},{0,8},{4,12},{9,1},{13,5},{1,9},{5,13},{10,2},{14,6},... | collective-permute-start | bytes 2088968 | tf_op jit(solution)/shard_map/ppermute | solution.py:378
  86.8 11.2 %collective-permute-done.6.refs_0_ = bf16[160,2176]{1,0:T(8,128)(2,1)S(1)} collective-permute-done((bf16[160,2176]{1,0:T(8,128)(2,1)S(1)}, bf16[160,2176]{1,0:T(8,128)(2,1)S(1)}, u32[]{:S(2)}, u32[]{:S(2)}) %collective-permute-start.6) | collective-permute-done | bytes 696352 | tf_op jit(solution)/shard_map/ppermute | solution.py:378
  98.0 12.6 %other_part.7 = bf16[160,2176]{1,0:T(8,128)(2,1)} custom-call(s32[4]{0:T(128)} %refs_0_.7, s32[4,32]{1,0:T(4,128)} %refs_1_.7, s32[4,32]{1,0:T(4,128)} %refs_2_.7, bf16[160,2560]{1,0:T(8,128)(2,1)} %collective-permute-done.4.refs_3_, bf16[160,2560]{1,0:T(8,128)(2,1)} %collective-permute-done.5.refs_4_, bf16[32,256,256]{2,1,0:T(8,128)(2,1)} %refs_5_.7, ...), custom_call_target="tpu_custom_call" | custom-call | flops 5368709120 | bytes 1280 | tf_op jit(solution)/shard_map/other_part/pallas_call | solution.py:320
  110.6 4.0 %collective-permute-start.9 = (bf16[160,2176]{1,0:T(8,128)(2,1)}, bf16[160,2176]{1,0:T(8,128)(2,1)S(1)}, u32[]{:S(2)}, u32[]{:S(2)}) collective-permute-start(bf16[160,2176]{1,0:T(8,128)(2,1)} %other_part.7), channel_id=1, source_target_pairs={{12,0},{0,12},{13,1},{1,13},{14,2},{2,14},{15,3},{3,15},{28,16},{1... | collective-permute-start | bytes 2088968 | tf_op jit(solution)/shard_map/ppermute | solution.py:378
  114.6 0.7 constant_dynamic-slice_fusion.6
  124.0 0.7 fusion.1
  129.8 1.5 %select_bitcast_fusion.1 = bf16[1,160,512]{2,1,0:T(8,128)(2,1)S(1)} fusion(pred[]{:T(512)} %bitcast.18, pred[]{:T(512)S(6)} %and.102, pred[]{:T(512)S(6)} %and.99, pred[]{:T(512)S(6)} %and.96, pred[]{:T(512)S(6)} %and.93, pred[]{:T(512)S(6)} %and.90, pred[]{:T(512)S(6)} %and.87, bf16[160,2560]{1,0:T(8,128)(2,1)} %copy-done.7, ...), kind=kLoop, calls=%fused_computation.7 | loop fusion | flops 901120 | bytes 1310727 | tf_op jit(solution)/shard_map/stack | solution.py:406
  131.2 1.5 %select_bitcast_fusion = bf16[1,160,512]{2,1,0:T(8,128)(2,1)S(1)} fusion(pred[]{:T(512)} %bitcast.27, pred[]{:T(512)S(6)} %and.110, pred[]{:T(512)S(6)} %and.109, pred[]{:T(512)S(6)} %and.108, pred[]{:T(512)S(6)} %and.107, pred[]{:T(512)S(6)} %and.106, pred[]{:T(512)S(6)} %and.105, bf16[160,2560]{1,0:T(8,128)(2,1)} %copy-done.7, ...), kind=kLoop, calls=%fused_computation.6 | loop fusion | flops 901120 | bytes 1310727 | tf_op jit(solution)/shard_map/stack | solution.py:406
  132.7 0.7 pad_maximum_fusion.1
  133.5 0.9 copy-done.5
  134.4 0.9 copy-done.6
  135.2 5.0 %combine.1 = bf16[160,2048]{1,0:T(8,128)(2,1)} custom-call(f32[160,2048]{1,0:T(8,128)} %get-tuple-element.17.own_ref, f32[160,128]{1,0:T(8,128)} %get-tuple-element.18.log_ref, bf16[160,2176]{1,0:T(8,128)(2,1)} %copy-done.3, bf16[160,2176]{1,0:T(8,128)(2,1)} %copy-done.4, bf16[160,2176]{1,0:T(8,128)(2,1)} %copy-done.5, bf16[160,2176]{1,0:T(8,128)(2,1)} %copy-done.6), custom_call_target="tpu_custom_call" | custom-call | tf_op jit(solution)/shard_map/combine/pallas_call | solution.py:390
  (23 shorter events, 0.1 us)
Async XLA Ops:
  1.9 4.9 %copy-start = (bf16[160,2560]{1,0:T(8,128)(2,1)}, bf16[160,2560]{1,0:T(8,128)(2,1)S(1)}, u32[]{:S(2)}) copy-start(bf16[160,2560]{1,0:T(8,128)(2,1)S(1)} %pad_maximum_fusion.payload_ref) | copy-start | bytes 2457604
  1.9 21.0 %collective-permute-start = (bf16[160,2560]{1,0:T(8,128)(2,1)S(1)}, bf16[160,2560]{1,0:T(8,128)(2,1)S(1)}, u32[]{:S(2)}, u32[]{:S(2)}) collective-permute-start(bf16[160,2560]{1,0:T(8,128)(2,1)S(1)} %pad_maximum_fusion.payload_ref), channel_id=1, source_target_pairs={{0,4},{4,8},{8,12},{1,5},{5,9},{9,13},{2,6},{6,10},{10,14},{3,7},{... | collective-permute-start | bytes 2457608 | tf_op jit(solution)/shard_map/ppermute | solution.py:345
  5.4 21.7 %collective-permute-start.1 = (bf16[160,2560]{1,0:T(8,128)(2,1)S(1)}, bf16[160,2560]{1,0:T(8,128)(2,1)}, u32[]{:S(2)}, u32[]{:S(2)}) collective-permute-start(bf16[160,2560]{1,0:T(8,128)(2,1)S(1)} %pad_maximum_fusion.payload_ref), channel_id=1, source_target_pairs={{4,0},{8,4},{12,8},{5,1},{9,5},{13,9},{6,2},{10,6},{14,10},{7,3},{... | collective-permute-start | bytes 2457608 | tf_op jit(solution)/shard_map/ppermute | solution.py:345
  22.9 7.1 %copy-start.7 = (bf16[160,2560]{1,0:T(8,128)(2,1)}, bf16[160,2560]{1,0:T(8,128)(2,1)S(1)}, u32[]{:S(2)}) copy-start(bf16[160,2560]{1,0:T(8,128)(2,1)S(1)} %collective-permute-done.refs_3_) | copy-start | bytes 2457604
  27.1 19.2 %collective-permute-start.2 = (bf16[160,2560]{1,0:T(8,128)(2,1)S(1)}, bf16[160,2560]{1,0:T(8,128)(2,1)}, u32[]{:S(2)}, u32[]{:S(2)}) collective-permute-start(bf16[160,2560]{1,0:T(8,128)(2,1)S(1)} %collective-permute-done.refs_3_), channel_id=1, source_target_pairs={{4,8},{8,12},{5,9},{9,13},{6,10},{10,14},{7,11},{11,15},{20,24},{2... | collective-permute-start | bytes 2457608 | tf_op jit(solution)/shard_map/ppermute | solution.py:345
  28.7 23.3 %collective-permute-start.3 = (bf16[160,2560]{1,0:T(8,128)(2,1)}, bf16[160,2560]{1,0:T(8,128)(2,1)}, u32[]{:S(2)}, u32[]{:S(2)}) collective-permute-start(bf16[160,2560]{1,0:T(8,128)(2,1)} %collective-permute-done.1.refs_3_), channel_id=1, source_target_pairs={{4,0},{8,4},{5,1},{9,5},{6,2},{10,6},{7,3},{11,7},{20,16},{24,20},... | collective-permute-start | bytes 2457608 | tf_op jit(solution)/shard_map/ppermute | solution.py:345
  32.2 22.7 %copy-start.9 = (bf16[160,2176]{1,0:T(8,128)(2,1)S(1)}, bf16[160,2176]{1,0:T(8,128)(2,1)}, u32[]{:S(2)}) copy-start(bf16[160,2176]{1,0:T(8,128)(2,1)} %other_part.4) | copy-start | bytes 2088964
  32.2 38.6 %copy-start.8 = (s32[4]{0:T(128)S(1)}, s32[4]{0:T(128)}, u32[]{:S(2)}) copy-start(s32[4]{0:T(128)} %param.17) | copy-start | bytes 52
  52.0 46.0 %collective-permute-start.4 = (bf16[160,2560]{1,0:T(8,128)(2,1)}, bf16[160,2560]{1,0:T(8,128)(2,1)}, u32[]{:S(2)}, u32[]{:S(2)}) collective-permute-start(bf16[160,2560]{1,0:T(8,128)(2,1)} %collective-permute-done.2.refs_3_), channel_id=1, source_target_pairs={{8,12},{9,13},{10,14},{11,15},{24,28},{25,29},{26,30},{27,31}} | collective-permute-start | bytes 2457608 | tf_op jit(solution)/shard_map/ppermute | solution.py:345
  53.6 44.4 %collective-permute-start.5 = (bf16[160,2560]{1,0:T(8,128)(2,1)}, bf16[160,2560]{1,0:T(8,128)(2,1)}, u32[]{:S(2)}, u32[]{:S(2)}) collective-permute-start(bf16[160,2560]{1,0:T(8,128)(2,1)} %collective-permute-done.3.refs_4_), channel_id=1, source_target_pairs={{4,0},{5,1},{6,2},{7,3},{20,16},{21,17},{22,18},{23,19}} | collective-permute-start | bytes 2457608 | tf_op jit(solution)/shard_map/ppermute | solution.py:345
  54.9 43.1 %collective-permute-start.6 = (bf16[160,2176]{1,0:T(8,128)(2,1)S(1)}, bf16[160,2176]{1,0:T(8,128)(2,1)S(1)}, u32[]{:S(2)}, u32[]{:S(2)}) collective-permute-start(bf16[160,2176]{1,0:T(8,128)(2,1)S(1)} %copy-done.9), channel_id=1, source_target_pairs={{4,0},{8,4},{12,8},{5,1},{9,5},{13,9},{6,2},{10,6},{14,10},{7,3},{... | collective-permute-start | bytes 2088968 | tf_op jit(solution)/shard_map/ppermute | solution.py:378
  56.2 41.8 %collective-permute-start.7 = (bf16[160,2176]{1,0:T(8,128)(2,1)}, bf16[160,2176]{1,0:T(8,128)(2,1)S(1)}, u32[]{:S(2)}, u32[]{:S(2)}) collective-permute-start(bf16[160,2176]{1,0:T(8,128)(2,1)} %other_part.5), channel_id=1, source_target_pairs={{0,4},{4,8},{8,12},{1,5},{5,9},{9,13},{2,6},{6,10},{10,14},{3,7},{... | collective-permute-start | bytes 2088968 | tf_op jit(solution)/shard_map/ppermute | solution.py:378
  85.3 44.4 %copy-start.1 = (bf16[1,160,256]{2,1,0:T(8,128)(2,1)S(1)}, bf16[1,160,256]{2,1,0:T(8,128)(2,1)}, u32[]{:S(2)}) copy-start(bf16[1,160,256]{2,1,0:T(8,128)(2,1)} %param.11) | copy-start | bytes 245764
  85.3 44.4 %copy-start.2 = (bf16[1,160,256]{2,1,0:T(8,128)(2,1)S(1)}, bf16[1,160,256]{2,1,0:T(8,128)(2,1)}, u32[]{:S(2)}) copy-start(bf16[1,160,256]{2,1,0:T(8,128)(2,1)} %param.10) | copy-start | bytes 245764
  85.3 48.1 %collective-permute-start.8 = (bf16[160,2176]{1,0:T(8,128)(2,1)}, bf16[160,2176]{1,0:T(8,128)(2,1)S(1)}, u32[]{:S(2)}, u32[]{:S(2)}) collective-permute-start(bf16[160,2176]{1,0:T(8,128)(2,1)} %other_part.6), channel_id=1, source_target_pairs={{8,0},{12,4},{0,8},{4,12},{9,1},{13,5},{1,9},{5,13},{10,2},{14,6},... | collective-permute-start | bytes 2088968 | tf_op jit(solution)/shard_map/ppermute | solution.py:378
  98.0 12.6 %copy-start.3 = (bf16[160,2176]{1,0:T(8,128)(2,1)}, bf16[160,2176]{1,0:T(8,128)(2,1)S(1)}, u32[]{:S(2)}) copy-start(bf16[160,2176]{1,0:T(8,128)(2,1)S(1)} %collective-permute-done.6.refs_0_) | copy-start | bytes 2088964
  98.0 12.6 %copy-start.4 = (bf16[160,2176]{1,0:T(8,128)(2,1)}, bf16[160,2176]{1,0:T(8,128)(2,1)S(1)}, u32[]{:S(2)}) copy-start(bf16[160,2176]{1,0:T(8,128)(2,1)S(1)} %collective-permute-done.7.refs_1_) | copy-start | bytes 2088964
  110.6 22.9 %collective-permute-start.9 = (bf16[160,2176]{1,0:T(8,128)(2,1)}, bf16[160,2176]{1,0:T(8,128)(2,1)S(1)}, u32[]{:S(2)}, u32[]{:S(2)}) collective-permute-start(bf16[160,2176]{1,0:T(8,128)(2,1)} %other_part.7), channel_id=1, source_target_pairs={{12,0},{0,12},{13,1},{1,13},{14,2},{2,14},{15,3},{3,15},{28,16},{1... | collective-permute-start | bytes 2088968 | tf_op jit(solution)/shard_map/ppermute | solution.py:378
  133.5 0.9 copy-start.5
  134.4 0.9 copy-start.6

commit v4 on v3

v4 whole, which is shorter than its diff:
```python
import functools
import math

import jax
import jax.numpy as jnp
from jax import lax
from jax.experimental import pallas as pl
from jax.experimental.pallas import tpu as pltpu
from jax.sharding import PartitionSpec as P

HEADS = 64
KVH = 8
HD = 128
MAXBLK = 32
CAPP = 2
GROUP = HEADS // KVH
EMPTY = -1e30
LINE = 8
TILE = 256
ONES = 16
SCALE = 1.0 / math.sqrt(HD)
EXP2_SCALE = SCALE * math.log2(math.e)
VMEM_LIMIT = 60 * 1024 * 1024 + 256 * 1024


def fetch(pool_size, tables, request, stores, buffers, sems):
    prefix_ref, store_ref, slot_ref = tables
    me = lax.axis_index("pool")
    first = lax.rem(me - store_ref[request, 0] + pool_size, pool_size)
    count = lax.max(lax.div(prefix_ref[request] - first + pool_size - 1, pool_size), 0)

    def copies(entry):
        slot = slot_ref[request, first + entry * pool_size]
        return [
            pltpu.make_async_copy(stores[i].at[slot], buffers[i].at[entry], sems.at[i, entry])
            for i in range(2)
        ]

    def start(entry, carry):
        for copy in copies(entry):
            copy.start()
        return carry

    lax.fori_loop(0, count, start, 0)

    def ready(entry):
        for copy in copies(entry):
            copy.wait()

    return count, ready


def attend(
    key_ref, value_ref, count, ready, fresh, new_rows, columns, turned, peaks, acc, log_type, put
):
    kv_local, _, rows = columns.shape

    def visit(keys, values, seen):
        for kv in range(kv_local):
            turned[kv, :HD, :] = values[kv].T
        tiles = [(kv, i) for kv in range(kv_local) for i in range(0, rows, TILE)]
        blocks = {}
        weights = {}
        for step in range(len(tiles) + 2):
            if step < len(tiles):
                kv, i = tiles[step]
                block = lax.dot_general(
                    keys[kv],
                    columns[kv, :, i : i + TILE],
                    (((1,), (0,)), ((), ())),
                    preferred_element_type=jnp.float32,
                )
                if seen is not None:
                    block = jnp.where(seen(i), block, EMPTY)
                blocks[step] = block
            if step >= 2:
                kv, i = tiles[step - 2]
                part = slice(i, i + TILE)
                weight, factor = weights.pop(step - 2)
                added = lax.dot_general(
                    turned[kv], weight, (((1,), (0,)), ((), ())), preferred_element_type=jnp.float32
                )
                acc[kv, :, part] = acc[kv, :, part] * factor + added
            if 1 <= step <= len(tiles):
                kv, i = tiles[step - 1]
                part = slice(i, i + TILE)
                block = blocks.pop(step - 1)
                before = peaks[kv, :, part]
                peak = jnp.maximum(before, jnp.max(block, axis=0, keepdims=True))
                peaks[kv, :, part] = peak
                factor = jnp.exp2((before - peak) * EXP2_SCALE)[0:1]
                weight = jnp.exp2(block * EXP2_SCALE - peak[0:1] * EXP2_SCALE)
                weights[step - 1] = (weight.astype(jnp.bfloat16), factor)

    def lanes_of(ref):
        return [ref[:, kv * HD : (kv + 1) * HD] for kv in range(kv_local)]

    peaks[...] = jnp.full(peaks.shape, EMPTY, jnp.float32)
    acc[...] = jnp.zeros(acc.shape, jnp.float32)
    turned[:, HD:, :] = jnp.ones((kv_local, ONES, turned.shape[2]), jnp.bfloat16)
    if fresh is not None:
        new_key_ref, new_value_ref = fresh

        def seen(i):
            shape = (new_key_ref.shape[0], TILE)
            row = lax.rem(lax.broadcasted_iota(jnp.int32, (1, TILE), 1) + i, new_rows)
            return lax.broadcasted_iota(jnp.int32, shape, 0) <= row

        visit(lanes_of(new_key_ref), lanes_of(new_value_ref), seen)

    def visit_block(entry, carry):
        ready(entry)
        visit(lanes_of(key_ref.at[entry]), lanes_of(value_ref.at[entry]), None)
        return carry

    lax.fori_loop(0, count, visit_block, 0)
    heads = kv_local * GROUP
    logs = []
    for kv in range(kv_local):
        total = acc[kv, HD : HD + 1, :]
        safe = jnp.where(total > 0, total, 1.0)
        logs.append(jnp.where(total > 0, peaks[kv, 0:1] * SCALE + jnp.log(safe), EMPTY))
        out = (acc[kv, :HD, :] * (1.0 / safe)).astype(log_type).T
        for g in range(GROUP):
            put(kv * GROUP + g, out[g * new_rows : (g + 1) * new_rows])
    logs += [logs[-1]] * (8 - len(logs))
    log_columns = jnp.concatenate(logs, axis=0).T
    lane = lax.broadcasted_iota(jnp.int32, (new_rows, HD), 1)
    place = jnp.where(lane < 3 * heads, lax.rem(lane, heads), -1)
    tile = jnp.zeros((new_rows, HD), jnp.float32)
    for kv in range(kv_local):
        for g in range(GROUP):
            column = log_columns[g * new_rows : (g + 1) * new_rows, kv : kv + 1]
            tile = jnp.where(place == kv * GROUP + g, column, tile)
    return tile


def load_heads(query_ref, query_rows, columns):
    new_rows = query_ref.shape[0]
    for kv in range(columns.shape[0]):
        for g in range(GROUP):
            head = kv * GROUP + g
            query_rows[g * new_rows : (g + 1) * new_rows, :] = query_ref[
                :, head * HD : (head + 1) * HD
            ]
        columns[kv] = query_rows[...].T


def split_lanes(tile, heads):
    lane = lax.broadcasted_iota(jnp.int32, tile.shape, 1)
    high = tile.astype(jnp.bfloat16).astype(jnp.float32)
    middle = (tile - high).astype(jnp.bfloat16).astype(jnp.float32)
    low = tile - high - middle
    return jnp.where(lane < heads, high, jnp.where(lane < 2 * heads, middle, low)).astype(
        jnp.bfloat16
    )


def own_kernel(
    pool_size,
    prefix_ref,
    store_ref,
    slot_ref,
    payload_ref,
    store_keys,
    store_values,
    out_ref,
    log_ref,
    key_buf,
    value_buf,
    new_key_buf,
    new_value_buf,
    query_rows,
    columns,
    *state,
):
    *work, sems = state
    count, ready = fetch(
        pool_size,
        (prefix_ref, store_ref, slot_ref),
        lax.axis_index("pool"),
        (store_keys, store_values),
        (key_buf, value_buf),
        sems,
    )
    new_rows, width = out_ref.shape
    kv_width = new_key_buf.shape[1]
    for i, buffer in enumerate((new_key_buf, new_value_buf)):
        buffer[:new_rows, :] = payload_ref[:, width + i * kv_width : width + (i + 1) * kv_width]
        buffer[new_rows:, :] = jnp.zeros((buffer.shape[0] - new_rows, kv_width), jnp.bfloat16)

    def put(head, out):
        out_ref[:, head * HD : (head + 1) * HD] = out

    load_heads(payload_ref, query_rows, columns)
    log_ref[...] = attend(
        key_buf,
        value_buf,
        count,
        ready,
        (new_key_buf, new_value_buf),
        new_rows,
        columns,
        *work,
        jnp.float32,
        put,
    )


def other_kernel(pool_size, offsets, *refs):
    if offsets[0] is None:
        wanted = [refs[0][0]]
        refs = refs[1:]
    else:
        wanted = [lax.axis_index("pool") + offset for offset in offsets]
    tables, refs = refs[:3], refs[3:]
    payload_refs = refs[: len(offsets)]
    store_keys, store_values, out_ref, key_buf, value_buf, query_rows, columns, *state = refs[
        len(offsets) :
    ]
    *work, sems = state
    there = [(x >= 0) & (x < pool_size) for x in wanted]
    request = wanted[0]
    for other, hit in zip(wanted[1:], there[1:]):
        request = jnp.where(hit, other, request)

    @pl.when(functools.reduce(jnp.logical_or, there))
    def _():
        count, ready = fetch(
            pool_size, tables, request, (store_keys, store_values), (key_buf, value_buf), sems
        )
        new_rows = out_ref.shape[0]
        width = out_ref.shape[1] - HD
        for payload_ref, hit in zip(payload_refs, there):
            pl.when(hit)(functools.partial(load_heads, payload_ref, query_rows, columns))

        def put(head, out):
            out_ref[:, head * HD : (head + 1) * HD] = out

        tile = attend(
            key_buf, value_buf, count, ready, None, new_rows, columns, *work, jnp.bfloat16, put
        )
        out_ref[:, width:] = split_lanes(tile, width // HD)


def push_kernel(pool_size, entries, owner_ref, *refs):
    payload_refs = refs[: len(entries)]
    key_out, value_out, zeros, sems = refs[len(entries) :]
    outs = (key_out, value_out)
    new_rows, kv_width = zeros.shape
    me = lax.axis_index("pool")
    zeros[...] = jnp.zeros(zeros.shape, jnp.bfloat16)

    def copy(source, i, place):
        return pltpu.make_async_copy(source, outs[i].at[place], sems.at[i, place])

    for (relative, request), payload_ref in zip(entries, payload_refs):
        source = me + request if relative else jnp.int32(request)
        there = (source >= 0) & (source < pool_size)
        source = jnp.clip(source, 0, pool_size - 1)
        rank = jnp.int32(0)
        for other in range(pool_size):
            rank += ((owner_ref[other] == me) & (other < source)).astype(jnp.int32)
        hit = there & (owner_ref[source] == me)
        width = payload_ref.shape[1] - 2 * kv_width
        for place in range(CAPP):

            @pl.when(hit & (rank == place))
            def _():
                for i in range(2):
                    start = width + i * kv_width
                    copy(payload_ref.at[:, start : start + kv_width], i, place).start()

    total = jnp.int32(0)
    for other in range(pool_size):
        total += (owner_ref[other] == me).astype(jnp.int32)
    for place in range(CAPP):

        @pl.when(total <= place)
        def _():
            for i in range(2):
                copy(zeros, i, place).start()

    for place in range(CAPP):
        for i in range(2):
            copy(zeros, i, place).wait()


def combine_kernel(sources, pool_size, out_ref_count, own_ref, log_ref, *refs):
    parts = refs[: len(sources)]
    out_ref = refs[len(sources)]
    width = own_ref.shape[1]
    heads = width // HD
    logs = [log_ref[...]]
    me = lax.axis_index("pool")
    for (offsets, source), part in zip(sources, parts):
        if offsets:
            wanted = [me + offset for offset in offsets]
            there = functools.reduce(
                jnp.logical_or, [(x >= 0) & (x < pool_size) for x in wanted]
            )
        else:
            there = me != source
        tile = part[:, width:].astype(jnp.float32)
        whole = (
            tile + pltpu.roll(tile, HD - heads, 1) + pltpu.roll(tile, HD - 2 * heads, 1)
        )
        logs.append(jnp.where(there, whole, EMPTY))
    peak = functools.reduce(jnp.maximum, logs)
    shares = [jnp.exp(x - peak) for x in logs]
    total = functools.reduce(jnp.add, shares)
    shares = [x * (1.0 / total) for x in shares]
    for head in range(heads):
        lanes = slice(head * HD, (head + 1) * HD)
        mixed = own_ref[:, lanes] * shares[0][:, head : head + 1]
        for share, part in zip(shares[1:], parts):
            mixed = mixed + part[:, lanes].astype(jnp.float32) * share[:, head : head + 1]
        out_ref[:, lanes] = mixed.astype(out_ref.dtype)
    if out_ref_count == 2:
        refs[len(sources) + 1][...] = peak + jnp.log(total)


def shards(
    queries,
    new_keys,
    new_values,
    store_keys,
    store_values,
    prefix_blocks,
    hit_store,
    hit_slot,
    decode_owner,
):
    pool_size = lax.axis_size("pool")
    capacity = (MAXBLK + pool_size - 1) // pool_size
    new_rows = queries.shape[1]
    width = queries.shape[2]
    kv_width = new_keys.shape[2]
    block_len = store_keys.shape[1]
    rows = GROUP * new_rows
    tables = (prefix_blocks, hit_store, hit_slot)
    smem_spec = pl.BlockSpec(memory_space=pltpu.SMEM)
    hbm_spec = pl.BlockSpec(memory_space=pltpu.HBM)
    vmem_spec = pl.BlockSpec(memory_space=pltpu.VMEM)
    params = pltpu.CompilerParams(vmem_limit_bytes=VMEM_LIMIT)

    def cost(share):
        return pl.CostEstimate(
            flops=share * rows * block_len * kv_width * capacity,
            bytes_accessed=rows,
            transcendentals=0,
        )

    buffers = [pltpu.VMEM((capacity, block_len, kv_width), jnp.bfloat16)] * 2
    kv_local = kv_width // HD
    work = [
        pltpu.VMEM((rows, HD), jnp.bfloat16),
        pltpu.VMEM((kv_local, HD, rows), jnp.bfloat16),
        pltpu.VMEM((kv_local, HD + ONES, block_len), jnp.bfloat16),
        pltpu.VMEM((kv_local, 8, rows), jnp.float32),
        pltpu.VMEM((kv_local, HD + ONES, rows), jnp.float32),
    ]
    sems = pltpu.SemaphoreType.DMA((2, capacity))

    def own_part(payload):
        return pl.pallas_call(
            functools.partial(own_kernel, pool_size),
            in_specs=[smem_spec] * 3 + [vmem_spec] + [hbm_spec] * 2,
            out_specs=[vmem_spec] * 2,
            scratch_shapes=[
                *buffers,
                *[pltpu.VMEM((block_len, kv_width), jnp.bfloat16)] * 2,
                *work,
                sems,
            ],
            out_shape=[
                jax.ShapeDtypeStruct((new_rows, width), jnp.float32),
                jax.ShapeDtypeStruct((new_rows, HD), jnp.float32),
            ],
            compiler_params=params,
            cost_estimate=cost(8),
            name="own_part",
        )(*tables, payload, store_keys, store_values)

    def other_part(offsets, held, *request):
        return pl.pallas_call(
            functools.partial(other_kernel, pool_size, offsets),
            in_specs=[smem_spec] * (3 + len(request)) + [vmem_spec] * len(held) + [hbm_spec] * 2,
            out_specs=vmem_spec,
            scratch_shapes=[
                *buffers,
                *work,
                sems,
            ],
            out_shape=jax.ShapeDtypeStruct((new_rows, width + HD), jnp.bfloat16),
            compiler_params=params,
            cost_estimate=cost(0 if len(held) == 1 else 8),
            name="other_part",
        )(*request, *tables, *held, store_keys, store_values)

    def combine(own, log, sources, parts, last=True):
        out_shape = [jax.ShapeDtypeStruct((new_rows, width), jnp.bfloat16 if last else jnp.float32)]
        if not last:
            out_shape.append(jax.ShapeDtypeStruct((new_rows, HD), jnp.float32))
        out = pl.pallas_call(
            functools.partial(combine_kernel, tuple(sources), pool_size, len(out_shape)),
            in_specs=[vmem_spec] * (2 + len(sources)),
            out_specs=[vmem_spec] * len(out_shape),
            out_shape=out_shape,
            compiler_params=params,
            name="combine",
        )(own, log, *parts)
        return out[0] if last else out

    def inside(index):
        return 0 <= index < pool_size

    def forward(array, distance, first):
        pairs = [
            (i, i + distance)
            for i in range(pool_size)
            if inside(i + distance) and inside(i - first)
        ]
        return lax.ppermute(array, "pool", pairs)

    payload = jnp.concatenate([queries[0], new_keys[0], new_values[0]], axis=1)
    own_out, own_log = own_part(payload)
    if pool_size <= LINE:
        sources = []
        parts = []
        right, left = payload, payload
        moved = [((True, 0), payload)]
        done = [own_out, own_log]
        for step in range(1, pool_size):
            right = forward(right, 1, step - 1)
            left = forward(left, -1, 1 - step)
            right, left, done = lax.optimization_barrier((right, left, done))
            if step == 1:
                own_out, own_log = done
            done = []
            moved += [((True, -step), right), ((True, step), left)]
            held_right, held_left = right, left
            if step == 2:
                held_right, held_left, parts = lax.optimization_barrier((right, left, parts))
            if 2 * step < pool_size:
                groups = [((-step,), (held_right,)), ((step,), (held_left,))]
            else:
                groups = [((-step, step), (held_right, held_left))]
            for offsets, held in groups:
                packed = other_part(offsets, held)
                done.append(packed)
                pairs = [(i, i + x) for x in offsets for i in range(pool_size) if inside(i + x)]
                parts.append(lax.ppermute(packed, "pool", pairs))
                sources.append((tuple(-x for x in offsets), None))
        if len(parts) > 2:
            own_out, own_log, done = lax.optimization_barrier((own_out, own_log, done))
            own_out, own_log = combine(own_out, own_log, sources[:-2], parts[:-2], last=False)
            sources, parts = sources[-2:], parts[-2:]
    else:
        gathered = lax.all_gather(payload, "pool", axis=0, tiled=False)
        packed = lax.map(
            lambda pair: other_part((None,), (pair[0],), pair[1].reshape(1)),
            (gathered, jnp.arange(pool_size, dtype=jnp.int32)),
        )
        parts = lax.all_to_all(packed, "pool", split_axis=0, concat_axis=0, tiled=True)
        sources = [(None, source) for source in range(pool_size)]
        moved = [((False, source), gathered[source]) for source in range(pool_size)]

    attended = combine(own_out, own_log, sources, parts)
    pushed_keys, pushed_values = pl.pallas_call(
        functools.partial(push_kernel, pool_size, tuple(entry for entry, _ in moved)),
        in_specs=[smem_spec] + [hbm_spec] * len(moved),
        out_specs=[hbm_spec] * 2,
        scratch_shapes=[
            pltpu.VMEM((new_rows, kv_width), jnp.bfloat16),
            pltpu.SemaphoreType.DMA((2, CAPP)),
        ],
        out_shape=[jax.ShapeDtypeStruct((CAPP, new_rows, kv_width), jnp.bfloat16)] * 2,
        compiler_params=params,
        name="push",
    )(decode_owner, *[array for _, array in moved])
    return (attended[None], pushed_keys, pushed_values)


def solution(mesh):
    in_specs = (
        P(("groups", "pool"), None, ("tensor", "sub")),
        P(("groups", "pool"), None, ("tensor", "sub")),
        P(("groups", "pool"), None, ("tensor", "sub")),
        P(("groups", "pool"), None, ("tensor", "sub")),
        P(("groups", "pool"), None, ("tensor", "sub")),
        P("groups"),
        P("groups", None),
        P("groups", None),
        P("groups"),
    )
    out_specs = (
        P(("groups", "pool"), None, ("tensor", "sub")),
        P(("groups", "pool"), None, ("tensor", "sub")),
        P(("groups", "pool"), None, ("tensor", "sub")),
    )
    return jax.shard_map(shards, mesh=mesh, in_specs=in_specs, out_specs=out_specs, check_vma=False)
```

time: 139 us -> 145 us (1.043); the launches traced: 140 us -> 144 us
  between operations: 14.7 us -> 0.83 us
  starting transfers between devices: 31.8 us -> 42.9 us
  waiting for transfers between devices: 22.8 us -> 32.8 us
  other arithmetic: 5.09 us -> 1.23 us
    ppermute x4, waiting for transfers between devices: 11.2 us -> 26.3 us  [shards(): parts.append(lax.ppermute(packed, 'pool', pairs))]
    ppermute x4, starting transfers between devices: 21.3 us -> 34.1 us  [shards(): parts.append(lax.ppermute(packed, 'pool', pairs))]
    ppermute x6, waiting for transfers between devices: 11.6 us -> 6.51 us  [forward(): return lax.ppermute(array, 'pool', pairs)]
    pallas_call x1 -> x3, Pallas kernels: 5.03 us -> 9.5 us  [the longest x2 7.92 us: combine(): pl.pallas_call(functools.partial(combine_kernel, tuple(sources), pool_siz...]
    another operation x5 -> x0, other arithmetic: 3.86 us -> none  [the longest x3 3.67 us: shards(): pushed = jnp.stack(pushed)]
    pallas_call x4, Pallas kernels: 43.1 us -> 40.5 us  [other_part(): pl.pallas_call(functools.partial(other_kernel, pool_size, offsets), in_sp...]
    ppermute x6, starting transfers between devices: 10.5 us -> 8.82 us  [forward(): return lax.ppermute(array, 'pool', pairs)]
  transfers between devices with their start and end apart: 10 -> 10, of which waited for: 4 -> 4; matrix products, arithmetic and copies ran while one was open for 4% -> 0% of each run, Pallas kernels for 41% -> 42%
where the time goes in v4:
time: 145 us; the launch traced here: 144 us
  Pallas kernels  63.8 us (44%)
  starting transfers between devices  42.9 us (30%)
  waiting for transfers between devices  32.8 us (23%)
  local copies, waits for them, and re-layouts  2.71 us (2%)
    pallas_call x4, Pallas kernels, other_part(): pl.pallas_call(functools.partial(other_kernel, pool_size, offsets), in_sp...  40.5 us
    ppermute x4, starting transfers between devices, shards(): parts.append(lax.ppermute(packed, 'pool', pairs))  34.1 us
    ppermute x4, waiting for transfers between devices, shards(): parts.append(lax.ppermute(packed, 'pool', pairs))  26.3 us
    pallas_call x1, Pallas kernels, own_part(): pl.pallas_call(functools.partial(own_kernel, pool_size), in_specs=[smem_s...  13.8 us
    ppermute x6, starting transfers between devices, forward(): return lax.ppermute(array, 'pool', pairs)  8.82 us
    pallas_call x2, Pallas kernels, combine(): pl.pallas_call(functools.partial(combine_kernel, tuple(sources), pool_siz...  7.92 us
    ppermute x6, waiting for transfers between devices, forward(): return lax.ppermute(array, 'pool', pairs)  6.51 us
  transfers between devices with their start and end apart: 10, of which 4 were waited for; matrix products, arithmetic and copies ran while one was open for 0% of the time, Pallas kernels for 42%

profile of v4, /device:TPU:4, one launch (start us, length us, event | category | flops | bytes accessed | tf_op | source)
XLA Modules:
  0.0 144.3 jit_solution(12734576028510504580)
XLA Ops:
  0.6 1.2 pad_maximum_fusion.payload_ref.refs_0_
  1.9 3.5 %collective-permute-start = (bf16[160,2560]{1,0:T(8,128)(2,1)S(1)}, bf16[160,2560]{1,0:T(8,128)(2,1)S(1)}, u32[]{:S(2)}, u32[]{:S(2)}) collective-permute-start(bf16[160,2560]{1,0:T(8,128)(2,1)S(1)} %pad_maximum_fusion.payload_ref.refs_0_), channel_id=1, source_target_pairs={{0,4},{4,8},{8,12},{1,5},{5,9},{9,13},{2,6},{6,10},{10,14},{3,7},{... | collective-permute-start | bytes 2457608 | tf_op jit(solution)/shard_map/ppermute | solution.py:424
  5.4 1.3 collective-permute-start.1
  6.7 13.8 %own_part.1 = (f32[160,2048]{1,0:T(8,128)}, f32[160,128]{1,0:T(8,128)}) custom-call(s32[4]{0:T(128)} %refs_0_.7, s32[4,32]{1,0:T(4,128)} %refs_1_.7, s32[4,32]{1,0:T(4,128)} %refs_2_.7, bf16[160,2560]{1,0:T(8,128)(2,1)} %copy-done, bf16[32,256,256]{2,1,0:T(8,128)(2,1)} %refs_5_.7, bf16[32,256,256]{2,1,0:T(8,128)(2,1)} %refs_6_.3), custom_call_target="tpu_custom_call" | custom-call | flops 5368709120 | bytes 1280 | tf_op jit(solution)/shard_map/own_part/pallas_call | solution.py:366
  20.5 2.3 %collective-permute-done.refs_3_.refs_1_ = bf16[160,2560]{1,0:T(8,128)(2,1)S(1)} collective-permute-done((bf16[160,2560]{1,0:T(8,128)(2,1)S(1)}, bf16[160,2560]{1,0:T(8,128)(2,1)S(1)}, u32[]{:S(2)}, u32[]{:S(2)}) %collective-permute-start) | collective-permute-done | bytes 819232 | tf_op jit(solution)/shard_map/ppermute | solution.py:424
  22.9 4.2 %collective-permute-done.1.refs_3_.refs_2_ = bf16[160,2560]{1,0:T(8,128)(2,1)S(1)} collective-permute-done((bf16[160,2560]{1,0:T(8,128)(2,1)S(1)}, bf16[160,2560]{1,0:T(8,128)(2,1)S(1)}, u32[]{:S(2)}, u32[]{:S(2)}) %collective-permute-start.1) | collective-permute-done | bytes 819232 | tf_op jit(solution)/shard_map/ppermute | solution.py:424
  27.0 0.7 collective-permute-start.2
  27.7 1.3 collective-permute-start.3
  29.0 2.2 %other_part.4 = bf16[160,2176]{1,0:T(8,128)(2,1)} custom-call(s32[4]{0:T(128)} %refs_0_.7, s32[4,32]{1,0:T(4,128)} %refs_1_.7, s32[4,32]{1,0:T(4,128)} %refs_2_.7, bf16[160,2560]{1,0:T(8,128)(2,1)} %copy-done.1, bf16[32,256,256]{2,1,0:T(8,128)(2,1)} %refs_5_.7, bf16[32,256,256]{2,1,0:T(8,128)(2,1)} %refs_6_.3), custom_call_target="tpu_custom_call" | custom-call | bytes 1280 | tf_op jit(solution)/shard_map/other_part/pallas_call | solution.py:386
  31.2 11.5 %other_part.5 = bf16[160,2176]{1,0:T(8,128)(2,1)} custom-call(s32[4]{0:T(128)} %refs_0_.7, s32[4,32]{1,0:T(4,128)} %refs_1_.7, s32[4,32]{1,0:T(4,128)} %refs_2_.7, bf16[160,2560]{1,0:T(8,128)(2,1)} %copy-done.2, bf16[32,256,256]{2,1,0:T(8,128)(2,1)} %refs_5_.7, bf16[32,256,256]{2,1,0:T(8,128)(2,1)} %refs_6_.3), custom_call_target="tpu_custom_call" | custom-call | bytes 1280 | tf_op jit(solution)/shard_map/other_part/pallas_call | solution.py:386
  42.8 1.3 collective-permute-start.6
  44.1 23.9 %collective-permute-start.7 = (bf16[160,2176]{1,0:T(8,128)(2,1)}, bf16[160,2176]{1,0:T(8,128)(2,1)}, u32[]{:S(2)}, u32[]{:S(2)}) collective-permute-start(bf16[160,2176]{1,0:T(8,128)(2,1)} %other_part.5), channel_id=1, source_target_pairs={{0,4},{4,8},{8,12},{1,5},{5,9},{9,13},{2,6},{6,10},{10,14},{3,7},{... | collective-permute-start | bytes 2088968 | tf_op jit(solution)/shard_map/ppermute | solution.py:453
  67.9 0.0 collective-permute-done.2.refs_3_
  67.9 0.0 collective-permute-done.3.refs_4_
  67.9 0.7 collective-permute-start.4
  68.7 1.3 collective-permute-start.5
  70.0 11.9 %collective-permute-done.6.refs_0_ = bf16[160,2176]{1,0:T(8,128)(2,1)} collective-permute-done((bf16[160,2176]{1,0:T(8,128)(2,1)}, bf16[160,2176]{1,0:T(8,128)(2,1)}, u32[]{:S(2)}, u32[]{:S(2)}) %collective-permute-start.6) | collective-permute-done | bytes 696352 | tf_op jit(solution)/shard_map/ppermute | solution.py:453
  81.9 0.0 collective-permute-done.7.refs_1_
  81.9 16.5 %other_part.6 = bf16[160,2176]{1,0:T(8,128)(2,1)} custom-call(s32[4]{0:T(128)} %refs_0_.7, s32[4,32]{1,0:T(4,128)} %refs_1_.7, s32[4,32]{1,0:T(4,128)} %refs_2_.7, bf16[160,2560]{1,0:T(8,128)(2,1)} %copy-done.3, bf16[160,2560]{1,0:T(8,128)(2,1)} %copy-done.4, bf16[32,256,256]{2,1,0:T(8,128)(2,1)} %refs_5_.7, bf16[32,256,256]{2,1,0:T(8,128)(2,1)} %refs_6_.3), custom_call_target="tpu_custom_call" | custom-call | flops 5368709120 | bytes 1280 | tf_op jit(solution)/shard_map/other_part/pallas_call | solution.py:386
  98.4 0.1 collective-permute-start.8
  98.5 0.0 collective-permute-done.4.refs_3_.refs_5_
  98.5 0.0 collective-permute-done.5.refs_4_.refs_6_
  98.5 0.9 copy-done.5
  99.4 0.9 copy-done.6
  100.4 10.3 %other_part.7 = bf16[160,2176]{1,0:T(8,128)(2,1)} custom-call(s32[4]{0:T(128)} %refs_0_.7, s32[4,32]{1,0:T(4,128)} %refs_1_.7, s32[4,32]{1,0:T(4,128)} %refs_2_.7, bf16[160,2560]{1,0:T(8,128)(2,1)} %copy-done.5, bf16[160,2560]{1,0:T(8,128)(2,1)} %copy-done.6, bf16[32,256,256]{2,1,0:T(8,128)(2,1)} %refs_5_.7, bf16[32,256,256]{2,1,0:T(8,128)(2,1)} %refs_6_.3), custom_call_target="tpu_custom_call" | custom-call | flops 5368709120 | bytes 1280 | tf_op jit(solution)/shard_map/other_part/pallas_call | solution.py:386
  110.6 8.9 %collective-permute-start.9 = (bf16[160,2176]{1,0:T(8,128)(2,1)}, bf16[160,2176]{1,0:T(8,128)(2,1)S(1)}, u32[]{:S(2)}, u32[]{:S(2)}) collective-permute-start(bf16[160,2176]{1,0:T(8,128)(2,1)} %other_part.7), channel_id=1, source_target_pairs={{12,0},{0,12},{13,1},{1,13},{14,2},{2,14},{15,3},{3,15},{28,16},{1... | collective-permute-start | bytes 2088968 | tf_op jit(solution)/shard_map/ppermute | solution.py:453
  119.5 1.6 %push.1 = (bf16[2,160,256]{2,1,0:T(8,128)(2,1)}, bf16[2,160,256]{2,1,0:T(8,128)(2,1)}) custom-call(s32[4]{0:T(128)} %owner_ref.1, bf16[160,2560]{1,0:T(8,128)(2,1)} %copy-done, bf16[160,2560]{1,0:T(8,128)(2,1)} %copy-done.1, bf16[160,2560]{1,0:T(8,128)(2,1)} %copy-done.2, bf16[160,2560]{1,0:T(8,128)(2,1)} %copy-done.3, bf16[160,2560]{1,0:T(8,128)(2,1)} %copy-done.4, ...), custom_call_target="tpu_custom_call" | custom-call | tf_op jit(solution)/shard_map/push/pallas_call | solution.py:470
  121.1 4.1 %combine.2 = (f32[160,2048]{1,0:T(8,128)}, f32[160,128]{1,0:T(8,128)}) custom-call(f32[160,2048]{1,0:T(8,128)} %get-tuple-element.35.own_ref, f32[160,128]{1,0:T(8,128)} %get-tuple-element.36.log_ref, bf16[160,2176]{1,0:T(8,128)(2,1)} %collective-permute-done.6.refs_0_, bf16[160,2176]{1,0:T(8,128)(2,1)} %collective-permute-done.7.refs_1_), custom_call_target="tpu_custom_call" | custom-call | tf_op jit(solution)/shard_map/combine/pallas_call | solution.py:405
  125.2 14.3 %collective-permute-done.8.refs_0_ = bf16[160,2176]{1,0:T(8,128)(2,1)} collective-permute-done((bf16[160,2176]{1,0:T(8,128)(2,1)}, bf16[160,2176]{1,0:T(8,128)(2,1)}, u32[]{:S(2)}, u32[]{:S(2)}) %collective-permute-start.8) | collective-permute-done | bytes 696352 | tf_op jit(solution)/shard_map/ppermute | solution.py:453
  139.5 0.0 collective-permute-done.9.refs_1_
  139.5 0.9 copy-done.7
  140.4 3.8 %combine.3 = bf16[160,2048]{1,0:T(8,128)(2,1)} custom-call(f32[160,2048]{1,0:T(8,128)} %get-tuple-element.39.own_ref, f32[160,128]{1,0:T(8,128)} %get-tuple-element.40.log_ref, bf16[160,2176]{1,0:T(8,128)(2,1)} %collective-permute-done.8.refs_0_, bf16[160,2176]{1,0:T(8,128)(2,1)} %copy-done.7), custom_call_target="tpu_custom_call" | custom-call | tf_op jit(solution)/shard_map/combine/pallas_call | solution.py:405
  (13 shorter events, 0.0 us)
Async XLA Ops:
  1.9 4.9 %copy-start = (bf16[160,2560]{1,0:T(8,128)(2,1)}, bf16[160,2560]{1,0:T(8,128)(2,1)S(1)}, u32[]{:S(2)}) copy-start(bf16[160,2560]{1,0:T(8,128)(2,1)S(1)} %pad_maximum_fusion.payload_ref.refs_0_) | copy-start | bytes 2457604
  1.9 21.0 %collective-permute-start = (bf16[160,2560]{1,0:T(8,128)(2,1)S(1)}, bf16[160,2560]{1,0:T(8,128)(2,1)S(1)}, u32[]{:S(2)}, u32[]{:S(2)}) collective-permute-start(bf16[160,2560]{1,0:T(8,128)(2,1)S(1)} %pad_maximum_fusion.payload_ref.refs_0_), channel_id=1, source_target_pairs={{0,4},{4,8},{8,12},{1,5},{5,9},{9,13},{2,6},{6,10},{10,14},{3,7},{... | collective-permute-start | bytes 2457608 | tf_op jit(solution)/shard_map/ppermute | solution.py:424
  5.4 21.6 %collective-permute-start.1 = (bf16[160,2560]{1,0:T(8,128)(2,1)S(1)}, bf16[160,2560]{1,0:T(8,128)(2,1)S(1)}, u32[]{:S(2)}, u32[]{:S(2)}) collective-permute-start(bf16[160,2560]{1,0:T(8,128)(2,1)S(1)} %pad_maximum_fusion.payload_ref.refs_0_), channel_id=1, source_target_pairs={{4,0},{8,4},{12,8},{5,1},{9,5},{13,9},{6,2},{10,6},{14,10},{7,3},{... | collective-permute-start | bytes 2457608 | tf_op jit(solution)/shard_map/ppermute | solution.py:424
  22.9 6.2 %copy-start.1 = (bf16[160,2560]{1,0:T(8,128)(2,1)}, bf16[160,2560]{1,0:T(8,128)(2,1)S(1)}, u32[]{:S(2)}) copy-start(bf16[160,2560]{1,0:T(8,128)(2,1)S(1)} %collective-permute-done.refs_3_.refs_1_) | copy-start | bytes 2457604
  27.0 4.2 %copy-start.2 = (bf16[160,2560]{1,0:T(8,128)(2,1)}, bf16[160,2560]{1,0:T(8,128)(2,1)S(1)}, u32[]{:S(2)}) copy-start(bf16[160,2560]{1,0:T(8,128)(2,1)S(1)} %collective-permute-done.1.refs_3_.refs_2_) | copy-start | bytes 2457604
  27.0 40.9 %collective-permute-start.2 = (bf16[160,2560]{1,0:T(8,128)(2,1)S(1)}, bf16[160,2560]{1,0:T(8,128)(2,1)S(1)}, u32[]{:S(2)}, u32[]{:S(2)}) collective-permute-start(bf16[160,2560]{1,0:T(8,128)(2,1)S(1)} %collective-permute-done.refs_3_.refs_1_), channel_id=1, source_target_pairs={{4,8},{8,12},{5,9},{9,13},{6,10},{10,14},{7,11},{11,15},{20,24},{2... | collective-permute-start | bytes 2457608 | tf_op jit(solution)/shard_map/ppermute | solution.py:424
  27.7 40.2 %collective-permute-start.3 = (bf16[160,2560]{1,0:T(8,128)(2,1)S(1)}, bf16[160,2560]{1,0:T(8,128)(2,1)S(1)}, u32[]{:S(2)}, u32[]{:S(2)}) collective-permute-start(bf16[160,2560]{1,0:T(8,128)(2,1)S(1)} %collective-permute-done.1.refs_3_.refs_2_), channel_id=1, source_target_pairs={{4,0},{8,4},{5,1},{9,5},{6,2},{10,6},{7,3},{11,7},{20,16},{24,20},... | collective-permute-start | bytes 2457608 | tf_op jit(solution)/shard_map/ppermute | solution.py:424
  42.8 39.1 %collective-permute-start.6 = (bf16[160,2176]{1,0:T(8,128)(2,1)}, bf16[160,2176]{1,0:T(8,128)(2,1)}, u32[]{:S(2)}, u32[]{:S(2)}) collective-permute-start(bf16[160,2176]{1,0:T(8,128)(2,1)} %other_part.4), channel_id=1, source_target_pairs={{4,0},{8,4},{12,8},{5,1},{9,5},{13,9},{6,2},{10,6},{14,10},{7,3},{... | collective-permute-start | bytes 2088968 | tf_op jit(solution)/shard_map/ppermute | solution.py:453
  44.1 37.8 %collective-permute-start.7 = (bf16[160,2176]{1,0:T(8,128)(2,1)}, bf16[160,2176]{1,0:T(8,128)(2,1)}, u32[]{:S(2)}, u32[]{:S(2)}) collective-permute-start(bf16[160,2176]{1,0:T(8,128)(2,1)} %other_part.5), channel_id=1, source_target_pairs={{0,4},{4,8},{8,12},{1,5},{5,9},{9,13},{2,6},{6,10},{10,14},{3,7},{... | collective-permute-start | bytes 2088968 | tf_op jit(solution)/shard_map/ppermute | solution.py:453
  67.9 14.0 %copy-start.3 = (bf16[160,2560]{1,0:T(8,128)(2,1)}, bf16[160,2560]{1,0:T(8,128)(2,1)S(1)}, u32[]{:S(2)}) copy-start(bf16[160,2560]{1,0:T(8,128)(2,1)S(1)} %collective-permute-done.2.refs_3_) | copy-start | bytes 2457604
  67.9 14.0 %copy-start.4 = (bf16[160,2560]{1,0:T(8,128)(2,1)}, bf16[160,2560]{1,0:T(8,128)(2,1)S(1)}, u32[]{:S(2)}) copy-start(bf16[160,2560]{1,0:T(8,128)(2,1)S(1)} %collective-permute-done.3.refs_4_) | copy-start | bytes 2457604
  67.9 30.6 %collective-permute-start.4 = (bf16[160,2560]{1,0:T(8,128)(2,1)S(1)}, bf16[160,2560]{1,0:T(8,128)(2,1)S(1)}, u32[]{:S(2)}, u32[]{:S(2)}) collective-permute-start(bf16[160,2560]{1,0:T(8,128)(2,1)S(1)} %collective-permute-done.2.refs_3_), channel_id=1, source_target_pairs={{8,12},{9,13},{10,14},{11,15},{24,28},{25,29},{26,30},{27,31}} | collective-permute-start | bytes 2457608 | tf_op jit(solution)/shard_map/ppermute | solution.py:424
  68.7 29.9 %collective-permute-start.5 = (bf16[160,2560]{1,0:T(8,128)(2,1)S(1)}, bf16[160,2560]{1,0:T(8,128)(2,1)S(1)}, u32[]{:S(2)}, u32[]{:S(2)}) collective-permute-start(bf16[160,2560]{1,0:T(8,128)(2,1)S(1)} %collective-permute-done.3.refs_4_), channel_id=1, source_target_pairs={{4,0},{5,1},{6,2},{7,3},{20,16},{21,17},{22,18},{23,19}} | collective-permute-start | bytes 2457608 | tf_op jit(solution)/shard_map/ppermute | solution.py:424
  98.4 41.1 %collective-permute-start.8 = (bf16[160,2176]{1,0:T(8,128)(2,1)}, bf16[160,2176]{1,0:T(8,128)(2,1)}, u32[]{:S(2)}, u32[]{:S(2)}) collective-permute-start(bf16[160,2176]{1,0:T(8,128)(2,1)} %other_part.6), channel_id=1, source_target_pairs={{8,0},{12,4},{0,8},{4,12},{9,1},{13,5},{1,9},{5,13},{10,2},{14,6},... | collective-permute-start | bytes 2088968 | tf_op jit(solution)/shard_map/ppermute | solution.py:453
  98.5 0.9 copy-start.5
  99.4 0.9 copy-start.6
  110.6 28.9 %collective-permute-start.9 = (bf16[160,2176]{1,0:T(8,128)(2,1)}, bf16[160,2176]{1,0:T(8,128)(2,1)S(1)}, u32[]{:S(2)}, u32[]{:S(2)}) collective-permute-start(bf16[160,2176]{1,0:T(8,128)(2,1)} %other_part.7), channel_id=1, source_target_pairs={{12,0},{0,12},{13,1},{1,13},{14,2},{2,14},{15,3},{3,15},{28,16},{1... | collective-permute-start | bytes 2088968 | tf_op jit(solution)/shard_map/ppermute | solution.py:453
  139.5 0.9 copy-start.7

commit v5 on v4

--- a/solution.py
+++ b/solution.py
@@ -15,12 +15,11 @@
 CAPP = 2
 GROUP = HEADS // KVH
 EMPTY = -1e30
-LINE = 8
 TILE = 256
 ONES = 16
 SCALE = 1.0 / math.sqrt(HD)
 EXP2_SCALE = SCALE * math.log2(math.e)
-VMEM_LIMIT = 60 * 1024 * 1024 + 256 * 1024
+VMEM_LIMIT = 63 * 1024 * 1024
 
 
 def fetch(pool_size, tables, request, stores, buffers, sems):
@@ -51,46 +50,55 @@
 
 
 def attend(
-    key_ref, value_ref, count, ready, fresh, new_rows, columns, turned, peaks, acc, log_type, put
+    key_ref,
+    value_ref,
+    count,
+    ready,
+    fresh,
+    new_rows,
+    columns,
+    scores,
+    weights,
+    peaks,
+    factors,
+    turned,
+    acc,
+    log_type,
+    put,
 ):
     kv_local, _, rows = columns.shape
 
     def visit(keys, values, seen):
-        for kv in range(kv_local):
+        def score(kv):
             turned[kv, :HD, :] = values[kv].T
-        tiles = [(kv, i) for kv in range(kv_local) for i in range(0, rows, TILE)]
-        blocks = {}
-        weights = {}
-        for step in range(len(tiles) + 2):
-            if step < len(tiles):
-                kv, i = tiles[step]
-                block = lax.dot_general(
-                    keys[kv],
-                    columns[kv, :, i : i + TILE],
-                    (((1,), (0,)), ((), ())),
-                    preferred_element_type=jnp.float32,
-                )
-                if seen is not None:
-                    block = jnp.where(seen(i), block, EMPTY)
-                blocks[step] = block
-            if step >= 2:
-                kv, i = tiles[step - 2]
+            block = lax.dot_general(
+                keys[kv], columns[kv], (((1,), (0,)), ((), ())), preferred_element_type=jnp.float32
+            )
+            if seen is not None:
+                block = jnp.where(seen, block, EMPTY)
+            scores[kv] = block
+
+        def weigh(kv):
+            for i in range(0, rows, TILE):
                 part = slice(i, i + TILE)
-                weight, factor = weights.pop(step - 2)
-                added = lax.dot_general(
-                    turned[kv], weight, (((1,), (0,)), ((), ())), preferred_element_type=jnp.float32
-                )
-                acc[kv, :, part] = acc[kv, :, part] * factor + added
-            if 1 <= step <= len(tiles):
-                kv, i = tiles[step - 1]
-                part = slice(i, i + TILE)
-                block = blocks.pop(step - 1)
                 before = peaks[kv, :, part]
+                block = scores[kv, :, part]
                 peak = jnp.maximum(before, jnp.max(block, axis=0, keepdims=True))
+                factors[kv, :, part] = jnp.exp2((before - peak) * EXP2_SCALE)
                 peaks[kv, :, part] = peak
-                factor = jnp.exp2((before - peak) * EXP2_SCALE)[0:1]
                 weight = jnp.exp2(block * EXP2_SCALE - peak[0:1] * EXP2_SCALE)
-                weights[step - 1] = (weight.astype(jnp.bfloat16), factor)
+                weights[kv, :, part] = weight.astype(jnp.bfloat16)
+
+        def mix(kv):
+            added = lax.dot_general(
+                turned[kv], weights[kv], (((1,), (0,)), ((), ())), preferred_element_type=jnp.float32
+            )
+            acc[kv] = acc[kv] * factors[kv, 0:1, :] + added
+
+        for step in range(kv_local + 2):
+            for offset, stage in ((0, score), (2, mix), (1, weigh)):
+                if 0 <= step - offset < kv_local:
+                    stage(step - offset)
 
     def lanes_of(ref):
         return [ref[:, kv * HD : (kv + 1) * HD] for kv in range(kv_local)]
@@ -101,11 +109,8 @@
     if fresh is not None:
         new_key_ref, new_value_ref = fresh
 
-        def seen(i):
-            shape = (new_key_ref.shape[0], TILE)
-            row = lax.rem(lax.broadcasted_iota(jnp.int32, (1, TILE), 1) + i, new_rows)
-            return lax.broadcasted_iota(jnp.int32, shape, 0) <= row
-
+        row = lax.rem(lax.broadcasted_iota(jnp.int32, (1, rows), 1), new_rows)
+        seen = lax.broadcasted_iota(jnp.int32, (new_key_ref.shape[0], rows), 0) <= row
         visit(lanes_of(new_key_ref), lanes_of(new_value_ref), seen)
 
     def visit_block(entry, carry):
@@ -207,40 +212,59 @@
     )
 
 
-def other_kernel(pool_size, offsets, *refs):
-    if offsets[0] is None:
-        wanted = [refs[0][0]]
+def other_kernel(pool_size, partners, *refs):
+    if partners is None:
+        request = refs[0][0]
+        choice = [None]
         refs = refs[1:]
     else:
-        wanted = [lax.axis_index("pool") + offset for offset in offsets]
+        me = lax.axis_index("pool")
+        inner = is_inner(me)
+        request = me ^ jnp.where(inner, partners[0], partners[1])
+        choice = [inner, jnp.logical_not(inner)]
     tables, refs = refs[:3], refs[3:]
-    payload_refs = refs[: len(offsets)]
+    payload_refs = refs[: len(choice)]
     store_keys, store_values, out_ref, key_buf, value_buf, query_rows, columns, *state = refs[
-        len(offsets) :
+        len(choice) :
     ]
-    *work, sems = state
-    there = [(x >= 0) & (x < pool_size) for x in wanted]
-    request = wanted[0]
-    for other, hit in zip(wanted[1:], there[1:]):
-        request = jnp.where(hit, other, request)
-
-    @pl.when(functools.reduce(jnp.logical_or, there))
-    def _():
-        count, ready = fetch(
-            pool_size, tables, request, (store_keys, store_values), (key_buf, value_buf), sems
-        )
-        new_rows = out_ref.shape[0]
-        width = out_ref.shape[1] - HD
-        for payload_ref, hit in zip(payload_refs, there):
-            pl.when(hit)(functools.partial(load_heads, payload_ref, query_rows, columns))
-
-        def put(head, out):
-            out_ref[:, head * HD : (head + 1) * HD] = out
-
-        tile = attend(
-            key_buf, value_buf, count, ready, None, new_rows, columns, *work, jnp.bfloat16, put
-        )
-        out_ref[:, width:] = split_lanes(tile, width // HD)
+    *work, query_buf, query_sem, sems = state
+    new_rows = out_ref.shape[0]
+    width = out_ref.shape[1] - HD
+
+    def query_copy(payload_ref):
+        return pltpu.make_async_copy(payload_ref.at[:, :width], query_buf, query_sem)
+
+    for payload_ref, hit in zip(payload_refs, choice):
+        if hit is None:
+            query_copy(payload_ref).start()
+        else:
+            pl.when(hit)(functools.partial(query_copy(payload_ref).start))
+    count, ready = fetch(
+        pool_size, tables, request, (store_keys, store_values), (key_buf, value_buf), sems
+    )
+    query_copy(payload_refs[0]).wait()
+    load_heads(query_buf, query_rows, columns)
+
+    def put(head, out):
+        out_ref[:, head * HD : (head + 1) * HD] = out
+
+    tile = attend(
+        key_buf, value_buf, count, ready, None, new_rows, columns, *work, jnp.bfloat16, put
+    )
+    out_ref[:, width:] = split_lanes(tile, width // HD)
+
+
+def is_inner(place):
+    return (place == 1) | (place == 2)
+
+
+def source_of(me, entry):
+    if isinstance(entry, int):
+        return jnp.bool_(True), jnp.int32(entry)
+    inner = is_inner(me)
+    masks = [0 if mask is None else mask for mask in entry]
+    there = jnp.where(inner, entry[0] is not None, entry[1] is not None)
+    return there, me ^ jnp.where(inner, masks[0], masks[1])
 
 
 def push_kernel(pool_size, entries, owner_ref, *refs):
@@ -254,10 +278,8 @@
     def copy(source, i, place):
         return pltpu.make_async_copy(source, outs[i].at[place], sems.at[i, place])
 
-    for (relative, request), payload_ref in zip(entries, payload_refs):
-        source = me + request if relative else jnp.int32(request)
-        there = (source >= 0) & (source < pool_size)
-        source = jnp.clip(source, 0, pool_size - 1)
+    for entry, payload_ref in zip(entries, payload_refs):
+        there, source = source_of(me, entry)
         rank = jnp.int32(0)
         for other in range(pool_size):
             rank += ((owner_ref[other] == me) & (other < source)).astype(jnp.int32)
@@ -293,14 +315,9 @@
     heads = width // HD
     logs = [log_ref[...]]
     me = lax.axis_index("pool")
-    for (offsets, source), part in zip(sources, parts):
-        if offsets:
-            wanted = [me + offset for offset in offsets]
-            there = functools.reduce(
-                jnp.logical_or, [(x >= 0) & (x < pool_size) for x in wanted]
-            )
-        else:
-            there = me != source
+    for source, part in zip(sources, parts):
+        there, request = source_of(me, source)
+        there = there & (request != me)
         tile = part[:, width:].astype(jnp.float32)
         whole = (
             tile + pltpu.roll(tile, HD - heads, 1) + pltpu.roll(tile, HD - 2 * heads, 1)
@@ -356,8 +373,11 @@
     work = [
         pltpu.VMEM((rows, HD), jnp.bfloat16),
         pltpu.VMEM((kv_local, HD, rows), jnp.bfloat16),
+        pltpu.VMEM((kv_local, block_len, rows), jnp.float32),
+        pltpu.VMEM((kv_local, block_len, rows), jnp.bfloat16),
+        pltpu.VMEM((kv_local, 8, rows), jnp.float32),
+        pltpu.VMEM((kv_local, 8, rows), jnp.float32),
         pltpu.VMEM((kv_local, HD + ONES, block_len), jnp.bfloat16),
-        pltpu.VMEM((kv_local, 8, rows), jnp.float32),
         pltpu.VMEM((kv_local, HD + ONES, rows), jnp.float32),
     ]
     sems = pltpu.SemaphoreType.DMA((2, capacity))
@@ -382,19 +402,21 @@
             name="own_part",
         )(*tables, payload, store_keys, store_values)
 
-    def other_part(offsets, held, *request):
+    def other_part(partners, held, *request, share=8):
         return pl.pallas_call(
-            functools.partial(other_kernel, pool_size, offsets),
-            in_specs=[smem_spec] * (3 + len(request)) + [vmem_spec] * len(held) + [hbm_spec] * 2,
+            functools.partial(other_kernel, pool_size, partners),
+            in_specs=[smem_spec] * (3 + len(request)) + [hbm_spec] * (len(held) + 2),
             out_specs=vmem_spec,
             scratch_shapes=[
                 *buffers,
                 *work,
+                pltpu.VMEM((new_rows, width), jnp.bfloat16),
+                pltpu.SemaphoreType.DMA,
                 sems,
             ],
             out_shape=jax.ShapeDtypeStruct((new_rows, width + HD), jnp.bfloat16),
             compiler_params=params,
-            cost_estimate=cost(0 if len(held) == 1 else 8),
+            cost_estimate=cost(share),
             name="other_part",
         )(*request, *tables, *held, store_keys, store_values)
 
@@ -412,59 +434,51 @@
         )(own, log, *parts)
         return out[0] if last else out
 
-    def inside(index):
-        return 0 <= index < pool_size
-
-    def forward(array, distance, first):
-        pairs = [
-            (i, i + distance)
-            for i in range(pool_size)
-            if inside(i + distance) and inside(i - first)
-        ]
-        return lax.ppermute(array, "pool", pairs)
-
     payload = jnp.concatenate([queries[0], new_keys[0], new_values[0]], axis=1)
     own_out, own_log = own_part(payload)
-    if pool_size <= LINE:
-        sources = []
-        parts = []
-        right, left = payload, payload
-        moved = [((True, 0), payload)]
-        done = [own_out, own_log]
-        for step in range(1, pool_size):
-            right = forward(right, 1, step - 1)
-            left = forward(left, -1, 1 - step)
-            right, left, done = lax.optimization_barrier((right, left, done))
-            if step == 1:
-                own_out, own_log = done
-            done = []
-            moved += [((True, -step), right), ((True, step), left)]
-            held_right, held_left = right, left
-            if step == 2:
-                held_right, held_left, parts = lax.optimization_barrier((right, left, parts))
-            if 2 * step < pool_size:
-                groups = [((-step,), (held_right,)), ((step,), (held_left,))]
-            else:
-                groups = [((-step, step), (held_right, held_left))]
-            for offsets, held in groups:
-                packed = other_part(offsets, held)
-                done.append(packed)
-                pairs = [(i, i + x) for x in offsets for i in range(pool_size) if inside(i + x)]
-                parts.append(lax.ppermute(packed, "pool", pairs))
-                sources.append((tuple(-x for x in offsets), None))
-        if len(parts) > 2:
-            own_out, own_log, done = lax.optimization_barrier((own_out, own_log, done))
-            own_out, own_log = combine(own_out, own_log, sources[:-2], parts[:-2], last=False)
-            sources, parts = sources[-2:], parts[-2:]
+    if pool_size == 4:
+        def send(array, *pairs):
+            return lax.ppermute(array, "pool", pairs)
+
+        near = send(payload, (0, 1), (1, 0), (2, 3), (3, 2))
+        middle = send(payload, (1, 2), (2, 1))
+        near, middle, own_out, own_log = lax.optimization_barrier((near, middle, own_out, own_log))
+        crossed = send(near, (1, 2), (2, 1))
+        outward = send(middle, (1, 0), (2, 3))
+        first = other_part((3, 1), (middle, near))
+        crossed, outward, first = lax.optimization_barrier((crossed, outward, first))
+        across = send(first, (1, 2), (2, 1))
+        inward = send(first, (0, 1), (3, 2))
+        far = send(crossed, (1, 0), (2, 3))
+        second = other_part((2, 2), (crossed, outward))
+        far, second = lax.optimization_barrier((far, second))
+        apart = send(second, (0, 2), (2, 0), (1, 3), (3, 1))
+        third = other_part((1, 3), (near, far), share=8)
+        ends = send(third, (0, 3), (3, 0))
+        back = send(third, (1, 0), (2, 3))
+        own_out, own_log, third = lax.optimization_barrier((own_out, own_log, third))
+        own_out, own_log = combine(
+            own_out, own_log, [(3, None), (1, None), (2, 2)], [across, inward, apart], last=False
+        )
+        sources = [(None, 1), (None, 3)]
+        parts = [back, ends]
+        moved = [
+            ((0, 0), payload),
+            ((1, 1), near),
+            ((3, None), middle),
+            ((2, None), crossed),
+            ((None, 2), outward),
+            ((None, 3), far),
+        ]
     else:
         gathered = lax.all_gather(payload, "pool", axis=0, tiled=False)
         packed = lax.map(
-            lambda pair: other_part((None,), (pair[0],), pair[1].reshape(1)),
+            lambda pair: other_part(None, (pair[0],), pair[1].reshape(1)),
             (gathered, jnp.arange(pool_size, dtype=jnp.int32)),
         )
         parts = lax.all_to_all(packed, "pool", split_axis=0, concat_axis=0, tiled=True)
-        sources = [(None, source) for source in range(pool_size)]
-        moved = [((False, source), gathered[source]) for source in range(pool_size)]
+        sources = list(range(pool_size))
+        moved = [(source, gathered[source]) for source in range(pool_size)]
 
     attended = combine(own_out, own_log, sources, parts)
     pushed_keys, pushed_values = pl.pallas_call(

time: 145 us -> 134 us (0.924)
  the two profiles are of different devices: /device:TPU:4 before, /device:TPU:0 now
where the time goes in v5:
time: 134 us; the launch traced here: 132 us
  Pallas kernels  58.8 us (44%)
  waiting for transfers between devices  45.4 us (34%)
  starting transfers between devices  25 us (19%)
    ppermute x10, waiting for transfers between devices, send(): return lax.ppermute(array, 'pool', pairs)  45.4 us
    pallas_call x3, Pallas kernels, other_part(): pl.pallas_call(functools.partial(other_kernel, pool_size, partners), in_s...  29.7 us
    ppermute x10, starting transfers between devices, send(): return lax.ppermute(array, 'pool', pairs)  25 us
    pallas_call x1, Pallas kernels, own_part(): pl.pallas_call(functools.partial(own_kernel, pool_size), in_specs=[smem_s...  13.7 us
    pallas_call x2, Pallas kernels, combine(): pl.pallas_call(functools.partial(combine_kernel, tuple(sources), pool_siz...  8.51 us
    pallas_call x1, Pallas kernels, shards(): pl.pallas_call(functools.partial(push_kernel, pool_size, tuple((entry for...  6.88 us
  transfers between devices with their start and end apart: 10, of which 5 were waited for; matrix products, arithmetic and copies ran while one was open for 0% of the time, Pallas kernels for 42%

profile of v5, /device:TPU:0, one launch (start us, length us, event | category | flops | bytes accessed | tf_op | source)
XLA Modules:
  0.0 132.0 jit_solution(8592256254892054938)
XLA Ops:
  0.6 1.2 pad_maximum_fusion.payload_ref.refs_0_
  1.9 0.0 copy-start
  1.9 3.1 %collective-permute-start = (bf16[160,2560]{1,0:T(8,128)(2,1)S(1)}, bf16[160,2560]{1,0:T(8,128)(2,1)}, u32[]{:S(2)}, u32[]{:S(2)}) collective-permute-start(bf16[160,2560]{1,0:T(8,128)(2,1)S(1)} %pad_maximum_fusion.payload_ref.refs_0_), channel_id=1, source_target_pairs={{0,4},{4,0},{8,12},{12,8},{1,5},{5,1},{9,13},{13,9},{2,6},{6,2},{1... | collective-permute-start | bytes 2457608 | tf_op jit(solution)/shard_map/ppermute | solution.py:441
  5.0 1.6 %collective-permute-start.1 = (bf16[160,2560]{1,0:T(8,128)(2,1)S(1)}, bf16[160,2560]{1,0:T(8,128)(2,1)}, u32[]{:S(2)}, u32[]{:S(2)}) collective-permute-start(bf16[160,2560]{1,0:T(8,128)(2,1)S(1)} %pad_maximum_fusion.payload_ref.refs_0_), channel_id=1, source_target_pairs={{4,8},{8,4},{5,9},{9,5},{6,10},{10,6},{7,11},{11,7},{20,24},{24,20... | collective-permute-start | bytes 2457608 | tf_op jit(solution)/shard_map/ppermute | solution.py:441
  6.5 13.7 %own_part.1 = (f32[160,2048]{1,0:T(8,128)}, f32[160,128]{1,0:T(8,128)}) custom-call(s32[4]{0:T(128)} %refs_0_.5, s32[4,32]{1,0:T(4,128)} %refs_1_.5, s32[4,32]{1,0:T(4,128)} %refs_2_.5, bf16[160,2560]{1,0:T(8,128)(2,1)} %copy-done, bf16[32,256,256]{2,1,0:T(8,128)(2,1)} %refs_5_.5, bf16[32,256,256]{2,1,0:T(8,128)(2,1)} %refs_6_.5), custom_call_target="tpu_custom_call" | custom-call | flops 5368709120 | bytes 1280 | tf_op jit(solution)/shard_map/own_part/pallas_call | solution.py:386
  20.3 3.0 %collective-permute-done.refs_4_.refs_3_.refs_1_ = bf16[160,2560]{1,0:T(8,128)(2,1)} collective-permute-done((bf16[160,2560]{1,0:T(8,128)(2,1)S(1)}, bf16[160,2560]{1,0:T(8,128)(2,1)}, u32[]{:S(2)}, u32[]{:S(2)}) %collective-permute-start) | collective-permute-done | bytes 819232 | tf_op jit(solution)/shard_map/ppermute | solution.py:441
  23.3 0.0 collective-permute-done.1.refs_3_.refs_2_
  23.3 0.7 collective-permute-start.2
  24.0 1.3 collective-permute-start.3
  25.3 9.9 %other_part.3 = bf16[160,2176]{1,0:T(8,128)(2,1)} custom-call(s32[4]{0:T(128)} %refs_0_.5, s32[4,32]{1,0:T(4,128)} %refs_1_.5, s32[4,32]{1,0:T(4,128)} %refs_2_.5, bf16[160,2560]{1,0:T(8,128)(2,1)} %collective-permute-done.1.refs_3_.refs_2_, bf16[160,2560]{1,0:T(8,128)(2,1)} %collective-permute-done.refs_4_.refs_3_.refs_1_, bf16[32,256,256]{2,1,0:T(8,128)(2,1)} %refs_5_.5, ...), custom_call_target="tpu_custom_call" | custom-call | flops 5368709120 | bytes 1280 | tf_op jit(solution)/shard_map/other_part/pallas_call | solution.py:406
  35.2 0.0 collective-permute-done.2.refs_3_
  35.2 0.0 copy-start.1
  35.2 14.9 %collective-permute-done.3.refs_4_ = bf16[160,2560]{1,0:T(8,128)(2,1)} collective-permute-done((bf16[160,2560]{1,0:T(8,128)(2,1)}, bf16[160,2560]{1,0:T(8,128)(2,1)}, u32[]{:S(2)}, u32[]{:S(2)}) %collective-permute-start.3) | collective-permute-done | bytes 819232 | tf_op jit(solution)/shard_map/ppermute | solution.py:441
  50.1 1.3 collective-permute-start.4
  51.4 1.5 %collective-permute-start.5 = (bf16[160,2176]{1,0:T(8,128)(2,1)}, bf16[160,2176]{1,0:T(8,128)(2,1)}, u32[]{:S(2)}, u32[]{:S(2)}) collective-permute-start(bf16[160,2176]{1,0:T(8,128)(2,1)} %other_part.3), channel_id=1, source_target_pairs={{4,8},{8,4},{5,9},{9,5},{6,10},{10,6},{7,11},{11,7},{20,24},{24,20... | collective-permute-start | bytes 2088968 | tf_op jit(solution)/shard_map/ppermute | solution.py:441
  52.9 7.3 %collective-permute-start.6 = (bf16[160,2176]{1,0:T(8,128)(2,1)}, bf16[160,2176]{1,0:T(8,128)(2,1)}, u32[]{:S(2)}, u32[]{:S(2)}) collective-permute-start(bf16[160,2176]{1,0:T(8,128)(2,1)} %other_part.3), channel_id=1, source_target_pairs={{0,4},{12,8},{1,5},{13,9},{2,6},{14,10},{3,7},{15,11},{16,20},{28,... | collective-permute-start | bytes 2088968 | tf_op jit(solution)/shard_map/ppermute | solution.py:441
  60.2 0.0 copy-done.1
  60.2 8.7 %other_part.4 = bf16[160,2176]{1,0:T(8,128)(2,1)} custom-call(s32[4]{0:T(128)} %refs_0_.5, s32[4,32]{1,0:T(4,128)} %refs_1_.5, s32[4,32]{1,0:T(4,128)} %refs_2_.5, bf16[160,2560]{1,0:T(8,128)(2,1)} %copy-done.1, bf16[160,2560]{1,0:T(8,128)(2,1)} %collective-permute-done.3.refs_4_, bf16[32,256,256]{2,1,0:T(8,128)(2,1)} %refs_5_.5, bf16[32,256,256]{2,1,0:T(8,128)(2,1)} %refs_6_.5), custom_call_target="tpu_custom_call" | custom-call | flops 5368709120 | bytes 1280 | tf_op jit(solution)/shard_map/other_part/pallas_call | solution.py:406
  68.9 1.0 collective-permute-done.4.refs_4_.refs_5_
  69.9 3.1 %collective-permute-start.7 = (bf16[160,2176]{1,0:T(8,128)(2,1)}, bf16[160,2176]{1,0:T(8,128)(2,1)}, u32[]{:S(2)}, u32[]{:S(2)}) collective-permute-start(bf16[160,2176]{1,0:T(8,128)(2,1)} %other_part.4), channel_id=1, source_target_pairs={{0,8},{8,0},{4,12},{12,4},{1,9},{9,1},{5,13},{13,5},{2,10},{10,2},... | collective-permute-start | bytes 2088968 | tf_op jit(solution)/shard_map/ppermute | solution.py:441
  73.0 11.1 %other_part.5 = bf16[160,2176]{1,0:T(8,128)(2,1)} custom-call(s32[4]{0:T(128)} %refs_0_.5, s32[4,32]{1,0:T(4,128)} %refs_1_.5, s32[4,32]{1,0:T(4,128)} %refs_2_.5, bf16[160,2560]{1,0:T(8,128)(2,1)} %collective-permute-done.refs_4_.refs_3_.refs_1_, bf16[160,2560]{1,0:T(8,128)(2,1)} %collective-permute-done.4.refs_4_.refs_5_, bf16[32,256,256]{2,1,0:T(8,128)(2,1)} %refs_5_.5, ...), custom_call_target="tpu_custom_call" | custom-call | flops 5368709120 | bytes 1280 | tf_op jit(solution)/shard_map/other_part/pallas_call | solution.py:406
  84.1 1.3 collective-permute-start.8
  85.4 3.9 %collective-permute-start.9 = (bf16[160,2176]{1,0:T(8,128)(2,1)}, bf16[160,2176]{1,0:T(8,128)(2,1)}, u32[]{:S(2)}, u32[]{:S(2)}) collective-permute-start(bf16[160,2176]{1,0:T(8,128)(2,1)} %other_part.5), channel_id=1, source_target_pairs={{0,12},{12,0},{1,13},{13,1},{2,14},{14,2},{3,15},{15,3},{16,28},{2... | collective-permute-start | bytes 2088968 | tf_op jit(solution)/shard_map/ppermute | solution.py:441
  89.3 6.9 %push.1 = (bf16[2,160,256]{2,1,0:T(8,128)(2,1)}, bf16[2,160,256]{2,1,0:T(8,128)(2,1)}) custom-call(s32[4]{0:T(128)} %owner_ref.1, bf16[160,2560]{1,0:T(8,128)(2,1)} %copy-done, bf16[160,2560]{1,0:T(8,128)(2,1)} %collective-permute-done.refs_4_.refs_3_.refs_1_, bf16[160,2560]{1,0:T(8,128)(2,1)} %collective-permute-done.1.refs_3_.refs_2_, ...), custom_call_target="tpu_custom_call" | custom-call | tf_op jit(solution)/shard_map/push/pallas_call | solution.py:484
  96.2 0.0 collective-permute-done.5.refs_0_
  96.2 0.0 collective-permute-done.6.refs_1_
  96.2 20.2 %collective-permute-done.7.refs_2_ = bf16[160,2176]{1,0:T(8,128)(2,1)} collective-permute-done((bf16[160,2176]{1,0:T(8,128)(2,1)}, bf16[160,2176]{1,0:T(8,128)(2,1)}, u32[]{:S(2)}, u32[]{:S(2)}) %collective-permute-start.7) | collective-permute-done | bytes 696352 | tf_op jit(solution)/shard_map/ppermute | solution.py:441
  116.4 4.7 %combine.2 = (f32[160,2048]{1,0:T(8,128)}, f32[160,128]{1,0:T(8,128)}) custom-call(f32[160,2048]{1,0:T(8,128)} %get-tuple-element.29.own_ref, f32[160,128]{1,0:T(8,128)} %get-tuple-element.30.log_ref, bf16[160,2176]{1,0:T(8,128)(2,1)} %collective-permute-done.5.refs_0_, bf16[160,2176]{1,0:T(8,128)(2,1)} %collective-permute-done.6.refs_1_, ...), custom_call_target="tpu_custom_call" | custom-call | tf_op jit(solution)/shard_map/combine/pallas_call | solution.py:427
  121.0 6.2 %collective-permute-done.8.refs_0_ = bf16[160,2176]{1,0:T(8,128)(2,1)S(1)} collective-permute-done((bf16[160,2176]{1,0:T(8,128)(2,1)}, bf16[160,2176]{1,0:T(8,128)(2,1)S(1)}, u32[]{:S(2)}, u32[]{:S(2)}) %collective-permute-start.8) | collective-permute-done | bytes 696352 | tf_op jit(solution)/shard_map/ppermute | solution.py:441
  127.3 0.0 collective-permute-done.9.refs_1_
  127.3 0.8 copy-done.2
  128.1 3.8 %combine.3 = bf16[160,2048]{1,0:T(8,128)(2,1)} custom-call(f32[160,2048]{1,0:T(8,128)} %get-tuple-element.33.own_ref, f32[160,128]{1,0:T(8,128)} %get-tuple-element.34.log_ref, bf16[160,2176]{1,0:T(8,128)(2,1)} %copy-done.2, bf16[160,2176]{1,0:T(8,128)(2,1)} %collective-permute-done.9.refs_1_), custom_call_target="tpu_custom_call" | custom-call | tf_op jit(solution)/shard_map/combine/pallas_call | solution.py:427
  (2 shorter events, 0.0 us)
Async XLA Ops:
  1.9 4.7 %copy-start = (bf16[160,2560]{1,0:T(8,128)(2,1)}, bf16[160,2560]{1,0:T(8,128)(2,1)S(1)}, u32[]{:S(2)}) copy-start(bf16[160,2560]{1,0:T(8,128)(2,1)S(1)} %pad_maximum_fusion.payload_ref.refs_0_) | copy-start | bytes 2457604
  1.9 21.4 %collective-permute-start = (bf16[160,2560]{1,0:T(8,128)(2,1)S(1)}, bf16[160,2560]{1,0:T(8,128)(2,1)}, u32[]{:S(2)}, u32[]{:S(2)}) collective-permute-start(bf16[160,2560]{1,0:T(8,128)(2,1)S(1)} %pad_maximum_fusion.payload_ref.refs_0_), channel_id=1, source_target_pairs={{0,4},{4,0},{8,12},{12,8},{1,5},{5,1},{9,13},{13,9},{2,6},{6,2},{1... | collective-permute-start | bytes 2457608 | tf_op jit(solution)/shard_map/ppermute | solution.py:441
  5.0 18.4 %collective-permute-start.1 = (bf16[160,2560]{1,0:T(8,128)(2,1)S(1)}, bf16[160,2560]{1,0:T(8,128)(2,1)}, u32[]{:S(2)}, u32[]{:S(2)}) collective-permute-start(bf16[160,2560]{1,0:T(8,128)(2,1)S(1)} %pad_maximum_fusion.payload_ref.refs_0_), channel_id=1, source_target_pairs={{4,8},{8,4},{5,9},{9,5},{6,10},{10,6},{7,11},{11,7},{20,24},{24,20... | collective-permute-start | bytes 2457608 | tf_op jit(solution)/shard_map/ppermute | solution.py:441
  23.3 11.9 %collective-permute-start.2 = (bf16[160,2560]{1,0:T(8,128)(2,1)}, bf16[160,2560]{1,0:T(8,128)(2,1)S(1)}, u32[]{:S(2)}, u32[]{:S(2)}) collective-permute-start(bf16[160,2560]{1,0:T(8,128)(2,1)} %collective-permute-done.refs_4_.refs_3_.refs_1_), channel_id=1, source_target_pairs={{4,8},{8,4},{5,9},{9,5},{6,10},{10,6},{7,11},{11,7},{20,24},{24,20... | collective-permute-start | bytes 2457608 | tf_op jit(solution)/shard_map/ppermute | solution.py:441
  24.0 26.0 %collective-permute-start.3 = (bf16[160,2560]{1,0:T(8,128)(2,1)}, bf16[160,2560]{1,0:T(8,128)(2,1)}, u32[]{:S(2)}, u32[]{:S(2)}) collective-permute-start(bf16[160,2560]{1,0:T(8,128)(2,1)} %collective-permute-done.1.refs_3_.refs_2_), channel_id=1, source_target_pairs={{4,0},{8,12},{5,1},{9,13},{6,2},{10,14},{7,3},{11,15},{20,16},{24,... | collective-permute-start | bytes 2457608 | tf_op jit(solution)/shard_map/ppermute | solution.py:441
  35.2 25.0 %copy-start.1 = (bf16[160,2560]{1,0:T(8,128)(2,1)}, bf16[160,2560]{1,0:T(8,128)(2,1)S(1)}, u32[]{:S(2)}) copy-start(bf16[160,2560]{1,0:T(8,128)(2,1)S(1)} %collective-permute-done.2.refs_3_) | copy-start | bytes 2457604
  50.1 19.9 %collective-permute-start.4 = (bf16[160,2560]{1,0:T(8,128)(2,1)S(1)}, bf16[160,2560]{1,0:T(8,128)(2,1)}, u32[]{:S(2)}, u32[]{:S(2)}) collective-permute-start(bf16[160,2560]{1,0:T(8,128)(2,1)S(1)} %collective-permute-done.2.refs_3_), channel_id=1, source_target_pairs={{4,0},{8,12},{5,1},{9,13},{6,2},{10,14},{7,3},{11,15},{20,16},{24,... | collective-permute-start | bytes 2457608 | tf_op jit(solution)/shard_map/ppermute | solution.py:441
  51.4 44.8 %collective-permute-start.5 = (bf16[160,2176]{1,0:T(8,128)(2,1)}, bf16[160,2176]{1,0:T(8,128)(2,1)}, u32[]{:S(2)}, u32[]{:S(2)}) collective-permute-start(bf16[160,2176]{1,0:T(8,128)(2,1)} %other_part.3), channel_id=1, source_target_pairs={{4,8},{8,4},{5,9},{9,5},{6,10},{10,6},{7,11},{11,7},{20,24},{24,20... | collective-permute-start | bytes 2088968 | tf_op jit(solution)/shard_map/ppermute | solution.py:441
  52.9 43.3 %collective-permute-start.6 = (bf16[160,2176]{1,0:T(8,128)(2,1)}, bf16[160,2176]{1,0:T(8,128)(2,1)}, u32[]{:S(2)}, u32[]{:S(2)}) collective-permute-start(bf16[160,2176]{1,0:T(8,128)(2,1)} %other_part.3), channel_id=1, source_target_pairs={{0,4},{12,8},{1,5},{13,9},{2,6},{14,10},{3,7},{15,11},{16,20},{28,... | collective-permute-start | bytes 2088968 | tf_op jit(solution)/shard_map/ppermute | solution.py:441
  69.9 46.4 %collective-permute-start.7 = (bf16[160,2176]{1,0:T(8,128)(2,1)}, bf16[160,2176]{1,0:T(8,128)(2,1)}, u32[]{:S(2)}, u32[]{:S(2)}) collective-permute-start(bf16[160,2176]{1,0:T(8,128)(2,1)} %other_part.4), channel_id=1, source_target_pairs={{0,8},{8,0},{4,12},{12,4},{1,9},{9,1},{5,13},{13,5},{2,10},{10,2},... | collective-permute-start | bytes 2088968 | tf_op jit(solution)/shard_map/ppermute | solution.py:441
  84.1 43.1 %collective-permute-start.8 = (bf16[160,2176]{1,0:T(8,128)(2,1)}, bf16[160,2176]{1,0:T(8,128)(2,1)S(1)}, u32[]{:S(2)}, u32[]{:S(2)}) collective-permute-start(bf16[160,2176]{1,0:T(8,128)(2,1)} %other_part.5), channel_id=1, source_target_pairs={{4,0},{8,12},{5,1},{9,13},{6,2},{10,14},{7,3},{11,15},{20,16},{24,... | collective-permute-start | bytes 2088968 | tf_op jit(solution)/shard_map/ppermute | solution.py:441
  85.4 41.9 %collective-permute-start.9 = (bf16[160,2176]{1,0:T(8,128)(2,1)}, bf16[160,2176]{1,0:T(8,128)(2,1)}, u32[]{:S(2)}, u32[]{:S(2)}) collective-permute-start(bf16[160,2176]{1,0:T(8,128)(2,1)} %other_part.5), channel_id=1, source_target_pairs={{0,12},{12,0},{1,13},{13,1},{2,14},{14,2},{3,15},{15,3},{16,28},{2... | collective-permute-start | bytes 2088968 | tf_op jit(solution)/shard_map/ppermute | solution.py:441
  127.3 0.9 copy-start.2

commit v6 on v5

--- a/solution.py
+++ b/solution.py
@@ -17,6 +17,7 @@
 EMPTY = -1e30
 TILE = 256
 ONES = 16
+MERGE_STEPS = 5
 SCALE = 1.0 / math.sqrt(HD)
 EXP2_SCALE = SCALE * math.log2(math.e)
 VMEM_LIMIT = 63 * 1024 * 1024
@@ -269,14 +270,19 @@
 
 def push_kernel(pool_size, entries, owner_ref, *refs):
     payload_refs = refs[: len(entries)]
-    key_out, value_out, zeros, sems = refs[len(entries) :]
+    key_out, value_out, sems = refs[len(entries) :]
     outs = (key_out, value_out)
-    new_rows, kv_width = zeros.shape
+    kv_width = key_out.shape[2]
     me = lax.axis_index("pool")
-    zeros[...] = jnp.zeros(zeros.shape, jnp.bfloat16)
-
-    def copy(source, i, place):
-        return pltpu.make_async_copy(source, outs[i].at[place], sems.at[i, place])
+    total = jnp.int32(0)
+    for other in range(pool_size):
+        total += (owner_ref[other] == me).astype(jnp.int32)
+
+    def copy(payload_ref, i, place):
+        start = payload_ref.shape[1] - (2 - i) * kv_width
+        return pltpu.make_async_copy(
+            payload_ref.at[:, start : start + kv_width], outs[i].at[place], sems.at[i, place]
+        )
 
     for entry, payload_ref in zip(entries, payload_refs):
         there, source = source_of(me, entry)
@@ -284,28 +290,24 @@
         for other in range(pool_size):
             rank += ((owner_ref[other] == me) & (other < source)).astype(jnp.int32)
         hit = there & (owner_ref[source] == me)
-        width = payload_ref.shape[1] - 2 * kv_width
         for place in range(CAPP):
 
             @pl.when(hit & (rank == place))
             def _():
                 for i in range(2):
-                    start = width + i * kv_width
-                    copy(payload_ref.at[:, start : start + kv_width], i, place).start()
-
-    total = jnp.int32(0)
-    for other in range(pool_size):
-        total += (owner_ref[other] == me).astype(jnp.int32)
+                    copy(payload_ref, i, place).start()
+
     for place in range(CAPP):
 
         @pl.when(total <= place)
         def _():
+            for out in outs:
+                out[place] = jnp.zeros(out.shape[1:], jnp.bfloat16)
+
+        @pl.when(total > place)
+        def _():
             for i in range(2):
-                copy(zeros, i, place).start()
-
-    for place in range(CAPP):
-        for i in range(2):
-            copy(zeros, i, place).wait()
+                copy(payload_refs[0], i, place).wait()
 
 
 def combine_kernel(sources, pool_size, out_ref_count, own_ref, log_ref, *refs):
@@ -424,14 +426,21 @@
         out_shape = [jax.ShapeDtypeStruct((new_rows, width), jnp.bfloat16 if last else jnp.float32)]
         if not last:
             out_shape.append(jax.ShapeDtypeStruct((new_rows, HD), jnp.float32))
+        arrays = [own, log, *parts]
+
+        def by_rows(array):
+            return pl.BlockSpec((new_rows // MERGE_STEPS, array.shape[1]), lambda i: (i, 0))
+
         out = pl.pallas_call(
             functools.partial(combine_kernel, tuple(sources), pool_size, len(out_shape)),
-            in_specs=[vmem_spec] * (2 + len(sources)),
-            out_specs=[vmem_spec] * len(out_shape),
+            grid=(MERGE_STEPS,),
+            in_specs=[by_rows(array) for array in arrays],
+            out_specs=[by_rows(array) for array in out_shape],
             out_shape=out_shape,
             compiler_params=params,
+            cost_estimate=cost(0 if last else 32),
             name="combine",
-        )(own, log, *parts)
+        )(*arrays)
         return out[0] if last else out
 
     payload = jnp.concatenate([queries[0], new_keys[0], new_values[0]], axis=1)
@@ -442,24 +451,28 @@
 
         near = send(payload, (0, 1), (1, 0), (2, 3), (3, 2))
         middle = send(payload, (1, 2), (2, 1))
-        near, middle, own_out, own_log = lax.optimization_barrier((near, middle, own_out, own_log))
-        crossed = send(near, (1, 2), (2, 1))
+        near, middle, own_out, own_log, payload = lax.optimization_barrier(
+            (near, middle, own_out, own_log, payload)
+        )
+        crossed = send(payload, (0, 2), (3, 1))
         outward = send(middle, (1, 0), (2, 3))
         first = other_part((3, 1), (middle, near))
         crossed, outward, first = lax.optimization_barrier((crossed, outward, first))
         across = send(first, (1, 2), (2, 1))
         inward = send(first, (0, 1), (3, 2))
         far = send(crossed, (1, 0), (2, 3))
-        second = other_part((2, 2), (crossed, outward))
-        far, second = lax.optimization_barrier((far, second))
+        second = other_part((2, 2), (crossed, outward), share=0)
+        near, second = lax.optimization_barrier((near, second))
         apart = send(second, (0, 2), (2, 0), (1, 3), (3, 1))
+        own_out, own_log = combine(
+            own_out, own_log, [(3, None), (1, None)], [across, inward], last=False
+        )
+        near, own_out, own_log = lax.optimization_barrier((near, own_out, own_log))
         third = other_part((1, 3), (near, far), share=8)
         ends = send(third, (0, 3), (3, 0))
         back = send(third, (1, 0), (2, 3))
         own_out, own_log, third = lax.optimization_barrier((own_out, own_log, third))
-        own_out, own_log = combine(
-            own_out, own_log, [(3, None), (1, None), (2, 2)], [across, inward, apart], last=False
-        )
+        own_out, own_log = combine(own_out, own_log, [(2, 2)], [apart], last=False)
         sources = [(None, 1), (None, 3)]
         parts = [back, ends]
         moved = [
@@ -484,11 +497,8 @@
     pushed_keys, pushed_values = pl.pallas_call(
         functools.partial(push_kernel, pool_size, tuple(entry for entry, _ in moved)),
         in_specs=[smem_spec] + [hbm_spec] * len(moved),
-        out_specs=[hbm_spec] * 2,
-        scratch_shapes=[
-            pltpu.VMEM((new_rows, kv_width), jnp.bfloat16),
-            pltpu.SemaphoreType.DMA((2, CAPP)),
-        ],
+        out_specs=[vmem_spec] * 2,
+        scratch_shapes=[pltpu.SemaphoreType.DMA((2, CAPP))],
         out_shape=[jax.ShapeDtypeStruct((CAPP, new_rows, kv_width), jnp.bfloat16)] * 2,
         compiler_params=params,
         name="push",

time: 134 us -> 138 us (1.030); the launches traced: 132 us -> 138 us
  starting transfers between devices: 25 us -> 37.3 us
  waiting for transfers between devices: 45.4 us -> 36 us
  Pallas kernels: 58.8 us -> 61.6 us
    ppermute x10, starting transfers between devices: 25 us -> 37.3 us  [send(): return lax.ppermute(array, 'pool', pairs)]
    ppermute x10, waiting for transfers between devices: 45.4 us -> 36 us  [send(): return lax.ppermute(array, 'pool', pairs)]
    pallas_call x2 -> x3, Pallas kernels: 8.51 us -> 15.5 us  [combine(): pl.pallas_call(functools.partial(combine_kernel, tuple(sources), pool_siz...]
    pallas_call x1, Pallas kernels: 6.88 us -> 1.53 us  [shards(): pl.pallas_call(functools.partial(push_kernel, pool_size, tuple((entry for...]
    pallas_call x3, Pallas kernels: 29.7 us -> 32 us  [other_part(): pl.pallas_call(functools.partial(other_kernel, pool_size, partners), in_s...]
  transfers between devices with their start and end apart: 10 -> 10, of which waited for: 5 -> 5; matrix products, arithmetic and copies ran while one was open for 0% -> 0% of each run, Pallas kernels for 42% -> 41%
where the time goes in v6:
time: 138 us
  Pallas kernels  61.6 us (45%)
  starting transfers between devices  37.3 us (27%)
  waiting for transfers between devices  36 us (26%)
    ppermute x10, starting transfers between devices, send(): return lax.ppermute(array, 'pool', pairs)  37.3 us
    ppermute x10, waiting for transfers between devices, send(): return lax.ppermute(array, 'pool', pairs)  36 us
    pallas_call x3, Pallas kernels, other_part(): pl.pallas_call(functools.partial(other_kernel, pool_size, partners), in_s...  32 us
    pallas_call x3, Pallas kernels, combine(): pl.pallas_call(functools.partial(combine_kernel, tuple(sources), pool_siz...  15.5 us
    pallas_call x1, Pallas kernels, own_part(): pl.pallas_call(functools.partial(own_kernel, pool_size), in_specs=[smem_s...  12.6 us
  transfers between devices with their start and end apart: 10, of which 5 were waited for; matrix products, arithmetic and copies ran while one was open for 0% of the time, Pallas kernels for 41%

profile of v6, /device:TPU:0, one launch (start us, length us, event | category | flops | bytes accessed | tf_op | source)
XLA Modules:
  0.0 137.7 jit_solution(11130129323278363211)
XLA Ops:
  0.6 1.2 pad_maximum_fusion.payload_ref.refs_0_
  1.9 0.0 copy-start.1
  1.9 3.1 %collective-permute-start = (bf16[160,2560]{1,0:T(8,128)(2,1)S(1)}, bf16[160,2560]{1,0:T(8,128)(2,1)}, u32[]{:S(2)}, u32[]{:S(2)}) collective-permute-start(bf16[160,2560]{1,0:T(8,128)(2,1)S(1)} %pad_maximum_fusion.payload_ref.refs_0_), channel_id=1, source_target_pairs={{0,4},{4,0},{8,12},{12,8},{1,5},{5,1},{9,13},{13,9},{2,6},{6,2},{1... | collective-permute-start | bytes 2457608 | tf_op jit(solution)/shard_map/ppermute | solution.py:450
  5.0 1.5 %collective-permute-start.1 = (bf16[160,2560]{1,0:T(8,128)(2,1)S(1)}, bf16[160,2560]{1,0:T(8,128)(2,1)}, u32[]{:S(2)}, u32[]{:S(2)}) collective-permute-start(bf16[160,2560]{1,0:T(8,128)(2,1)S(1)} %pad_maximum_fusion.payload_ref.refs_0_), channel_id=1, source_target_pairs={{4,8},{8,4},{5,9},{9,5},{6,10},{10,6},{7,11},{11,7},{20,24},{24,20... | collective-permute-start | bytes 2457608 | tf_op jit(solution)/shard_map/ppermute | solution.py:450
  6.5 12.6 %own_part.1 = (f32[160,2048]{1,0:T(8,128)}, f32[160,128]{1,0:T(8,128)}) custom-call(s32[4]{0:T(128)} %refs_0_.5, s32[4,32]{1,0:T(4,128)} %refs_1_.5, s32[4,32]{1,0:T(4,128)} %refs_2_.5, bf16[160,2560]{1,0:T(8,128)(2,1)} %copy-done.1, bf16[32,256,256]{2,1,0:T(8,128)(2,1)} %refs_5_.5, bf16[32,256,256]{2,1,0:T(8,128)(2,1)} %refs_6_.5), custom_call_target="tpu_custom_call" | custom-call | flops 5368709120 | bytes 1280 | tf_op jit(solution)/shard_map/own_part/pallas_call | solution.py:388
  19.1 4.2 %collective-permute-done.refs_4_.refs_3_.refs_1_ = bf16[160,2560]{1,0:T(8,128)(2,1)} collective-permute-done((bf16[160,2560]{1,0:T(8,128)(2,1)S(1)}, bf16[160,2560]{1,0:T(8,128)(2,1)}, u32[]{:S(2)}, u32[]{:S(2)}) %collective-permute-start) | collective-permute-done | bytes 819232 | tf_op jit(solution)/shard_map/ppermute | solution.py:450
  23.3 0.0 collective-permute-done.1.refs_3_.refs_2_
  23.3 1.3 collective-permute-start.3
  24.6 8.8 %collective-permute-start.2 = (bf16[160,2560]{1,0:T(8,128)(2,1)}, bf16[160,2560]{1,0:T(8,128)(2,1)}, u32[]{:S(2)}, u32[]{:S(2)}) collective-permute-start(bf16[160,2560]{1,0:T(8,128)(2,1)} %copy-done.1), channel_id=1, source_target_pairs={{0,8},{12,4},{1,9},{13,5},{2,10},{14,6},{3,11},{15,7},{16,24},{28,... | collective-permute-start | bytes 2457608 | tf_op jit(solution)/shard_map/ppermute | solution.py:450
  33.4 13.4 %other_part.3 = bf16[160,2176]{1,0:T(8,128)(2,1)} custom-call(s32[4]{0:T(128)} %refs_0_.5, s32[4,32]{1,0:T(4,128)} %refs_1_.5, s32[4,32]{1,0:T(4,128)} %refs_2_.5, bf16[160,2560]{1,0:T(8,128)(2,1)} %collective-permute-done.1.refs_3_.refs_2_, bf16[160,2560]{1,0:T(8,128)(2,1)} %collective-permute-done.refs_4_.refs_3_.refs_1_, bf16[32,256,256]{2,1,0:T(8,128)(2,1)} %refs_5_.5, ...), custom_call_target="tpu_custom_call" | custom-call | flops 5368709120 | bytes 1280 | tf_op jit(solution)/shard_map/other_part/pallas_call | solution.py:408
  46.8 0.1 collective-permute-done.3.refs_4_
  46.9 2.2 %collective-permute-done.2.refs_3_ = bf16[160,2560]{1,0:T(8,128)(2,1)} collective-permute-done((bf16[160,2560]{1,0:T(8,128)(2,1)}, bf16[160,2560]{1,0:T(8,128)(2,1)}, u32[]{:S(2)}, u32[]{:S(2)}) %collective-permute-start.2) | collective-permute-done | bytes 819232 | tf_op jit(solution)/shard_map/ppermute | solution.py:450
  49.1 1.6 %collective-permute-start.4 = (bf16[160,2176]{1,0:T(8,128)(2,1)}, bf16[160,2176]{1,0:T(8,128)(2,1)}, u32[]{:S(2)}, u32[]{:S(2)}) collective-permute-start(bf16[160,2176]{1,0:T(8,128)(2,1)} %other_part.3), channel_id=1, source_target_pairs={{4,8},{8,4},{5,9},{9,5},{6,10},{10,6},{7,11},{11,7},{20,24},{24,20... | collective-permute-start | bytes 2088968 | tf_op jit(solution)/shard_map/ppermute | solution.py:450
  50.7 7.1 %collective-permute-start.5 = (bf16[160,2176]{1,0:T(8,128)(2,1)}, bf16[160,2176]{1,0:T(8,128)(2,1)}, u32[]{:S(2)}, u32[]{:S(2)}) collective-permute-start(bf16[160,2176]{1,0:T(8,128)(2,1)} %other_part.3), channel_id=1, source_target_pairs={{0,4},{12,8},{1,5},{13,9},{2,6},{14,10},{3,7},{15,11},{16,20},{28,... | collective-permute-start | bytes 2088968 | tf_op jit(solution)/shard_map/ppermute | solution.py:450
  57.8 1.3 collective-permute-start.6
  59.1 0.0 copy-done
  59.1 8.7 %other_part.4 = bf16[160,2176]{1,0:T(8,128)(2,1)} custom-call(s32[4]{0:T(128)} %refs_0_.5, s32[4,32]{1,0:T(4,128)} %refs_1_.5, s32[4,32]{1,0:T(4,128)} %refs_2_.5, bf16[160,2560]{1,0:T(8,128)(2,1)} %collective-permute-done.2.refs_3_, bf16[160,2560]{1,0:T(8,128)(2,1)} %copy-done, bf16[32,256,256]{2,1,0:T(8,128)(2,1)} %refs_5_.5, bf16[32,256,256]{2,1,0:T(8,128)(2,1)} %refs_6_.5), custom_call_target="tpu_custom_call" | custom-call | bytes 1280 | tf_op jit(solution)/shard_map/other_part/pallas_call | solution.py:408
  67.8 6.0 %collective-permute-start.7 = (bf16[160,2176]{1,0:T(8,128)(2,1)}, bf16[160,2176]{1,0:T(8,128)(2,1)}, u32[]{:S(2)}, u32[]{:S(2)}) collective-permute-start(bf16[160,2176]{1,0:T(8,128)(2,1)} %other_part.4), channel_id=1, source_target_pairs={{0,8},{8,0},{4,12},{12,4},{1,9},{9,1},{5,13},{13,5},{2,10},{10,2},... | collective-permute-start | bytes 2088968 | tf_op jit(solution)/shard_map/ppermute | solution.py:450
  73.7 0.0 collective-permute-done.4.refs_0_
  73.7 0.0 collective-permute-done.5.refs_1_
  73.7 5.4 %combine.3 = (f32[160,2048]{1,0:T(8,128)}, f32[160,128]{1,0:T(8,128)}) custom-call(f32[160,2048]{1,0:T(8,128)} %get-tuple-element.34.own_ref, f32[160,128]{1,0:T(8,128)} %get-tuple-element.35.log_ref, bf16[160,2176]{1,0:T(8,128)(2,1)} %collective-permute-done.4.refs_0_, bf16[160,2176]{1,0:T(8,128)(2,1)} %collective-permute-done.5.refs_1_), custom_call_target="tpu_custom_call" | custom-call | flops 21474836480 | bytes 1280 | tf_op jit(solution)/shard_map/combine/pallas_call | solution.py:434
  79.1 0.0 collective-permute-done.6.refs_4_.refs_5_
  79.1 9.9 %other_part.5 = bf16[160,2176]{1,0:T(8,128)(2,1)} custom-call(s32[4]{0:T(128)} %refs_0_.5, s32[4,32]{1,0:T(4,128)} %refs_1_.5, s32[4,32]{1,0:T(4,128)} %refs_2_.5, bf16[160,2560]{1,0:T(8,128)(2,1)} %collective-permute-done.refs_4_.refs_3_.refs_1_, bf16[160,2560]{1,0:T(8,128)(2,1)} %collective-permute-done.6.refs_4_.refs_5_, bf16[32,256,256]{2,1,0:T(8,128)(2,1)} %refs_5_.5, ...), custom_call_target="tpu_custom_call" | custom-call | flops 5368709120 | bytes 1280 | tf_op jit(solution)/shard_map/other_part/pallas_call | solution.py:408
  89.0 1.3 collective-permute-start.8
  90.3 5.4 %collective-permute-start.9 = (bf16[160,2176]{1,0:T(8,128)(2,1)}, bf16[160,2176]{1,0:T(8,128)(2,1)}, u32[]{:S(2)}, u32[]{:S(2)}) collective-permute-start(bf16[160,2176]{1,0:T(8,128)(2,1)} %other_part.5), channel_id=1, source_target_pairs={{0,12},{12,0},{1,13},{13,1},{2,14},{14,2},{3,15},{15,3},{16,28},{2... | collective-permute-start | bytes 2088968 | tf_op jit(solution)/shard_map/ppermute | solution.py:450
  95.7 21.3 %collective-permute-done.7.refs_0_ = bf16[160,2176]{1,0:T(8,128)(2,1)} collective-permute-done((bf16[160,2176]{1,0:T(8,128)(2,1)}, bf16[160,2176]{1,0:T(8,128)(2,1)}, u32[]{:S(2)}, u32[]{:S(2)}) %collective-permute-start.7) | collective-permute-done | bytes 696352 | tf_op jit(solution)/shard_map/ppermute | solution.py:450
  117.0 5.0 %combine.4 = (f32[160,2048]{1,0:T(8,128)}, f32[160,128]{1,0:T(8,128)}) custom-call(f32[160,2048]{1,0:T(8,128)} %get-tuple-element.42.own_ref, f32[160,128]{1,0:T(8,128)} %get-tuple-element.43.log_ref, bf16[160,2176]{1,0:T(8,128)(2,1)} %collective-permute-done.7.refs_0_), custom_call_target="tpu_custom_call" | custom-call | flops 21474836480 | bytes 1280 | tf_op jit(solution)/shard_map/combine/pallas_call | solution.py:434
  121.9 1.5 %push.1 = (bf16[2,160,256]{2,1,0:T(8,128)(2,1)}, bf16[2,160,256]{2,1,0:T(8,128)(2,1)}) custom-call(s32[4]{0:T(128)} %owner_ref.1, bf16[160,2560]{1,0:T(8,128)(2,1)} %copy-done.1, bf16[160,2560]{1,0:T(8,128)(2,1)} %collective-permute-done.refs_4_.refs_3_.refs_1_, bf16[160,2560]{1,0:T(8,128)(2,1)} %collective-permute-done.1.refs_3_.refs_2_, ...), custom_call_target="tpu_custom_call" | custom-call | tf_op jit(solution)/shard_map/push/pallas_call | solution.py:497
  123.5 8.2 %collective-permute-done.8.refs_0_ = bf16[160,2176]{1,0:T(8,128)(2,1)S(1)} collective-permute-done((bf16[160,2176]{1,0:T(8,128)(2,1)}, bf16[160,2176]{1,0:T(8,128)(2,1)S(1)}, u32[]{:S(2)}, u32[]{:S(2)}) %collective-permute-start.8) | collective-permute-done | bytes 696352 | tf_op jit(solution)/shard_map/ppermute | solution.py:450
  131.7 0.0 collective-permute-done.9.refs_1_
  131.7 0.9 copy-done.2
  132.5 5.2 %combine.5 = bf16[160,2048]{1,0:T(8,128)(2,1)} custom-call(f32[160,2048]{1,0:T(8,128)} %get-tuple-element.45.own_ref, f32[160,128]{1,0:T(8,128)} %get-tuple-element.46.log_ref, bf16[160,2176]{1,0:T(8,128)(2,1)} %copy-done.2, bf16[160,2176]{1,0:T(8,128)(2,1)} %collective-permute-done.9.refs_1_), custom_call_target="tpu_custom_call" | custom-call | bytes 1280 | tf_op jit(solution)/shard_map/combine/pallas_call | solution.py:434
  (3 shorter events, 0.0 us)
Async XLA Ops:
  1.9 4.7 %copy-start.1 = (bf16[160,2560]{1,0:T(8,128)(2,1)}, bf16[160,2560]{1,0:T(8,128)(2,1)S(1)}, u32[]{:S(2)}) copy-start(bf16[160,2560]{1,0:T(8,128)(2,1)S(1)} %pad_maximum_fusion.payload_ref.refs_0_) | copy-start | bytes 2457604
  1.9 21.4 %collective-permute-start = (bf16[160,2560]{1,0:T(8,128)(2,1)S(1)}, bf16[160,2560]{1,0:T(8,128)(2,1)}, u32[]{:S(2)}, u32[]{:S(2)}) collective-permute-start(bf16[160,2560]{1,0:T(8,128)(2,1)S(1)} %pad_maximum_fusion.payload_ref.refs_0_), channel_id=1, source_target_pairs={{0,4},{4,0},{8,12},{12,8},{1,5},{5,1},{9,13},{13,9},{2,6},{6,2},{1... | collective-permute-start | bytes 2457608 | tf_op jit(solution)/shard_map/ppermute | solution.py:450
  5.0 18.4 %collective-permute-start.1 = (bf16[160,2560]{1,0:T(8,128)(2,1)S(1)}, bf16[160,2560]{1,0:T(8,128)(2,1)}, u32[]{:S(2)}, u32[]{:S(2)}) collective-permute-start(bf16[160,2560]{1,0:T(8,128)(2,1)S(1)} %pad_maximum_fusion.payload_ref.refs_0_), channel_id=1, source_target_pairs={{4,8},{8,4},{5,9},{9,5},{6,10},{10,6},{7,11},{11,7},{20,24},{24,20... | collective-permute-start | bytes 2457608 | tf_op jit(solution)/shard_map/ppermute | solution.py:450
  23.3 23.6 %collective-permute-start.3 = (bf16[160,2560]{1,0:T(8,128)(2,1)}, bf16[160,2560]{1,0:T(8,128)(2,1)S(1)}, u32[]{:S(2)}, u32[]{:S(2)}) collective-permute-start(bf16[160,2560]{1,0:T(8,128)(2,1)} %collective-permute-done.1.refs_3_.refs_2_), channel_id=1, source_target_pairs={{4,0},{8,12},{5,1},{9,13},{6,2},{10,14},{7,3},{11,15},{20,16},{24,... | collective-permute-start | bytes 2457608 | tf_op jit(solution)/shard_map/ppermute | solution.py:450
  24.6 24.5 %collective-permute-start.2 = (bf16[160,2560]{1,0:T(8,128)(2,1)}, bf16[160,2560]{1,0:T(8,128)(2,1)}, u32[]{:S(2)}, u32[]{:S(2)}) collective-permute-start(bf16[160,2560]{1,0:T(8,128)(2,1)} %copy-done.1), channel_id=1, source_target_pairs={{0,8},{12,4},{1,9},{13,5},{2,10},{14,6},{3,11},{15,7},{16,24},{28,... | collective-permute-start | bytes 2457608 | tf_op jit(solution)/shard_map/ppermute | solution.py:450
  46.9 12.1 %copy-start = (bf16[160,2560]{1,0:T(8,128)(2,1)}, bf16[160,2560]{1,0:T(8,128)(2,1)S(1)}, u32[]{:S(2)}) copy-start(bf16[160,2560]{1,0:T(8,128)(2,1)S(1)} %collective-permute-done.3.refs_4_) | copy-start | bytes 2457604
  49.1 24.6 %collective-permute-start.4 = (bf16[160,2176]{1,0:T(8,128)(2,1)}, bf16[160,2176]{1,0:T(8,128)(2,1)}, u32[]{:S(2)}, u32[]{:S(2)}) collective-permute-start(bf16[160,2176]{1,0:T(8,128)(2,1)} %other_part.3), channel_id=1, source_target_pairs={{4,8},{8,4},{5,9},{9,5},{6,10},{10,6},{7,11},{11,7},{20,24},{24,20... | collective-permute-start | bytes 2088968 | tf_op jit(solution)/shard_map/ppermute | solution.py:450
  50.7 23.1 %collective-permute-start.5 = (bf16[160,2176]{1,0:T(8,128)(2,1)}, bf16[160,2176]{1,0:T(8,128)(2,1)}, u32[]{:S(2)}, u32[]{:S(2)}) collective-permute-start(bf16[160,2176]{1,0:T(8,128)(2,1)} %other_part.3), channel_id=1, source_target_pairs={{0,4},{12,8},{1,5},{13,9},{2,6},{14,10},{3,7},{15,11},{16,20},{28,... | collective-permute-start | bytes 2088968 | tf_op jit(solution)/shard_map/ppermute | solution.py:450
  57.8 21.3 %collective-permute-start.6 = (bf16[160,2560]{1,0:T(8,128)(2,1)}, bf16[160,2560]{1,0:T(8,128)(2,1)}, u32[]{:S(2)}, u32[]{:S(2)}) collective-permute-start(bf16[160,2560]{1,0:T(8,128)(2,1)} %collective-permute-done.2.refs_3_), channel_id=1, source_target_pairs={{4,0},{8,12},{5,1},{9,13},{6,2},{10,14},{7,3},{11,15},{20,16},{24,... | collective-permute-start | bytes 2457608 | tf_op jit(solution)/shard_map/ppermute | solution.py:450
  67.8 49.2 %collective-permute-start.7 = (bf16[160,2176]{1,0:T(8,128)(2,1)}, bf16[160,2176]{1,0:T(8,128)(2,1)}, u32[]{:S(2)}, u32[]{:S(2)}) collective-permute-start(bf16[160,2176]{1,0:T(8,128)(2,1)} %other_part.4), channel_id=1, source_target_pairs={{0,8},{8,0},{4,12},{12,4},{1,9},{9,1},{5,13},{13,5},{2,10},{10,2},... | collective-permute-start | bytes 2088968 | tf_op jit(solution)/shard_map/ppermute | solution.py:450
  89.0 42.6 %collective-permute-start.8 = (bf16[160,2176]{1,0:T(8,128)(2,1)}, bf16[160,2176]{1,0:T(8,128)(2,1)S(1)}, u32[]{:S(2)}, u32[]{:S(2)}) collective-permute-start(bf16[160,2176]{1,0:T(8,128)(2,1)} %other_part.5), channel_id=1, source_target_pairs={{4,0},{8,12},{5,1},{9,13},{6,2},{10,14},{7,3},{11,15},{20,16},{24,... | collective-permute-start | bytes 2088968 | tf_op jit(solution)/shard_map/ppermute | solution.py:450
  90.3 41.3 %collective-permute-start.9 = (bf16[160,2176]{1,0:T(8,128)(2,1)}, bf16[160,2176]{1,0:T(8,128)(2,1)}, u32[]{:S(2)}, u32[]{:S(2)}) collective-permute-start(bf16[160,2176]{1,0:T(8,128)(2,1)} %other_part.5), channel_id=1, source_target_pairs={{0,12},{12,0},{1,13},{13,1},{2,14},{14,2},{3,15},{15,3},{16,28},{2... | collective-permute-start | bytes 2088968 | tf_op jit(solution)/shard_map/ppermute | solution.py:450
  131.7 0.9 copy-start.2

commit v7 on v6

v7 whole, which is shorter than its diff:
```python
import functools
import math

import jax
import jax.numpy as jnp
from jax import lax
from jax.experimental import pallas as pl
from jax.experimental.pallas import tpu as pltpu
from jax.sharding import PartitionSpec as P

HEADS = 64
KVH = 8
HD = 128
MAXBLK = 32
CAPP = 2
GROUP = HEADS // KVH
EMPTY = -1e30
TILE = 256
ONES = 16
PIECE = 32
SCALE = 1.0 / math.sqrt(HD)
EXP2_SCALE = SCALE * math.log2(math.e)
VMEM_LIMIT = 63 * 1024 * 1024 + 512 * 1024


def fetch(pool_size, tables, request, stores, buffers, sems):
    prefix_ref, store_ref, slot_ref = tables
    me = lax.axis_index("pool")
    first = lax.rem(me - store_ref[request, 0] + pool_size, pool_size)
    count = lax.max(lax.div(prefix_ref[request] - first + pool_size - 1, pool_size), 0)

    def copies(entry):
        slot = slot_ref[request, first + entry * pool_size]
        return [
            pltpu.make_async_copy(stores[i].at[slot], buffers[i].at[entry], sems.at[i, entry])
            for i in range(2)
        ]

    def start(entry, carry):
        for copy in copies(entry):
            copy.start()
        return carry

    lax.fori_loop(0, count, start, 0)

    def ready(entry):
        for copy in copies(entry):
            copy.wait()

    return count, ready


def attend(
    key_ref,
    value_ref,
    count,
    ready,
    fresh,
    new_rows,
    columns,
    scores,
    weights,
    peaks,
    factors,
    turned,
    acc,
):
    rows = columns.shape[1]
    kv_local = columns.shape[0] // HD

    def visit(keys, values, seen):
        size = keys[0].shape[0]

        def score(kv):
            turned[kv, :HD, :size] = values[kv].T
            block = lax.dot_general(
                keys[kv],
                columns[kv * HD : (kv + 1) * HD, :],
                (((1,), (0,)), ((), ())),
                preferred_element_type=jnp.float32,
            )
            if seen is not None:
                block = jnp.where(seen, block, EMPTY)
            scores[kv, :size, :] = block

        def weigh(kv):
            for i in range(0, rows, TILE):
                part = slice(i, i + TILE)
                before = peaks[kv, :, part]
                block = scores[kv, :size, part]
                peak = jnp.maximum(before, jnp.max(block, axis=0, keepdims=True))
                factors[kv, :, part] = jnp.exp2((before - peak) * EXP2_SCALE)
                peaks[kv, :, part] = peak
                weight = jnp.exp2(block * EXP2_SCALE - peak[0:1] * EXP2_SCALE)
                weights[kv, :size, part] = weight.astype(jnp.bfloat16)

        def mix(kv):
            added = lax.dot_general(
                turned[kv, :, :size],
                weights[kv, :size, :],
                (((1,), (0,)), ((), ())),
                preferred_element_type=jnp.float32,
            )
            acc[kv] = acc[kv] * factors[kv, 0:1, :] + added

        for step in range(kv_local + 2):
            for offset, stage in ((0, score), (2, mix), (1, weigh)):
                if 0 <= step - offset < kv_local:
                    stage(step - offset)

    def lanes_of(array):
        return [array[:, kv * HD : (kv + 1) * HD] for kv in range(kv_local)]

    def blocks_of(ref, first, number):
        return lanes_of(ref[pl.ds(first, number)].reshape(number * ref.shape[1], ref.shape[2]))

    peaks[...] = jnp.full(peaks.shape, EMPTY, jnp.float32)
    acc[...] = jnp.zeros(acc.shape, jnp.float32)
    turned[:, HD:, :] = jnp.ones((kv_local, ONES, turned.shape[2]), jnp.bfloat16)
    if fresh is not None:
        new_key_ref, new_value_ref = fresh
        row = lax.rem(lax.broadcasted_iota(jnp.int32, (1, rows), 1), new_rows)
        seen = lax.broadcasted_iota(jnp.int32, (new_key_ref.shape[0], rows), 0) <= row
        visit(lanes_of(new_key_ref), lanes_of(new_value_ref), seen)

    def visit_blocks(number):
        def body(index, carry):
            for i in range(number):
                ready(index * number + i)
            visit(
                blocks_of(key_ref, index * number, number),
                blocks_of(value_ref, index * number, number),
                None,
            )
            return carry

        return body

    pairs = count // 2 if key_ref.shape[0] > 1 else 0
    if key_ref.shape[0] > 1:
        lax.fori_loop(0, pairs, visit_blocks(2), 0)
    lax.fori_loop(2 * pairs, count, visit_blocks(1), 0)
    outs = []
    logs = []
    for kv in range(kv_local):
        total = acc[kv, HD : HD + 1, :]
        safe = jnp.where(total > 0, total, 1.0)
        logs.append(jnp.where(total > 0, peaks[kv, 0:1] * SCALE + jnp.log(safe), EMPTY))
        outs.append(acc[kv, :HD, :] * (1.0 / safe))
    return outs, logs


def prepare_kernel(query_ref, new_key_ref, new_value_ref, payload_ref, query_rows):
    new_rows = query_ref.shape[0]
    kv_width = new_key_ref.shape[1]
    for kv in range(kv_width // HD):
        for g in range(GROUP):
            head = kv * GROUP + g
            query_rows[g * new_rows : (g + 1) * new_rows, :] = query_ref[
                :, head * HD : (head + 1) * HD
            ]
        payload_ref[kv * HD : (kv + 1) * HD, :] = query_rows[...].T
    for i, new_ref in enumerate((new_key_ref, new_value_ref)):
        for piece in range(new_rows // PIECE):
            row, lane = piece_place(i, piece, new_rows, kv_width)
            payload_ref[row : row + PIECE, lane : lane + kv_width] = new_ref[
                piece * PIECE : (piece + 1) * PIECE, :
            ]


def piece_place(i, piece, new_rows, kv_width):
    index = i * (new_rows // PIECE) + piece
    beside = GROUP * new_rows // kv_width
    return kv_width + index // beside * PIECE, index % beside * kv_width


def payload_rows(new_rows, kv_width):
    return piece_place(1, new_rows // PIECE - 1, new_rows, kv_width)[0] + PIECE


def own_kernel(
    pool_size,
    prefix_ref,
    store_ref,
    slot_ref,
    payload_ref,
    new_key_ref,
    new_value_ref,
    store_keys,
    store_values,
    out_ref,
    log_ref,
    key_buf,
    value_buf,
    new_key_buf,
    new_value_buf,
    *state,
):
    *work, sems = state
    count, ready = fetch(
        pool_size,
        (prefix_ref, store_ref, slot_ref),
        lax.axis_index("pool"),
        (store_keys, store_values),
        (key_buf, value_buf),
        sems,
    )
    new_rows, kv_width = new_key_ref.shape
    for buffer, source in ((new_key_buf, new_key_ref), (new_value_buf, new_value_ref)):
        buffer[:new_rows, :] = source[...]
        buffer[new_rows:, :] = jnp.zeros((buffer.shape[0] - new_rows, kv_width), jnp.bfloat16)
    fresh = (new_key_buf, new_value_buf)
    outs, logs = attend(
        key_buf, value_buf, count, ready, fresh, new_rows, payload_ref.at[:kv_width], *work
    )
    log_ref[...] = jnp.zeros(log_ref.shape, jnp.float32)
    for kv, (out, log) in enumerate(zip(outs, logs)):
        out_ref[kv * HD : (kv + 1) * HD, :] = out
        log_ref[kv : kv + 1, :] = log


def other_kernel(pool_size, new_rows, partners, *refs):
    if partners is None:
        request = refs[0][0]
        choice = [None]
        refs = refs[1:]
    else:
        me = lax.axis_index("pool")
        inner = is_inner(me)
        request = me ^ jnp.where(inner, partners[0], partners[1])
        choice = [inner, jnp.logical_not(inner)]
    tables, refs = refs[:3], refs[3:]
    payload_refs = refs[: len(choice)]
    store_keys, store_values, out_ref, key_buf, value_buf, *state = refs[len(choice) :]
    *work, columns, query_sem, sems = state
    kv_width = columns.shape[0]

    def query_copy(payload_ref):
        return pltpu.make_async_copy(payload_ref.at[:kv_width], columns, query_sem)

    for payload_ref, hit in zip(payload_refs, choice):
        if hit is None:
            query_copy(payload_ref).start()
        else:
            pl.when(hit)(query_copy(payload_ref).start)
    count, ready = fetch(
        pool_size, tables, request, (store_keys, store_values), (key_buf, value_buf), sems
    )
    query_copy(payload_refs[0]).wait()
    outs, logs = attend(key_buf, value_buf, count, ready, None, new_rows, columns, *work)
    tail = []
    for kv, (out, log) in enumerate(zip(outs, logs)):
        out_ref[kv * HD : (kv + 1) * HD, :] = out.astype(jnp.bfloat16)
        high = log.astype(jnp.bfloat16).astype(jnp.float32)
        middle = (log - high).astype(jnp.bfloat16).astype(jnp.float32)
        tail += [high, middle, log - high - middle]
    tail.append(jnp.zeros((ONES - len(tail), columns.shape[1]), jnp.float32))
    out_ref[kv_width:, :] = jnp.concatenate(tail, axis=0).astype(jnp.bfloat16)


def is_inner(place):
    return (place == 1) | (place == 2)


def source_of(me, entry):
    if isinstance(entry, int):
        return jnp.bool_(True), jnp.int32(entry)
    inner = is_inner(me)
    masks = [0 if mask is None else mask for mask in entry]
    there = jnp.where(inner, entry[0] is not None, entry[1] is not None)
    return there, me ^ jnp.where(inner, masks[0], masks[1])


def push_kernel(pool_size, entries, owner_ref, *refs):
    payload_refs = refs[: len(entries)]
    key_out, value_out, sems = refs[len(entries) :]
    outs = (key_out, value_out)
    kv_width = key_out.shape[2]
    me = lax.axis_index("pool")
    total = jnp.int32(0)
    for other in range(pool_size):
        total += (owner_ref[other] == me).astype(jnp.int32)

    new_rows = key_out.shape[1]

    def copies(payload_ref, place):
        for i in range(2):
            for piece in range(new_rows // PIECE):
                row, lane = piece_place(i, piece, new_rows, kv_width)
                yield pltpu.make_async_copy(
                    payload_ref.at[row : row + PIECE, lane : lane + kv_width],
                    outs[i].at[place, piece * PIECE : (piece + 1) * PIECE],
                    sems.at[i, place, piece],
                )

    for entry, payload_ref in zip(entries, payload_refs):
        there, source = source_of(me, entry)
        rank = jnp.int32(0)
        for other in range(pool_size):
            rank += ((owner_ref[other] == me) & (other < source)).astype(jnp.int32)
        hit = there & (owner_ref[source] == me)
        for place in range(CAPP):

            @pl.when(hit & (rank == place))
            def _():
                for copy in copies(payload_ref, place):
                    copy.start()

    for place in range(CAPP):

        @pl.when(total <= place)
        def _():
            for out in outs:
                out[place] = jnp.zeros(out.shape[1:], jnp.bfloat16)

        @pl.when(total > place)
        def _():
            for copy in copies(payload_refs[0], place):
                copy.wait()


def combine_kernel(sources, last, own_ref, log_ref, *refs):
    parts = refs[: len(sources)]
    out_ref = refs[len(sources)]
    kv_width, rows = own_ref.shape
    me = lax.axis_index("pool")
    arrived = []
    tails = []
    for source, part in zip(sources, parts):
        there, request = source_of(me, source)
        arrived.append(there & (request != me))
        tails.append(part[kv_width:, :].astype(jnp.float32))
    if not last:
        refs[len(sources) + 1][...] = log_ref[...]
    for kv in range(kv_width // HD):
        logs = [log_ref[kv : kv + 1, :]]
        for there, tail in zip(arrived, tails):
            log = sum(tail[3 * kv + i : 3 * kv + i + 1] for i in range(3))
            logs.append(jnp.where(there, log, EMPTY))
        peak = functools.reduce(jnp.maximum, logs)
        shares = [jnp.exp(x - peak) for x in logs]
        total = functools.reduce(jnp.add, shares)
        shares = [x * (1.0 / total) for x in shares]
        band = slice(kv * HD, (kv + 1) * HD)
        for i in range(0, rows, TILE):
            part = slice(i, i + TILE)
            mixed = own_ref[band, part] * shares[0][:, part]
            for share, ref in zip(shares[1:], parts):
                mixed = mixed + ref[band, part].astype(jnp.float32) * share[:, part]
            if last:
                refs[len(sources) + 1][part, :] = mixed.astype(jnp.bfloat16).T
            else:
                out_ref[band, part] = mixed
        if last:
            turned = refs[len(sources) + 1]
            new_rows = out_ref.shape[0]
            for g in range(GROUP):
                head = kv * GROUP + g
                out_ref[:, head * HD : (head + 1) * HD] = turned[g * new_rows : (g + 1) * new_rows, :]
        else:
            refs[len(sources) + 1][kv : kv + 1, :] = peak + jnp.log(total)


def shards(
    queries,
    new_keys,
    new_values,
    store_keys,
    store_values,
    prefix_blocks,
    hit_store,
    hit_slot,
    decode_owner,
):
    pool_size = lax.axis_size("pool")
    capacity = (MAXBLK + pool_size - 1) // pool_size
    new_rows = queries.shape[1]
    width = queries.shape[2]
    kv_width = new_keys.shape[2]
    block_len = store_keys.shape[1]
    rows = GROUP * new_rows
    tables = (prefix_blocks, hit_store, hit_slot)
    smem_spec = pl.BlockSpec(memory_space=pltpu.SMEM)
    hbm_spec = pl.BlockSpec(memory_space=pltpu.HBM)
    vmem_spec = pl.BlockSpec(memory_space=pltpu.VMEM)
    params = pltpu.CompilerParams(vmem_limit_bytes=VMEM_LIMIT)

    def cost(share):
        return pl.CostEstimate(
            flops=share * rows * block_len * kv_width * capacity,
            bytes_accessed=rows,
            transcendentals=0,
        )

    buffers = [pltpu.VMEM((capacity, block_len, kv_width), jnp.bfloat16)] * 2
    kv_local = kv_width // HD
    widest = block_len * min(2, capacity)
    work = [
        pltpu.VMEM((kv_local, widest, rows), jnp.float32),
        pltpu.VMEM((kv_local, widest, rows), jnp.bfloat16),
        pltpu.VMEM((kv_local, 8, rows), jnp.float32),
        pltpu.VMEM((kv_local, 8, rows), jnp.float32),
        pltpu.VMEM((kv_local, HD + ONES, widest), jnp.bfloat16),
        pltpu.VMEM((kv_local, HD + ONES, rows), jnp.float32),
    ]
    sems = pltpu.SemaphoreType.DMA((2, capacity))

    def own_part(payload):
        return pl.pallas_call(
            functools.partial(own_kernel, pool_size),
            in_specs=[smem_spec] * 3 + [vmem_spec] * 3 + [hbm_spec] * 2,
            out_specs=[vmem_spec] * 2,
            scratch_shapes=[
                *buffers,
                *[pltpu.VMEM((block_len, kv_width), jnp.bfloat16)] * 2,
                *work,
                sems,
            ],
            out_shape=[
                jax.ShapeDtypeStruct((kv_width, rows), jnp.float32),
                jax.ShapeDtypeStruct((8, rows), jnp.float32),
            ],
            compiler_params=params,
            cost_estimate=cost(8),
            name="own_part",
        )(*tables, payload, new_keys[0], new_values[0], store_keys, store_values)

    def other_part(partners, held, *request, share=8):
        return pl.pallas_call(
            functools.partial(other_kernel, pool_size, new_rows, partners),
            in_specs=[smem_spec] * (3 + len(request)) + [hbm_spec] * (len(held) + 2),
            out_specs=vmem_spec,
            scratch_shapes=[
                *buffers,
                *work,
                pltpu.VMEM((kv_width, rows), jnp.bfloat16),
                pltpu.SemaphoreType.DMA,
                sems,
            ],
            out_shape=jax.ShapeDtypeStruct((kv_width + ONES, rows), jnp.bfloat16),
            compiler_params=params,
            cost_estimate=cost(share),
            name="other_part",
        )(*request, *tables, *held, store_keys, store_values)

    def combine(own, log, sources, parts, last=True):
        if last:
            out_shape = jax.ShapeDtypeStruct((new_rows, width), jnp.bfloat16)
        else:
            out_shape = [
                jax.ShapeDtypeStruct((kv_width, rows), jnp.float32),
                jax.ShapeDtypeStruct((8, rows), jnp.float32),
            ]
        return pl.pallas_call(
            functools.partial(combine_kernel, tuple(sources), last),
            in_specs=[vmem_spec] * (2 + len(parts)),
            out_specs=vmem_spec if last else [vmem_spec] * 2,
            scratch_shapes=[pltpu.VMEM((rows, HD), jnp.bfloat16)] if last else [],
            out_shape=out_shape,
            compiler_params=params,
            cost_estimate=cost(0),
            name="combine",
        )(own, log, *parts)

    payload = pl.pallas_call(
        prepare_kernel,
        in_specs=[vmem_spec] * 3,
        out_specs=vmem_spec,
        scratch_shapes=[pltpu.VMEM((rows, HD), jnp.bfloat16)],
        out_shape=jax.ShapeDtypeStruct((payload_rows(new_rows, kv_width), rows), jnp.bfloat16),
        compiler_params=params,
        name="prepare",
    )(queries[0], new_keys[0], new_values[0])
    own_out, own_log = own_part(payload)
    if pool_size == 4:
        def send(array, *pairs):
            return lax.ppermute(array, "pool", pairs)

        near = send(payload, (0, 1), (1, 0), (2, 3), (3, 2))
        middle = send(payload, (1, 2), (2, 1))
        near, middle, own_out, own_log = lax.optimization_barrier((near, middle, own_out, own_log))
        crossed = send(near, (1, 2), (2, 1))
        outward = send(middle, (1, 0), (2, 3))
        first = other_part((3, 1), (middle, near))
        crossed, outward, first = lax.optimization_barrier((crossed, outward, first))
        across = send(first, (1, 2), (2, 1))
        inward = send(first, (0, 1), (3, 2))
        far = send(crossed, (1, 0), (2, 3))
        second = other_part((2, 2), (crossed, outward), share=0)
        near, second = lax.optimization_barrier((near, second))
        apart = send(second, (0, 2), (2, 0), (1, 3), (3, 1))
        own_out, own_log = combine(
            own_out, own_log, [(3, None), (1, None)], [across, inward], last=False
        )
        near, own_out, own_log = lax.optimization_barrier((near, own_out, own_log))
        third = other_part((1, 3), (near, far), share=8)
        ends = send(third, (0, 3), (3, 0))
        back = send(third, (1, 0), (2, 3))
        own_out, own_log, third = lax.optimization_barrier((own_out, own_log, third))
        own_out, own_log = combine(own_out, own_log, [(2, 2)], [apart], last=False)
        sources = [(None, 1), (None, 3)]
        parts = [back, ends]
        moved = [
            ((0, 0), payload),
            ((1, 1), near),
            ((3, None), middle),
            ((2, None), crossed),
            ((None, 2), outward),
            ((None, 3), far),
        ]
    else:
        gathered = lax.all_gather(payload, "pool", axis=0, tiled=False)
        packed = lax.map(
            lambda pair: other_part(None, (pair[0],), pair[1].reshape(1)),
            (gathered, jnp.arange(pool_size, dtype=jnp.int32)),
        )
        parts = lax.all_to_all(packed, "pool", split_axis=0, concat_axis=0, tiled=True)
        sources = list(range(pool_size))
        moved = [(source, gathered[source]) for source in range(pool_size)]

    attended = combine(own_out, own_log, sources, parts)
    pushed_keys, pushed_values = pl.pallas_call(
        functools.partial(push_kernel, pool_size, tuple(entry for entry, _ in moved)),
        in_specs=[smem_spec] + [hbm_spec] * len(moved),
        out_specs=[vmem_spec] * 2,
        scratch_shapes=[pltpu.SemaphoreType.DMA((2, CAPP, new_rows // PIECE))],
        out_shape=[jax.ShapeDtypeStruct((CAPP, new_rows, kv_width), jnp.bfloat16)] * 2,
        compiler_params=params,
        name="push",
    )(decode_owner, *[array for _, array in moved])
    return (attended[None], pushed_keys, pushed_values)


def solution(mesh):
    in_specs = (
        P(("groups", "pool"), None, ("tensor", "sub")),
        P(("groups", "pool"), None, ("tensor", "sub")),
        P(("groups", "pool"), None, ("tensor", "sub")),
        P(("groups", "pool"), None, ("tensor", "sub")),
        P(("groups", "pool"), None, ("tensor", "sub")),
        P("groups"),
        P("groups", None),
        P("groups", None),
        P("groups"),
    )
    out_specs = (
        P(("groups", "pool"), None, ("tensor", "sub")),
        P(("groups", "pool"), None, ("tensor", "sub")),
        P(("groups", "pool"), None, ("tensor", "sub")),
    )
    return jax.shard_map(shards, mesh=mesh, in_specs=in_specs, out_specs=out_specs, check_vma=False)
```

time: 138 us -> 135 us (0.978)
  waiting for transfers between devices: 36 us -> 51.5 us
  starting transfers between devices: 37.3 us -> 25.5 us
  Pallas kernels: 61.6 us -> 57.2 us
    ppermute x10, waiting for transfers between devices: 36 us -> 51.5 us  [send(): return lax.ppermute(array, 'pool', pairs)]
    ppermute x10, starting transfers between devices: 37.3 us -> 25.5 us  [send(): return lax.ppermute(array, 'pool', pairs)]
    pallas_call x6 -> x7, Pallas kernels: 47.5 us -> 42.7 us  [the longest x3 31.1 us: other_part(): pl.pallas_call(functools.partial(other_kernel, pool_size, new_rows, partn...]
  transfers between devices with their start and end apart: 10 -> 10, of which waited for: 5 -> 5; matrix products, arithmetic and copies ran while one was open for 0% -> 0% of each run, Pallas kernels for 41% -> 38%
where the time goes in v7:
time: 135 us
  Pallas kernels  57.2 us (42%)
  waiting for transfers between devices  51.5 us (38%)
  starting transfers between devices  25.5 us (19%)
    ppermute x10, waiting for transfers between devices, send(): return lax.ppermute(array, 'pool', pairs)  51.5 us
    pallas_call x3, Pallas kernels, other_part(): pl.pallas_call(functools.partial(other_kernel, pool_size, new_rows, partn...  31.1 us
    ppermute x10, starting transfers between devices, send(): return lax.ppermute(array, 'pool', pairs)  25.5 us
    pallas_call x1, Pallas kernels, own_part(): pl.pallas_call(functools.partial(own_kernel, pool_size), in_specs=[smem_s...  12.7 us
    pallas_call x3, Pallas kernels, combine(): pl.pallas_call(functools.partial(combine_kernel, tuple(sources), last), i...  9.25 us
  transfers between devices with their start and end apart: 10, of which 5 were waited for; matrix products, arithmetic and copies ran while one was open for 0% of the time, Pallas kernels for 38%

profile of v7, /device:TPU:0, one launch (start us, length us, event | category | flops | bytes accessed | tf_op | source)
XLA Modules:
  0.0 135.0 jit_solution(2074705434955558232)
XLA Ops:
  0.6 2.4 %prepare.1.payload_ref.refs_0_ = bf16[320,1280]{1,0:T(8,128)(2,1)} custom-call(bf16[160,2048]{1,0:T(8,128)(2,1)} %bitcast.4, bf16[160,256]{1,0:T(8,128)(2,1)} %bitcast.6, bf16[160,256]{1,0:T(8,128)(2,1)} %bitcast.8), custom_call_target="tpu_custom_call" | custom-call | tf_op jit(solution)/shard_map/prepare/pallas_call | solution.py:465
  3.0 3.0 %collective-permute-start = (bf16[320,1280]{1,0:T(8,128)(2,1)}, bf16[320,1280]{1,0:T(8,128)(2,1)}, u32[]{:S(2)}, u32[]{:S(2)}) collective-permute-start(bf16[320,1280]{1,0:T(8,128)(2,1)} %prepare.1.payload_ref.refs_0_), channel_id=1, source_target_pairs={{0,4},{4,0},{8,12},{12,8},{1,5},{5,1},{9,13},{13,9},{2,6},{6,2},{1... | collective-permute-start | bytes 2457608 | tf_op jit(solution)/shard_map/ppermute | solution.py:477
  6.0 1.6 %collective-permute-start.1 = (bf16[320,1280]{1,0:T(8,128)(2,1)}, bf16[320,1280]{1,0:T(8,128)(2,1)}, u32[]{:S(2)}, u32[]{:S(2)}) collective-permute-start(bf16[320,1280]{1,0:T(8,128)(2,1)} %prepare.1.payload_ref.refs_0_), channel_id=1, source_target_pairs={{4,8},{8,4},{5,9},{9,5},{6,10},{10,6},{7,11},{11,7},{20,24},{24,20... | collective-permute-start | bytes 2457608 | tf_op jit(solution)/shard_map/ppermute | solution.py:477
  7.6 12.7 %own_part.1 = (f32[256,1280]{1,0:T(8,128)}, f32[8,1280]{1,0:T(8,128)}) custom-call(s32[4]{0:T(128)} %refs_0_.5, s32[4,32]{1,0:T(4,128)} %refs_1_.5, s32[4,32]{1,0:T(4,128)} %refs_2_.5, bf16[320,1280]{1,0:T(8,128)(2,1)} %prepare.1.payload_ref.refs_0_, bf16[160,256]{1,0:T(8,128)(2,1)} %bitcast.7, bf16[160,256]{1,0:T(8,128)(2,1)} %bitcast.9, ...), custom_call_target="tpu_custom_call" | custom-call | flops 5368709120 | bytes 1280 | tf_op jit(solution)/shard_map/own_part/pallas_call | solution.py:409
  20.3 4.3 %collective-permute-done.refs_4_.refs_3_.refs_1_ = bf16[320,1280]{1,0:T(8,128)(2,1)} collective-permute-done((bf16[320,1280]{1,0:T(8,128)(2,1)}, bf16[320,1280]{1,0:T(8,128)(2,1)}, u32[]{:S(2)}, u32[]{:S(2)}) %collective-permute-start) | collective-permute-done | bytes 819232 | tf_op jit(solution)/shard_map/ppermute | solution.py:477
  24.6 0.0 collective-permute-done.1.refs_3_.refs_2_
  24.6 1.6 %collective-permute-start.2 = (bf16[320,1280]{1,0:T(8,128)(2,1)}, bf16[320,1280]{1,0:T(8,128)(2,1)}, u32[]{:S(2)}, u32[]{:S(2)}) collective-permute-start(bf16[320,1280]{1,0:T(8,128)(2,1)} %collective-permute-done.refs_4_.refs_3_.refs_1_), channel_id=1, source_target_pairs={{4,8},{8,4},{5,9},{9,5},{6,10},{10,6},{7,11},{11,7},{20,24},{24,20... | collective-permute-start | bytes 2457608 | tf_op jit(solution)/shard_map/ppermute | solution.py:477
  26.1 1.3 collective-permute-start.3
  27.4 8.6 %other_part.3 = bf16[272,1280]{1,0:T(8,128)(2,1)} custom-call(s32[4]{0:T(128)} %refs_0_.5, s32[4,32]{1,0:T(4,128)} %refs_1_.5, s32[4,32]{1,0:T(4,128)} %refs_2_.5, bf16[320,1280]{1,0:T(8,128)(2,1)} %collective-permute-done.1.refs_3_.refs_2_, bf16[320,1280]{1,0:T(8,128)(2,1)} %collective-permute-done.refs_4_.refs_3_.refs_1_, bf16[32,256,256]{2,1,0:T(8,128)(2,1)} %refs_5_.5, ...), custom_call_target="tpu_custom_call" | custom-call | flops 5368709120 | bytes 1280 | tf_op jit(solution)/shard_map/other_part/pallas_call | solution.py:429
  36.0 0.0 collective-permute-done.2.refs_3_
  36.0 15.3 %collective-permute-done.3.refs_4_ = bf16[320,1280]{1,0:T(8,128)(2,1)} collective-permute-done((bf16[320,1280]{1,0:T(8,128)(2,1)}, bf16[320,1280]{1,0:T(8,128)(2,1)}, u32[]{:S(2)}, u32[]{:S(2)}) %collective-permute-start.3) | collective-permute-done | bytes 819232 | tf_op jit(solution)/shard_map/ppermute | solution.py:477
  51.3 1.3 collective-permute-start.6
  52.6 1.6 %collective-permute-start.4 = (bf16[272,1280]{1,0:T(8,128)(2,1)}, bf16[272,1280]{1,0:T(8,128)(2,1)}, u32[]{:S(2)}, u32[]{:S(2)}) collective-permute-start(bf16[272,1280]{1,0:T(8,128)(2,1)} %other_part.3), channel_id=1, source_target_pairs={{4,8},{8,4},{5,9},{9,5},{6,10},{10,6},{7,11},{11,7},{20,24},{24,20... | collective-permute-start | bytes 2088968 | tf_op jit(solution)/shard_map/ppermute | solution.py:477
  54.2 7.2 %collective-permute-start.5 = (bf16[272,1280]{1,0:T(8,128)(2,1)}, bf16[272,1280]{1,0:T(8,128)(2,1)}, u32[]{:S(2)}, u32[]{:S(2)}) collective-permute-start(bf16[272,1280]{1,0:T(8,128)(2,1)} %other_part.3), channel_id=1, source_target_pairs={{0,4},{12,8},{1,5},{13,9},{2,6},{14,10},{3,7},{15,11},{16,20},{28,... | collective-permute-start | bytes 2088968 | tf_op jit(solution)/shard_map/ppermute | solution.py:477
  61.4 11.8 %other_part.4 = bf16[272,1280]{1,0:T(8,128)(2,1)} custom-call(s32[4]{0:T(128)} %refs_0_.5, s32[4,32]{1,0:T(4,128)} %refs_1_.5, s32[4,32]{1,0:T(4,128)} %refs_2_.5, bf16[320,1280]{1,0:T(8,128)(2,1)} %collective-permute-done.2.refs_3_, bf16[320,1280]{1,0:T(8,128)(2,1)} %collective-permute-done.3.refs_4_, bf16[32,256,256]{2,1,0:T(8,128)(2,1)} %refs_5_.5, ...), custom_call_target="tpu_custom_call" | custom-call | bytes 1280 | tf_op jit(solution)/shard_map/other_part/pallas_call | solution.py:429
  73.3 0.1 collective-permute-start.7
  73.3 0.0 collective-permute-done.4.refs_0_
  73.4 2.2 %collective-permute-done.5.refs_1_ = bf16[272,1280]{1,0:T(8,128)(2,1)} collective-permute-done((bf16[272,1280]{1,0:T(8,128)(2,1)}, bf16[272,1280]{1,0:T(8,128)(2,1)}, u32[]{:S(2)}, u32[]{:S(2)}) %collective-permute-start.5) | collective-permute-done | bytes 696352 | tf_op jit(solution)/shard_map/ppermute | solution.py:477
  75.5 3.2 %combine.3 = (f32[256,1280]{1,0:T(8,128)}, f32[8,1280]{1,0:T(8,128)}) custom-call(f32[256,1280]{1,0:T(8,128)} %get-tuple-element.32.own_ref, f32[8,1280]{1,0:T(8,128)} %get-tuple-element.33.log_ref, bf16[272,1280]{1,0:T(8,128)(2,1)} %collective-permute-done.4.refs_0_, bf16[272,1280]{1,0:T(8,128)(2,1)} %collective-permute-done.5.refs_1_), custom_call_target="tpu_custom_call" | custom-call | bytes 1280 | tf_op jit(solution)/shard_map/combine/pallas_call | solution.py:454
  78.7 0.0 collective-permute-done.6.refs_4_.refs_5_
  78.7 10.7 %other_part.5 = bf16[272,1280]{1,0:T(8,128)(2,1)} custom-call(s32[4]{0:T(128)} %refs_0_.5, s32[4,32]{1,0:T(4,128)} %refs_1_.5, s32[4,32]{1,0:T(4,128)} %refs_2_.5, bf16[320,1280]{1,0:T(8,128)(2,1)} %collective-permute-done.refs_4_.refs_3_.refs_1_, bf16[320,1280]{1,0:T(8,128)(2,1)} %collective-permute-done.6.refs_4_.refs_5_, bf16[32,256,256]{2,1,0:T(8,128)(2,1)} %refs_5_.5, ...), custom_call_target="tpu_custom_call" | custom-call | flops 5368709120 | bytes 1280 | tf_op jit(solution)/shard_map/other_part/pallas_call | solution.py:429
  89.5 1.3 collective-permute-start.8
  90.8 6.6 %collective-permute-start.9 = (bf16[272,1280]{1,0:T(8,128)(2,1)}, bf16[272,1280]{1,0:T(8,128)(2,1)}, u32[]{:S(2)}, u32[]{:S(2)}) collective-permute-start(bf16[272,1280]{1,0:T(8,128)(2,1)} %other_part.5), channel_id=1, source_target_pairs={{0,12},{12,0},{1,13},{13,1},{2,14},{14,2},{3,15},{15,3},{16,28},{2... | collective-permute-start | bytes 2088968 | tf_op jit(solution)/shard_map/ppermute | solution.py:477
  97.4 1.8 %push.1 = (bf16[2,160,256]{2,1,0:T(8,128)(2,1)}, bf16[2,160,256]{2,1,0:T(8,128)(2,1)}) custom-call(s32[4]{0:T(128)} %owner_ref.1, bf16[320,1280]{1,0:T(8,128)(2,1)} %prepare.1.payload_ref.refs_0_, bf16[320,1280]{1,0:T(8,128)(2,1)} %collective-permute-done.refs_4_.refs_3_.refs_1_, bf16[320,1280]{1,0:T(8,128)(2,1)} %collective-permute-done.1.refs_3_.refs_2_, ...), custom_call_target="tpu_custom_call" | custom-call | tf_op jit(solution)/shard_map/push/pallas_call | solution.py:522
  99.2 18.8 %collective-permute-done.7.refs_0_ = bf16[272,1280]{1,0:T(8,128)(2,1)} collective-permute-done((bf16[272,1280]{1,0:T(8,128)(2,1)}, bf16[272,1280]{1,0:T(8,128)(2,1)}, u32[]{:S(2)}, u32[]{:S(2)}) %collective-permute-start.7) | collective-permute-done | bytes 696352 | tf_op jit(solution)/shard_map/ppermute | solution.py:477
  118.0 2.9 %combine.4 = (f32[256,1280]{1,0:T(8,128)}, f32[8,1280]{1,0:T(8,128)}) custom-call(f32[256,1280]{1,0:T(8,128)} %get-tuple-element.40.own_ref, f32[8,1280]{1,0:T(8,128)} %get-tuple-element.41.log_ref, bf16[272,1280]{1,0:T(8,128)(2,1)} %collective-permute-done.7.refs_0_), custom_call_target="tpu_custom_call" | custom-call | bytes 1280 | tf_op jit(solution)/shard_map/combine/pallas_call | solution.py:454
  120.9 10.9 %collective-permute-done.8.refs_0_ = bf16[272,1280]{1,0:T(8,128)(2,1)} collective-permute-done((bf16[272,1280]{1,0:T(8,128)(2,1)}, bf16[272,1280]{1,0:T(8,128)(2,1)}, u32[]{:S(2)}, u32[]{:S(2)}) %collective-permute-start.8) | collective-permute-done | bytes 696352 | tf_op jit(solution)/shard_map/ppermute | solution.py:477
  131.8 0.0 collective-permute-done.9.refs_1_
  131.8 3.2 %combine.5 = bf16[160,2048]{1,0:T(8,128)(2,1)} custom-call(f32[256,1280]{1,0:T(8,128)} %get-tuple-element.43.own_ref, f32[8,1280]{1,0:T(8,128)} %get-tuple-element.44.log_ref, bf16[272,1280]{1,0:T(8,128)(2,1)} %collective-permute-done.8.refs_0_, bf16[272,1280]{1,0:T(8,128)(2,1)} %collective-permute-done.9.refs_1_), custom_call_target="tpu_custom_call" | custom-call | bytes 1280 | tf_op jit(solution)/shard_map/combine/pallas_call | solution.py:454
Async XLA Ops:
  3.0 21.6 %collective-permute-start = (bf16[320,1280]{1,0:T(8,128)(2,1)}, bf16[320,1280]{1,0:T(8,128)(2,1)}, u32[]{:S(2)}, u32[]{:S(2)}) collective-permute-start(bf16[320,1280]{1,0:T(8,128)(2,1)} %prepare.1.payload_ref.refs_0_), channel_id=1, source_target_pairs={{0,4},{4,0},{8,12},{12,8},{1,5},{5,1},{9,13},{13,9},{2,6},{6,2},{1... | collective-permute-start | bytes 2457608 | tf_op jit(solution)/shard_map/ppermute | solution.py:477
  6.0 18.6 %collective-permute-start.1 = (bf16[320,1280]{1,0:T(8,128)(2,1)}, bf16[320,1280]{1,0:T(8,128)(2,1)}, u32[]{:S(2)}, u32[]{:S(2)}) collective-permute-start(bf16[320,1280]{1,0:T(8,128)(2,1)} %prepare.1.payload_ref.refs_0_), channel_id=1, source_target_pairs={{4,8},{8,4},{5,9},{9,5},{6,10},{10,6},{7,11},{11,7},{20,24},{24,20... | collective-permute-start | bytes 2457608 | tf_op jit(solution)/shard_map/ppermute | solution.py:477
  24.6 11.4 %collective-permute-start.2 = (bf16[320,1280]{1,0:T(8,128)(2,1)}, bf16[320,1280]{1,0:T(8,128)(2,1)}, u32[]{:S(2)}, u32[]{:S(2)}) collective-permute-start(bf16[320,1280]{1,0:T(8,128)(2,1)} %collective-permute-done.refs_4_.refs_3_.refs_1_), channel_id=1, source_target_pairs={{4,8},{8,4},{5,9},{9,5},{6,10},{10,6},{7,11},{11,7},{20,24},{24,20... | collective-permute-start | bytes 2457608 | tf_op jit(solution)/shard_map/ppermute | solution.py:477
  26.1 25.2 %collective-permute-start.3 = (bf16[320,1280]{1,0:T(8,128)(2,1)}, bf16[320,1280]{1,0:T(8,128)(2,1)}, u32[]{:S(2)}, u32[]{:S(2)}) collective-permute-start(bf16[320,1280]{1,0:T(8,128)(2,1)} %collective-permute-done.1.refs_3_.refs_2_), channel_id=1, source_target_pairs={{4,0},{8,12},{5,1},{9,13},{6,2},{10,14},{7,3},{11,15},{20,16},{24,... | collective-permute-start | bytes 2457608 | tf_op jit(solution)/shard_map/ppermute | solution.py:477
  51.3 27.4 %collective-permute-start.6 = (bf16[320,1280]{1,0:T(8,128)(2,1)}, bf16[320,1280]{1,0:T(8,128)(2,1)}, u32[]{:S(2)}, u32[]{:S(2)}) collective-permute-start(bf16[320,1280]{1,0:T(8,128)(2,1)} %collective-permute-done.2.refs_3_), channel_id=1, source_target_pairs={{4,0},{8,12},{5,1},{9,13},{6,2},{10,14},{7,3},{11,15},{20,16},{24,... | collective-permute-start | bytes 2457608 | tf_op jit(solution)/shard_map/ppermute | solution.py:477
  52.6 20.7 %collective-permute-start.4 = (bf16[272,1280]{1,0:T(8,128)(2,1)}, bf16[272,1280]{1,0:T(8,128)(2,1)}, u32[]{:S(2)}, u32[]{:S(2)}) collective-permute-start(bf16[272,1280]{1,0:T(8,128)(2,1)} %other_part.3), channel_id=1, source_target_pairs={{4,8},{8,4},{5,9},{9,5},{6,10},{10,6},{7,11},{11,7},{20,24},{24,20... | collective-permute-start | bytes 2088968 | tf_op jit(solution)/shard_map/ppermute | solution.py:477
  54.2 21.3 %collective-permute-start.5 = (bf16[272,1280]{1,0:T(8,128)(2,1)}, bf16[272,1280]{1,0:T(8,128)(2,1)}, u32[]{:S(2)}, u32[]{:S(2)}) collective-permute-start(bf16[272,1280]{1,0:T(8,128)(2,1)} %other_part.3), channel_id=1, source_target_pairs={{0,4},{12,8},{1,5},{13,9},{2,6},{14,10},{3,7},{15,11},{16,20},{28,... | collective-permute-start | bytes 2088968 | tf_op jit(solution)/shard_map/ppermute | solution.py:477
  73.3 44.8 %collective-permute-start.7 = (bf16[272,1280]{1,0:T(8,128)(2,1)}, bf16[272,1280]{1,0:T(8,128)(2,1)}, u32[]{:S(2)}, u32[]{:S(2)}) collective-permute-start(bf16[272,1280]{1,0:T(8,128)(2,1)} %other_part.4), channel_id=1, source_target_pairs={{0,8},{8,0},{4,12},{12,4},{1,9},{9,1},{5,13},{13,5},{2,10},{10,2},... | collective-permute-start | bytes 2088968 | tf_op jit(solution)/shard_map/ppermute | solution.py:477
  89.5 42.3 %collective-permute-start.8 = (bf16[272,1280]{1,0:T(8,128)(2,1)}, bf16[272,1280]{1,0:T(8,128)(2,1)}, u32[]{:S(2)}, u32[]{:S(2)}) collective-permute-start(bf16[272,1280]{1,0:T(8,128)(2,1)} %other_part.5), channel_id=1, source_target_pairs={{4,0},{8,12},{5,1},{9,13},{6,2},{10,14},{7,3},{11,15},{20,16},{24,... | collective-permute-start | bytes 2088968 | tf_op jit(solution)/shard_map/ppermute | solution.py:477
  90.8 41.0 %collective-permute-start.9 = (bf16[272,1280]{1,0:T(8,128)(2,1)}, bf16[272,1280]{1,0:T(8,128)(2,1)}, u32[]{:S(2)}, u32[]{:S(2)}) collective-permute-start(bf16[272,1280]{1,0:T(8,128)(2,1)} %other_part.5), channel_id=1, source_target_pairs={{0,12},{12,0},{1,13},{13,1},{2,14},{14,2},{3,15},{15,3},{16,28},{2... | collective-permute-start | bytes 2088968 | tf_op jit(solution)/shard_map/ppermute | solution.py:477
